TPU v7x, 512 devices: a whole 4x8x8 slice. The times are simulated.
512 devices in a mesh: row: 32 (over z, x), col: 16 (over y, core).
Axes of the slice: x: 4, y: 8, z: 8, core: 2. Of those that a mesh axis runs over, the one named last changes fastest.
Arguments:
- kernel: float32 [4, 4096, 8, 2048], P(None, 'row', None, 'col'), as said below
- targets: float32 [4, 32, 128, 1024], P(None, 'row', 'col'), may hold values from -6 to 6
Outputs:
- factor: float32 [4, 4096, 512], P(None, 'row')
- trailing: float32 [4, 4096, 8, 2048], P(None, 'row', None, 'col')
- targets_out: float32 [4, 32, 128, 1024], P(None, 'row', 'col')
Inputs may be any that keep to these rules, and one draw needn't show every extreme that they name: kernel is symmetric and positive definite.
All inputs are finite; a program needn't handle non-finite values.
Results may differ from a plain program's by a relative error of at most 0.00018.
Values sent between devices are 32-bit elements; how exact they have to be, the bound alone decides.
No kernel may reach another device: no remote copies, remote signals or barrier semaphores. Data moves between devices by JAX's collectives and lax.ppermute only.
A program may use at most 64 MiB of HBM per device.

v0:
```python
import jax
import jax.numpy as jnp
from jax import lax
from jax.sharding import PartitionSpec as P

highest = lax.Precision.HIGHEST


def broadcast(block, axis, source):
    block = jnp.where(lax.axis_index(axis) == source, block, jnp.zeros_like(block))
    return lax.psum(block, axis)


def tri_solve(lower, rhs):
    return jax.scipy.linalg.solve_triangular(lower, rhs, lower=True)


def per_device(kernel, targets):
    rows_loc, tile, cols_loc = (kernel.shape[0], kernel.shape[1], kernel.shape[2])
    width = 2 * tile
    n_row = lax.axis_size("row")
    n_col = lax.axis_size("col")
    my_row = lax.axis_index("row")
    my_col = lax.axis_index("col")
    row_ids = (
        (jnp.arange(rows_loc, dtype=jnp.int32)[:, None] * n_row + my_row) * tile
        + jnp.arange(tile, dtype=jnp.int32)[None, :]
    ).reshape(-1)
    col_ids = (
        (jnp.arange(cols_loc, dtype=jnp.int32)[:, None] * n_col + my_col) * tile
        + jnp.arange(tile, dtype=jnp.int32)[None, :]
    ).reshape(-1)
    matrix = kernel.reshape(rows_loc * tile, cols_loc * tile)
    identity = jnp.eye(width, dtype=jnp.float32)
    panels = []
    lowers = []
    middle = None
    for k in range(2):
        start = k * width
        pieces = []
        for j in range(2):
            pieces.append(broadcast(matrix[:, 0:tile], "col", 2 * k + j))
        column_panel = jnp.concatenate(pieces, axis=1)
        leading = []
        for j in range(4 - 2 * k):
            leading.append(broadcast(column_panel[0:tile], "row", 2 * k + j))
        leading = jnp.concatenate(leading, axis=0)
        lower = jnp.linalg.cholesky(leading[0:width])
        inverse = tri_solve(lower, identity)
        if k == 0:
            middle = jnp.dot(leading[width:], inverse.T, precision=highest)
        solved = jnp.dot(column_panel, inverse.T, precision=highest)
        own_rows = lax.dynamic_slice_in_dim(lower, jnp.clip(my_row - 2 * k, 0, 1) * tile, tile, 0)
        diag_full = jnp.concatenate(
            [own_rows, jnp.zeros(((rows_loc - 1) * tile, width), jnp.float32)], axis=0
        )
        before = (row_ids < start)[:, None]
        inside = ((row_ids >= start) & (row_ids < start + width))[:, None]
        panel = jnp.where(before, 0.0, jnp.where(inside, diag_full, solved))
        ratio = n_row // n_col
        received = []
        for j in range(ratio):
            part_rows = broadcast(panel, "row", my_col + j * n_col)
            received.append(part_rows.reshape(rows_loc, tile, width))
        transposed = jnp.stack(received, axis=1).reshape(cols_loc * tile, width)
        matrix = matrix - jnp.dot(panel, transposed.T, precision=highest)
        panels.append(panel)
        lowers.append(lower)
    lead = 2 * width
    top_factor = jnp.concatenate(
        [
            jnp.concatenate([lowers[0], jnp.zeros((width, width), jnp.float32)], axis=1),
            jnp.concatenate([middle, lowers[1]], axis=1),
        ],
        axis=0,
    )
    top_inverse = tri_solve(top_factor, jnp.eye(lead, dtype=jnp.float32))
    factor_loc = jnp.concatenate(panels, axis=1).reshape(rows_loc, tile, lead)
    slab = targets.shape[2]
    leading_tiles = lead // tile
    coeff = lax.dynamic_slice_in_dim(
        top_inverse, jnp.minimum(my_row, leading_tiles - 1) * tile + my_col * slab, slab, 1
    )
    weight = jnp.where(my_row < leading_tiles, 1.0, 0.0).astype(jnp.float32)
    term = jnp.dot(coeff, targets[0, 0], precision=highest) * weight
    solution = lax.psum(term, ("row", "col"))
    mine = lax.dynamic_slice_in_dim(factor_loc, my_col * slab, slab, 1)
    updated = targets[:, 0] - jnp.einsum("lsp,pe->lse", mine, solution, precision=highest)
    own_solution = lax.dynamic_slice_in_dim(
        solution, jnp.minimum(my_row, leading_tiles - 1) * tile + my_col * slab, slab, 0
    )
    filled = jnp.concatenate(
        [own_solution[None], jnp.zeros((rows_loc - 1, slab, solution.shape[1]), jnp.float32)],
        axis=0,
    )
    in_top = ((jnp.arange(rows_loc, dtype=jnp.int32) == 0) & (my_row < leading_tiles))[
        :, None, None
    ]
    targets_out = jnp.where(in_top, filled, updated)[:, None]
    keep = (row_ids[:, None] >= lead) & (col_ids[None, :] >= lead)
    trailing = jnp.where(keep, matrix, 0.0).reshape(kernel.shape)
    return (factor_loc, trailing, targets_out)


def solution(mesh):
    return jax.shard_map(
        per_device,
        mesh=mesh,
        in_specs=(P(None, "row", None, "col"), P(None, "row", "col", None)),
        out_specs=(P(None, "row", None), P(None, "row", None, "col"), P(None, "row", "col", None)),
        check_vma=False,
    )
```

profile of v0, /device:TPU:1, one launch (start us, length us, event | category | flops | bytes accessed | tf_op | source)
XLA Modules:
  0.0 1410.3 jit_solution(3959620525434283625)
XLA Ops:
  7.2 3.4 copy.31
  14.3 119.9 %all-reduce.31.cloned.1.call-done = (f32[512,128]{0,1:T(8,128)}, f32[512,128]{0,1:T(8,128)}) async-done(((f32[512,128]{0,1:T(8,128)}, f32[512,128]{0,1:T(8,128)}), (f32[512,128]{0,1:T(8,128)}, f32[512,128]{0,1:T(8,128)})) %all-reduce.31.cloned.1.call-update) | async-done | bytes 524304 | tf_op jit(solution)/shard_map/psum | solution.py:11
  137.2 152.9 %all-reduce.27.cloned.1.call-done = (f32[128,256]{0,1:T(8,128)}, f32[128,256]{0,1:T(8,128)}) async-done(((f32[128,256]{0,1:T(8,128)}, f32[128,256]{0,1:T(8,128)}), (f32[128,256]{0,1:T(8,128)}, f32[128,256]{0,1:T(8,128)})) %all-reduce.27.cloned.1.call-update) | async-done | bytes 262160 | tf_op jit(solution)/shard_map/psum | solution.py:11
  292.2 11.7 cholesky.130
  303.9 9.8 custom-call.18
  314.2 11.7 cholesky.147
  328.1 15.5 %while.6 = (s32[]{:T(128)}, f32[256,256]{1,0:T(8,128)S(1)}, s32[2,2]{1,0:T(2,128)S(1)}, f32[2,128,128]{2,1,0:T(8,128)S(1)}, s32[]{:T(128)}) while((s32[]{:T(128)}, f32[256,256]{1,0:T(8,128)S(1)}, s32[2,2]{1,0:T(2,128)S(1)}, f32[2,128,128]{2,1,0:T(8,128)S(1)}, s32[]{:T(128)}) %tuple.78), condition=%wide.while_cond, body=%wide.while_body.sunk | while | flops 2 | bytes 131189 | solution.py:15
  344.1 19.7 %custom-call.19 = f32[2,128,128]{1,2,0:T(8,128)S(1)} custom-call(f32[2,128,128]{2,1,0:T(8,128)S(1)} %get-tuple-element.27), custom_call_target="InvertDiagBlocksLowerTriangular" | custom-call | tf_op jit(solution)/shard_map/jit(_solve_triangular)/triangular_solve | solution.py:15
  366.8 157.7 %all-reduce.25.cloned.1.call-done = (f32[4,1,128,256]{3,2,1,0:T(8,128)}, f32[4,1,128,256]{3,2,1,0:T(8,128)}) async-done(((f32[4,1,128,256]{3,2,1,0:T(8,128)}, f32[4,1,128,256]{3,2,1,0:T(8,128)}), (f32[4,1,128,256]{3,2,1,0:T(8,128)}, f32[4,1,128,256]{3,2,1,0:T(8,128)})) %all-reduce.25.cloned.1.call-update) | async-done | bytes 1048592 | tf_op jit(solution)/shard_map/psum | solution.py:11
  525.8 3.5 convolution_subtract_fusion
  530.2 116.8 %all-reduce.29.cloned.1.call-done = (f32[512,128]{0,1:T(8,128)}, f32[512,128]{0,1:T(8,128)}) async-done(((f32[512,128]{0,1:T(8,128)}, f32[512,128]{0,1:T(8,128)}), (f32[512,128]{0,1:T(8,128)}, f32[512,128]{0,1:T(8,128)})) %all-reduce.29.cloned.1.call-update) | async-done | bytes 524304 | tf_op jit(solution)/shard_map/psum | solution.py:11
  650.5 152.4 %all-reduce.23.cloned.1.call-done = (f32[128,256]{0,1:T(8,128)}, f32[128,256]{0,1:T(8,128)}) async-done(((f32[128,256]{0,1:T(8,128)}, f32[128,256]{0,1:T(8,128)}), (f32[128,256]{0,1:T(8,128)}, f32[128,256]{0,1:T(8,128)})) %all-reduce.23.cloned.1.call-update) | async-done | bytes 262160 | tf_op jit(solution)/shard_map/psum | solution.py:11
  807.3 11.7 cholesky.164
  821.1 11.3 custom-call.20
  835.2 13.2 cholesky.181
  854.3 8.3 while.7
  862.7 21.1 %custom-call.21 = f32[2,128,128]{1,2,0:T(8,128)} custom-call(f32[2,128,128]{2,1,0:T(8,128)} %get-tuple-element.28), custom_call_target="InvertDiagBlocksLowerTriangular" | custom-call | tf_op jit(solution)/shard_map/jit(_solve_triangular)/triangular_solve | solution.py:15
  892.3 157.5 %all-reduce.21.cloned.1.call-done = (f32[4,1,128,256]{3,2,1,0:T(8,128)}, f32[4,1,128,256]{3,2,1,0:T(8,128)}, f32[128,256]{0,1:T(8,128)}, f32[128,256]{0,1:T(8,128)}) async-done(((f32[4,1,128,256]{3,2,1,0:T(8,128)}, f32[4,1,128,256]{3,2,1,0:T(8,128)}, f32[128,256]{0,1:T(8,128)}, f32[128,256]{0,1:T(8,128)}), (f32[4,1,128,256]{3,2,1,0:T(8,128)}, f32[4,1,128,256]{3,2,1,0:T(8,128)}, f32[128,256]{0,1:T(8,128)}, ...) | async-done | bytes 1310736 | tf_op jit(solution)/shard_map/psum | solution.py:11
  1053.4 14.1 while.5
  1067.5 40.1 %custom-call.15 = f32[4,128,128]{1,2,0:T(8,128)S(1)} custom-call(f32[4,128,128]{2,1,0:T(8,128)} %get-tuple-element.20), custom_call_target="InvertDiagBlocksLowerTriangular" | custom-call | tf_op jit(solution)/shard_map/jit(_solve_triangular)/triangular_solve | solution.py:15
  1114.5 3.1 convolution_multiply_fusion
  1119.1 3.3 subtract_select_fusion
  1126.3 272.4 %all-reduce.19.cloned.1.call-done = f32[512,1024]{1,0:T(8,128)} async-done(((f32[512,1024]{1,0:T(8,128)}), f32[512,1024]{1,0:T(8,128)}) %all-reduce.19.cloned.1.call-update) | async-done | bytes 2097168 | tf_op jit(solution)/shard_map/psum | solution.py:86
  1399.5 3.6 fusion.10
  (141 shorter events, 84.3 us)
Async XLA Ops:
  7.2 127.0 %all-reduce.31.cloned.1.call-start = ((), (), s32[]{:S(2)}) async-start(), calls=%async_computation.6 | async-start | bytes 1048576 | tf_op jit(solution)/shard_map/psum | solution.py:11
  12.5 279.6 %copy-start = (f32[512,1024]{0,1:T(8,128)}, f32[512,1024]{0,1:T(8,128)S(1)}, u32[]{:S(2)}) copy-start(f32[512,1024]{0,1:T(8,128)S(1)} %copy.28) | copy-start | bytes 6291460
  13.5 276.6 %all-reduce.27.cloned.1.call-start = ((), (), s32[]{:S(2)}) async-start(), calls=%async_computation.4 | async-start | bytes 524288 | tf_op jit(solution)/shard_map/psum | solution.py:11
  136.1 154.0 %copy-start.2 = (f32[512,256]{0,1:T(8,128)}, f32[512,256]{0,1:T(8,128)S(1)}, u32[]{:S(2)}) copy-start(f32[512,256]{0,1:T(8,128)S(1)} %constant_dynamic-update-slice_fusion) | copy-start | bytes 1572868
  137.1 387.5 %all-reduce.25.cloned.1.call-start = ((), (), s32[]{:S(2)}) async-start(), calls=%async_computation.3 | async-start | bytes 2097152 | tf_op jit(solution)/shard_map/psum | solution.py:11
  303.9 60.8 %copy-start.3 = (f32[512,256]{0,1:T(8,128)S(1)}, f32[512,256]{0,1:T(8,128)}, u32[]{:S(2)}) copy-start(f32[512,256]{0,1:T(8,128)} %copy-done.2) | copy-start | bytes 1572868
  303.9 60.8 %copy-start.12 = (pred[512]{0:T(512)(128)(4,1)S(1)}, pred[512]{0:T(512)(128)(4,1)}, u32[]{:S(2)}) copy-start(pred[512]{0:T(512)(128)(4,1)} %get-tuple-element.77) | copy-start | bytes 1540
  343.6 0.5 copy-start.13
  364.6 161.2 %copy-start.5 = (f32[128,256]{1,0:T(8,128)}, f32[128,256]{1,0:T(8,128)S(1)}, u32[]{:S(2)}) copy-start(f32[128,256]{1,0:T(8,128)S(1)} %fusion.56) | copy-start | bytes 393220
  366.8 280.2 %all-reduce.29.cloned.1.call-start = ((), (), s32[]{:S(2)}) async-start(), calls=%async_computation.5 | async-start | bytes 1048576 | tf_op jit(solution)/shard_map/psum | solution.py:11
  530.2 272.7 %all-reduce.23.cloned.1.call-start = ((), (), s32[]{:S(2)}) async-start(), calls=%async_computation.2 | async-start | bytes 524288 | tf_op jit(solution)/shard_map/psum | solution.py:11
  648.9 0.8 copy-start.4
  650.4 399.3 %all-reduce.21.cloned.1.call-start = ((), (), s32[]{:S(2)}) async-start(), calls=%async_computation.1 | async-start | bytes 2621440 | tf_op jit(solution)/shard_map/psum | solution.py:11
  806.6 0.7 copy-start.7
  819.0 0.6 copy-start.10
  849.9 2.0 copy-start.6
  853.6 33.6 %copy-start.1 = (f32[256,256]{1,0:T(8,128)}, f32[256,256]{1,0:T(8,128)S(1)}, u32[]{:S(2)}) copy-start(f32[256,256]{1,0:T(8,128)S(1)} %get-tuple-element.74) | copy-start | bytes 786436
  890.4 508.3 %all-reduce.19.cloned.1.call-start = ((), (), s32[]{:S(2)}) async-start(), calls=%async_computation | async-start | bytes 4194304 | tf_op jit(solution)/shard_map/psum | solution.py:86
  1110.1 4.5 copy-start.11
  1117.7 1.2 copy-start.8
  1117.7 1.3 copy-start.9
Sparse Core Ops, SparseCore 0:
  13.6 120.5 all-reduce.30
  138.1 151.9 all-reduce.26
  366.9 157.6 all-reduce.24
  530.3 116.6 all-reduce.28
  650.9 151.9 all-reduce.22
  890.5 159.2 all-reduce.20
  1117.8 280.8 all-reduce.18
where the time goes:
time: 1420 us; the launch traced here: 1410 us
  waiting for transfers between devices  1130 us (80%)
  other arithmetic  167 us (12%)
  local copies, waits for them, and re-layouts  49.1 us (3%)
  matrix products  34.7 us (2%)
  between operations  17.6 us (1%)
    psum x6, waiting for transfers between devices, broadcast(): return lax.psum(block, axis)  857 us
    psum x1, waiting for transfers between devices, per_device(): solution = lax.psum(term, ('row', 'col'))  272 us
    another operation x8, other arithmetic, tri_solve(): return jax.scipy.linalg.solve_triangular(lower, rhs, lower=True)  84.7 us
    another operation x13, other arithmetic, per_device(): lower = jnp.linalg.cholesky(leading[0:width])  73.1 us
  transfers between devices with their start and end apart: 7, of which 7 were waited for; matrix products, arithmetic and copies ran while one was open for 1% of the time, Pallas kernels for 0%

commit v1 on v0

v1 whole, which is shorter than its diff:
```python
import functools

import jax
import jax.numpy as jnp
from jax import lax
from jax.experimental import pallas as pl
from jax.experimental.pallas import tpu as pltpu
from jax.sharding import PartitionSpec as P

highest = lax.Precision.HIGHEST
TB = 128
LEAD = 512
TILES = LEAD // TB
PAIRS = [(i, j) for i in range(TILES) for j in range(i + 1)]
SLOT = 4 * len(PAIRS) + 16
VMEM = pl.BlockSpec(memory_space=pltpu.VMEM)
SMEM = pl.BlockSpec(memory_space=pltpu.SMEM)


def dot(a, b):
    return jnp.dot(a, b, precision=highest, preferred_element_type=jnp.float32)


def dot_nt(a, b):
    return lax.dot_general(
        a, b, (((1,), (1,)), ((), ())), precision=highest, preferred_element_type=jnp.float32
    )


def recip(p):
    r = pltpu.reciprocal(p, approx=True)
    return r * (2.0 - p * r)


def factor_tile(m_ref):
    n, w = TB, 8
    for g in range(n // w):
        base = w * g
        rows = [jnp.broadcast_to(m_ref[base + k : base + k + 1, 0:n], (8, n)) for k in range(w)]
        erow = [jnp.broadcast_to(m_ref[base + k : base + k + 1, n:], (8, n)) for k in range(w)]
        a, l, r = {}, {}, {}
        for k in range(w):
            for i in range(k + 1):
                a[k, i] = jnp.broadcast_to(rows[k][:, base + i : base + i + 1], (8, n))
        for i in range(w):
            r[i] = recip(a[i, i])
            for k in range(i + 1, w):
                l[k, i] = a[k, i] * r[i]
            for k in range(i + 1, w):
                for j in range(i + 1, k + 1):
                    a[k, j] = a[k, j] - l[k, i] * a[j, i]
                rows[k] = rows[k] - l[k, i] * rows[i]
                erow[k] = erow[k] - l[k, i] * erow[i]
        for k in range(w):
            m_ref[base + k : base + k + 1, n:] = (erow[k] * lax.rsqrt(a[k, k]))[0:1]
        if g == n // w - 1:
            break
        q = [rows[k] * r[k] for k in range(w)]
        qe = [erow[k] * r[k] for k in range(w)]
        for k in range(w - 1, -1, -1):
            for m in range(k + 1, w):
                q[k] = q[k] - l[m, k] * q[m]
                qe[k] = qe[k] - l[m, k] * qe[m]
        for rb in range(g + 1, n // w):
            d = m_ref[8 * rb : 8 * rb + 8, 0:n]
            e = m_ref[8 * rb : 8 * rb + 8, n:]
            cols = [jnp.broadcast_to(d[:, base + k : base + k + 1], (8, n)) for k in range(w)]
            for k in range(w):
                d = d - cols[k] * q[k]
                e = e - cols[k] * qe[k]
            m_ref[8 * rb : 8 * rb + 8, 0:n] = d
            m_ref[8 * rb : 8 * rb + 8, n:] = e


def chol_kernel(slots_ref, x_ref, s_ref, m_ref):
    n = TB
    for p, (i, j) in enumerate(PAIRS):
        for t in range(32):
            s_ref[n * i + 4 * t : n * i + 4 * t + 4, n * j : n * j + n] = slots_ref[
                SLOT * t + 4 * p : SLOT * t + 4 * p + 4, :
            ]
    eye = (
        lax.broadcasted_iota(jnp.int32, (n, n), 0) == lax.broadcasted_iota(jnp.int32, (n, n), 1)
    ).astype(jnp.float32)
    for k in range(TILES):
        sl = slice(n * k, n * k + n)
        m_ref[:, 0:n] = s_ref[sl, sl]
        m_ref[:, n:] = eye
        factor_tile(m_ref)
        inv = m_ref[:, n:]
        if k > 0:
            x_ref[sl, 0 : n * k] = -dot(inv, dot(s_ref[sl, 0 : n * k], x_ref[0 : n * k, 0 : n * k]))
        x_ref[sl, sl] = inv
        if k < TILES - 1:
            x_ref[sl, n * (k + 1) :] = jnp.zeros((n, LEAD - n * (k + 1)), jnp.float32)
            low = dot_nt(s_ref[n * (k + 1) :, sl], inv)
            s_ref[n * (k + 1) :, sl] = low
            for j in range(k + 1, TILES):
                o = n * (j - k - 1)
                s_ref[n * j :, n * j : n * j + n] = s_ref[n * j :, n * j : n * j + n] - dot_nt(
                    low[o:], low[o : o + n]
                )


def final_kernel(
    ids_ref, x_ref, slots_ref, kernel_ref,
    p0, p1, p2, p3, v0, v1, v2, v3,
    factor_ref, out_ref, z_ref,
    p_ref, v_ref, f_ref, y_ref, w_ref,
):
    n = TB
    my_row, my_col = ids_ref[0], ids_ref[1]
    x, core = lax.rem(my_row, 4), lax.rem(my_col, 2)
    group = lax.rem(my_col, 4)
    for k, src in enumerate((p0, p1, p2, p3)):
        p_ref[:, pl.ds(pl.multiple_of((group ^ k) * n, n), n)] = src[...]
    for k, src in enumerate((v0, v1, v2, v3)):
        at = pl.ds(pl.multiple_of((x ^ k) * n, n), n)
        for b in range(8):
            v_ref[at, n * b : n * b + n] = src[pl.ds(b, n, stride=8), :]
    for i in range(TILES):
        for c in range(16):
            y_ref[n * i + 8 * c : n * i + 8 * c + 8, :] = slots_ref[
                pl.ds(8 * i * SLOT + 4 * len(PAIRS) + c, 8, stride=SLOT), :
            ]
    row = lax.broadcasted_iota(jnp.int32, (LEAD, n), 0)
    col = lax.broadcasted_iota(jnp.int32, (LEAD, n), 1)
    whole_row = (row // n * 32 + my_row) * n + lax.rem(row, n)
    for i in range(TILES):
        upto = n * (i + 1)
        sl = slice(n * i, upto)
        inv = x_ref[sl, 0:upto]
        f = dot_nt(p_ref[:, 0:upto], inv)
        factor_ref[:, sl] = jnp.where(col + n * i <= whole_row, f, 0.0)
        w_ref[sl, :] = dot(inv, y_ref[0:upto, :])
        f_ref[sl, :] = dot(inv, v_ref[0:upto, :])
    z_ref[...] = dot(factor_ref[pl.ds(pl.multiple_of(core * 256, 256), 256), :], w_ref[...])

    @pl.when((my_row < TILES) & (core == 0))
    def _():
        z_ref[0:n, :] = w_ref[pl.ds(pl.multiple_of(my_row * n, n), n), :]

    @pl.loop(0, 4)
    def _(h):
        update = dot(factor_ref[...], f_ref[:, pl.ds(pl.multiple_of(h * 256, 256), 256)])
        for half in range(2):
            b = 2 * h + half
            at = pl.ds(b, LEAD, stride=8)
            left = kernel_ref[at, :] - update[:, n * half : n * half + n]
            drop = ((row < n) & (my_row < TILES)) | ((b == 0) & (my_col < TILES))
            out_ref[at, :] = jnp.where(drop, 0.0, left)


def per_device(kernel, targets):
    my_row = lax.axis_index("row")
    my_col = lax.axis_index("col")
    f32 = jnp.float32

    own = kernel[:, :, 0, :].reshape(LEAD, TB)
    got = [lax.ppermute(own, "col", [(c, c + d) for c in range(4)]) for d in (4, 8, 12)]
    own = jnp.where(my_col < 4, own, got[0] + got[1] + got[2])
    panel = [own] + [lax.ppermute(own, "col", [(c, c ^ k) for c in range(16)]) for k in (1, 2, 3)]

    lead = kernel[0].reshape(8 * TB, TB)
    have = [0]
    for d in (16, 8, 4):
        got = lax.ppermute(lead, "row", [(z + x, z + x + d) for z in have for x in range(4)])
        new = functools.reduce(jnp.logical_or, [my_row // 4 == (z + d) // 4 for z in have])
        lead = jnp.where(new, got, lead)
        have = have + [z + d for z in have]
    leads = [lead] + [lax.ppermute(lead, "row", [(r, r ^ k) for r in range(32)]) for k in (1, 2, 3)]

    tile = kernel[0, :, 0, :].reshape(32, 4, TB)
    wide = targets[0, 0].reshape(8, 8, TB)
    wide = jnp.broadcast_to(wide[None], (4, 8, 8, TB)).reshape(32, 8, TB)
    got = lax.all_to_all(jnp.concatenate([tile, wide], axis=1), "row", 0, 0)
    part = got[0:4, 0:4].reshape(1, 16, TB)
    wide = lax.dynamic_index_in_dim(got, my_row // 8, 0, keepdims=False)[4:12]
    send = jnp.concatenate(
        [jnp.broadcast_to(part, (16, 16, TB)), jnp.repeat(wide, 2, axis=0)[:, None]], axis=1
    )
    got = lax.all_to_all(send, "col", 0, 0)
    part = got[0:4, 0:16].reshape(4, 4, 4, TB)
    slot = jnp.concatenate([part[j, i] for i, j in PAIRS] + [got[:, 16]], axis=0)
    slots = lax.all_to_all(jnp.broadcast_to(slot[None], (32, SLOT, TB)), "row", 0, 0)
    slots = slots.reshape(32 * SLOT, TB)

    inverse = pl.pallas_call(
        chol_kernel,
        out_shape=jax.ShapeDtypeStruct((LEAD, LEAD), f32),
        in_specs=[VMEM],
        out_specs=VMEM,
        scratch_shapes=[pltpu.VMEM((LEAD, LEAD), f32), pltpu.VMEM((TB, 2 * TB), f32)],
        compiler_params=pltpu.CompilerParams(vmem_limit_bytes=16 << 20),
        cost_estimate=pl.CostEstimate(flops=2 * 10**10, bytes_accessed=3 << 20, transcendentals=0),
    )(slots)

    ids = jnp.stack([my_row, my_col]).astype(jnp.int32)
    factor, trailing, z = pl.pallas_call(
        final_kernel,
        out_shape=[
            jax.ShapeDtypeStruct((LEAD, LEAD), f32),
            jax.ShapeDtypeStruct((8 * LEAD, TB), f32),
            jax.ShapeDtypeStruct((2 * TB, TB), f32),
        ],
        in_specs=[SMEM] + [VMEM] * 11,
        out_specs=[VMEM] * 3,
        scratch_shapes=[
            pltpu.VMEM((LEAD, LEAD), f32),
            pltpu.VMEM((LEAD, 8 * TB), f32),
            pltpu.VMEM((LEAD, 8 * TB), f32),
            pltpu.VMEM((LEAD, TB), f32),
            pltpu.VMEM((LEAD, TB), f32),
        ],
        compiler_params=pltpu.CompilerParams(vmem_limit_bytes=40 << 20),
        cost_estimate=pl.CostEstimate(flops=10**10, bytes_accessed=10 << 20, transcendentals=0),
    )(ids, inverse, slots, kernel.reshape(8 * LEAD, TB), *panel, *leads)

    send = z.reshape(2, 16, 8, TB).transpose(1, 0, 2, 3)
    got = lax.all_to_all(send, "col", 0, 0).reshape(8, 2, 2, 8, TB)
    got = got.transpose(1, 2, 3, 0, 4).reshape(4, 8, 8 * TB)
    top = (jnp.arange(4, dtype=jnp.int32) == 0)[:, None, None] & (my_row < TILES)
    targets_out = jnp.where(top, got, targets[:, 0] - got)[:, None]
    return (
        factor.reshape(4, TB, LEAD),
        trailing.reshape(kernel.shape),
        targets_out,
    )


def solution(mesh):
    return jax.shard_map(
        per_device,
        mesh=mesh,
        in_specs=(P(None, "row", None, "col"), P(None, "row", "col", None)),
        out_specs=(P(None, "row", None), P(None, "row", None, "col"), P(None, "row", "col", None)),
        check_vma=False,
    )
```

time: 1420 us -> 186 us (0.13)
  waiting for transfers between devices: 1130 us -> 60.4 us
  other arithmetic: 167 us -> 7.4 us
  starting transfers between devices: 0.29 us -> 74.6 us
  local copies, waits for them, and re-layouts: 49.1 us -> 6.3 us
  Pallas kernels: 0 us -> 35.5 us
  matrix products: 34.7 us -> 0 us
  between operations: 17.6 us -> 0.91 us
    psum x7 -> x0, waiting for transfers between devices: 1130 us -> none  [the longest x6 857 us: broadcast(): return lax.psum(block, axis)]
    another operation x23 -> x1, other arithmetic: 159 us -> 0.07 us  [per_device(): ids = jnp.stack([my_row, my_col]).astype(jnp.int32)]
    ppermute x0 -> x12, starting transfers between devices: none -> 40.7 us  [the longest x3 14.9 us: per_device(): lax.ppermute(lead, 'row', [(z + x, z + x + d) for z in have for x in rang...]
    ppermute x0 -> x12, waiting for transfers between devices: none -> 38.8 us  [the longest x3 26.5 us: per_device(): lax.ppermute(lead, 'row', [(z + x, z + x + d) for z in have for x in rang...]
    pallas_call x0 -> x2, Pallas kernels: none -> 35.5 us  [the longest x1 21.7 us: per_device(): pl.pallas_call(chol_kernel, out_shape=jax.ShapeDtypeStruct((LEAD, LEAD),...]
    all_to_all x0 -> x4, starting transfers between devices: none -> 33.9 us  [the longest x1 13.7 us: per_device(): got = lax.all_to_all(jnp.concatenate([tile, wide], axis=1), 'row', 0, 0)]
    another operation x32 -> x1, local copies, waits for them, and re-layouts: 27.9 us -> 1.08 us  [per_device(): lead = kernel[0].reshape(8 * TB, TB)]
    all_to_all x0 -> x4, waiting for transfers between devices: none -> 21.6 us  [the longest x1 10.3 us: per_device(): got = lax.all_to_all(send, 'col', 0, 0)]
  transfers between devices with their start and end apart: 7 -> 16, of which waited for: 7 -> 5; matrix products, arithmetic and copies ran while one was open for 1% -> 4% of each run, Pallas kernels for 0% -> 12%
where the time goes in v1:
time: 186 us; the launch traced here: 185 us
  starting transfers between devices  74.6 us (40%)
  waiting for transfers between devices  60.4 us (32%)
  Pallas kernels  35.5 us (19%)
  other arithmetic  7.4 us (4%)
  local copies, waits for them, and re-layouts  6.3 us (3%)
    ppermute x3, waiting for transfers between devices, per_device(): lax.ppermute(lead, 'row', [(z + x, z + x + d) for z in have for x in rang...  26.5 us
    pallas_call x1, Pallas kernels, per_device(): pl.pallas_call(chol_kernel, out_shape=jax.ShapeDtypeStruct((LEAD, LEAD),...  21.7 us
    ppermute x3, starting transfers between devices, per_device(): lax.ppermute(lead, 'row', [(z + x, z + x + d) for z in have for x in rang...  14.9 us
    pallas_call x1, Pallas kernels, per_device(): pl.pallas_call(final_kernel, out_shape=[jax.ShapeDtypeStruct((LEAD, LEAD)...  13.8 us
    all_to_all x1, starting transfers between devices, per_device(): got = lax.all_to_all(jnp.concatenate([tile, wide], axis=1), 'row', 0, 0)  13.7 us
    ppermute x3, waiting for transfers between devices, per_device(): lax.ppermute(own, 'col', [(c, c + d) for c in range(4)])  12.3 us
    all_to_all x1, waiting for transfers between devices, per_device(): got = lax.all_to_all(send, 'col', 0, 0)  10.3 us
    ppermute x3, starting transfers between devices, per_device(): lax.ppermute(own, 'col', [(c, c ^ k) for c in range(16)])  10.2 us
  transfers between devices with their start and end apart: 16, of which 5 were waited for; matrix products, arithmetic and copies ran while one was open for 4% of the time, Pallas kernels for 12%

profile of v1, /device:TPU:1, one launch (start us, length us, event | category | flops | bytes accessed | tf_op | source)
XLA Modules:
  0.0 185.0 jit_solution(10657786665562049347)
XLA Ops:
  3.2 13.7 %all-to-all-start = ((f32[32,12,128]{2,1,0:T(8,128)}), f32[32,12,128]{2,1,0:T(8,128)S(1)}, u32[]{:S(2)}, u32[]{:S(2)}) async-start(f32[32,12,128]{2,1,0:T(8,128)} %pad_maximum_fusion), calls=%async_computation | async-start | bytes 524288 | tf_op jit(solution)/shard_map/all_to_all | solution.py:176
  18.1 8.0 %collective-permute-start.6 = (f32[1024,128]{1,0:T(8,128)S(1)}, f32[1024,128]{1,0:T(8,128)}, u32[]{:S(2)}, u32[]{:S(2)}) collective-permute-start(f32[1024,128]{1,0:T(8,128)S(1)} %slice_bitcast_fusion), channel_id=1, source_target_pairs={{0,256},{16,272},{32,288},{48,304},{1,257},{17,273},{33,289},{49,3... | collective-permute-start | bytes 1572872 | tf_op jit(solution)/shard_map/ppermute | solution.py:167
  26.0 2.1 %all-to-all-done = f32[32,12,128]{2,1,0:T(8,128)S(1)} async-done(((f32[32,12,128]{2,1,0:T(8,128)}), f32[32,12,128]{2,1,0:T(8,128)S(1)}, u32[]{:S(2)}, u32[]{:S(2)}) %all-to-all-start) | async-done | bytes 196640 | tf_op jit(solution)/shard_map/all_to_all | solution.py:176
  28.9 9.6 %all-to-all-start.1 = ((f32[16,17,128]{2,1,0:T(8,128)}), f32[16,17,128]{2,1,0:T(8,128)S(1)}, u32[]{:S(2)}, u32[]{:S(2)}) async-start(f32[16,17,128]{2,1,0:T(8,128)} %pad_maximum_fusion.1), calls=%async_computation.1 | async-start | bytes 393216 | tf_op jit(solution)/shard_map/all_to_all | solution.py:182
  38.5 10.3 %all-to-all-done.1 = f32[16,17,128]{2,1,0:T(8,128)S(1)} async-done(((f32[16,17,128]{2,1,0:T(8,128)}), f32[16,17,128]{2,1,0:T(8,128)S(1)}, u32[]{:S(2)}, u32[]{:S(2)}) %all-to-all-start.1) | async-done | bytes 139296 | tf_op jit(solution)/shard_map/all_to_all | solution.py:182
  49.9 3.9 %all-to-all-start.2 = ((f32[32,56,128]{2,1,0:T(8,128)}), f32[32,56,128]{2,1,0:T(8,128)S(1)}, u32[]{:S(2)}, u32[]{:S(2)}) async-start(f32[32,56,128]{2,1,0:T(8,128)} %broadcast_in_dim.38), calls=%async_computation.2 | async-start | bytes 1835008 | tf_op jit(solution)/shard_map/all_to_all | solution.py:185
  53.9 4.8 %collective-permute-start.7 = (f32[1024,128]{1,0:T(8,128)S(1)}, f32[1024,128]{1,0:T(8,128)}, u32[]{:S(2)}, u32[]{:S(2)}) collective-permute-start(f32[1024,128]{1,0:T(8,128)S(1)} %broadcast_select_fusion), channel_id=1, source_target_pairs={{0,128},{16,144},{32,160},{48,176},{256,384},{272,400},{288,416},{... | collective-permute-start | bytes 1572872 | tf_op jit(solution)/shard_map/ppermute | solution.py:167
  58.7 26.5 %collective-permute-done.7 = f32[1024,128]{1,0:T(8,128)} collective-permute-done((f32[1024,128]{1,0:T(8,128)S(1)}, f32[1024,128]{1,0:T(8,128)}, u32[]{:S(2)}, u32[]{:S(2)}) %collective-permute-start.7) | collective-permute-done | bytes 524320 | tf_op jit(solution)/shard_map/ppermute | solution.py:167
  86.3 2.1 %collective-permute-start.8 = (f32[1024,128]{1,0:T(8,128)S(1)}, f32[1024,128]{1,0:T(8,128)}, u32[]{:S(2)}, u32[]{:S(2)}) collective-permute-start(f32[1024,128]{1,0:T(8,128)S(1)} %broadcast_select_fusion.1), channel_id=1, source_target_pairs={{0,64},{16,80},{32,96},{48,112},{256,320},{272,336},{288,352},{304... | collective-permute-start | bytes 1572872 | tf_op jit(solution)/shard_map/ppermute | solution.py:167
  89.2 2.5 %collective-permute-start.2 = (f32[512,128]{1,0:T(8,128)}, f32[512,128]{1,0:T(8,128)}, u32[]{:S(2)}, u32[]{:S(2)}) collective-permute-start(f32[512,128]{1,0:T(8,128)} %bitcast.22), channel_id=1, source_target_pairs={{0,12},{1,13},{2,14},{3,15},{16,28},{17,29},{18,30},{19,31},{32,44... | collective-permute-start | bytes 786440 | tf_op jit(solution)/shard_map/ppermute | solution.py:160
  91.7 2.0 %collective-permute-start.1 = (f32[512,128]{1,0:T(8,128)}, f32[512,128]{1,0:T(8,128)}, u32[]{:S(2)}, u32[]{:S(2)}) collective-permute-start(f32[512,128]{1,0:T(8,128)} %bitcast.22), channel_id=1, source_target_pairs={{0,8},{1,9},{2,10},{3,11},{16,24},{17,25},{18,26},{19,27},{32,40},... | collective-permute-start | bytes 786440 | tf_op jit(solution)/shard_map/ppermute | solution.py:160
  93.7 2.0 %collective-permute-start = (f32[512,128]{1,0:T(8,128)}, f32[512,128]{1,0:T(8,128)}, u32[]{:S(2)}, u32[]{:S(2)}) collective-permute-start(f32[512,128]{1,0:T(8,128)} %bitcast.22), channel_id=1, source_target_pairs={{0,4},{1,5},{2,6},{3,7},{16,20},{17,21},{18,22},{19,23},{32,36},{3... | collective-permute-start | bytes 786440 | tf_op jit(solution)/shard_map/ppermute | solution.py:160
  95.8 12.3 %collective-permute-done.2 = f32[512,128]{1,0:T(8,128)} collective-permute-done((f32[512,128]{1,0:T(8,128)}, f32[512,128]{1,0:T(8,128)}, u32[]{:S(2)}, u32[]{:S(2)}) %collective-permute-start.2) | collective-permute-done | bytes 262176 | tf_op jit(solution)/shard_map/ppermute | solution.py:160
  108.1 2.0 %add_select_fusion.p0 = f32[512,128]{1,0:T(8,128)} fusion(f32[512,128]{1,0:T(8,128)} %bitcast.22, f32[512,128]{1,0:T(8,128)} %collective-permute-done.2, f32[512,128]{1,0:T(8,128)} %collective-permute-done, f32[512,128]{1,0:T(8,128)} %collective-permute-done.1, pred[]{:T(512)S(6)} %lt.11), kind=kLoop, calls=%fused_computation.2 | loop fusion | flops 196608 | bytes 1310721 | tf_op jit(solution)/shard_map/jit(_where)/select_n | solution.py:161
  110.0 6.0 %collective-permute-start.5 = (f32[512,128]{1,0:T(8,128)}, f32[512,128]{1,0:T(8,128)S(1)}, u32[]{:S(2)}, u32[]{:S(2)}) collective-permute-start(f32[512,128]{1,0:T(8,128)} %add_select_fusion.p0), channel_id=1, source_target_pairs={{0,3},{1,2},{2,1},{3,0},{4,7},{5,6},{6,5},{7,4},{8,11},{9,10},{10,... | collective-permute-start | bytes 786440 | tf_op jit(solution)/shard_map/ppermute | solution.py:162
  116.0 1.9 %collective-permute-start.4 = (f32[512,128]{1,0:T(8,128)}, f32[512,128]{1,0:T(8,128)}, u32[]{:S(2)}, u32[]{:S(2)}) collective-permute-start(f32[512,128]{1,0:T(8,128)} %add_select_fusion.p0), channel_id=1, source_target_pairs={{0,2},{1,3},{2,0},{3,1},{4,6},{5,7},{6,4},{7,5},{8,10},{9,11},{10,... | collective-permute-start | bytes 786440 | tf_op jit(solution)/shard_map/ppermute | solution.py:162
  117.9 2.3 %collective-permute-start.3 = (f32[512,128]{1,0:T(8,128)}, f32[512,128]{1,0:T(8,128)}, u32[]{:S(2)}, u32[]{:S(2)}) collective-permute-start(f32[512,128]{1,0:T(8,128)} %add_select_fusion.p0), channel_id=1, source_target_pairs={{0,1},{1,0},{2,3},{3,2},{4,5},{5,4},{6,7},{7,6},{8,9},{9,8},{10,11... | collective-permute-start | bytes 786440 | tf_op jit(solution)/shard_map/ppermute | solution.py:162
  121.4 3.9 %collective-permute-start.11 = (f32[1024,128]{1,0:T(8,128)S(1)}, f32[1024,128]{1,0:T(8,128)}, u32[]{:S(2)}, u32[]{:S(2)}) collective-permute-start(f32[1024,128]{1,0:T(8,128)S(1)} %broadcast_select_fusion.2.v0), channel_id=1, source_target_pairs={{0,48},{16,32},{32,16},{48,0},{64,112},{80,96},{96,80},{112,64},{1... | collective-permute-start | bytes 1572872 | tf_op jit(solution)/shard_map/ppermute | solution.py:171
  125.3 2.5 %collective-permute-start.10 = (f32[1024,128]{1,0:T(8,128)S(1)}, f32[1024,128]{1,0:T(8,128)}, u32[]{:S(2)}, u32[]{:S(2)}) collective-permute-start(f32[1024,128]{1,0:T(8,128)S(1)} %broadcast_select_fusion.2.v0), channel_id=1, source_target_pairs={{0,32},{16,48},{32,0},{48,16},{64,96},{80,112},{96,64},{112,80},{1... | collective-permute-start | bytes 1572872 | tf_op jit(solution)/shard_map/ppermute | solution.py:171
  128.5 2.7 %collective-permute-start.9 = (f32[1024,128]{1,0:T(8,128)S(1)}, f32[1024,128]{1,0:T(8,128)}, u32[]{:S(2)}, u32[]{:S(2)}) collective-permute-start(f32[1024,128]{1,0:T(8,128)S(1)} %broadcast_select_fusion.2.v0), channel_id=1, source_target_pairs={{0,16},{16,0},{32,48},{48,32},{64,80},{80,64},{96,112},{112,96},{1... | collective-permute-start | bytes 1572872 | tf_op jit(solution)/shard_map/ppermute | solution.py:171
  131.3 21.7 %shard_map.49.x_ref = f32[512,512]{1,0:T(8,128)S(1)} custom-call(f32[1792,128]{1,0:T(8,128)S(1)} %bitcast.49), custom_call_target="tpu_custom_call" | custom-call | flops 20000000000 | bytes 3145728 | tf_op jit(solution)/shard_map/pallas_call | solution.py:188
  153.0 13.8 %shard_map.50 = (f32[512,512]{1,0:T(8,128)}, f32[4096,128]{1,0:T(8,128)}, f32[256,128]{1,0:T(8,128)S(1)}) custom-call(s32[2]{0:T(128)S(1)} %pad_add_fusion.ids_ref, f32[512,512]{1,0:T(8,128)S(1)} %shard_map.49.x_ref, f32[1792,128]{1,0:T(8,128)S(1)} %bitcast.50, f32[4096,128]{1,0:T(8,128)S(1)} %bitcast.51, f32[512,128]{1,0:T(8,128)} %add_select_fusion.p0, ...), custom_call_target="tpu_custom_call" | custom-call | flops 10000000000 | bytes 10485760 | tf_op jit(solution)/shard_map/pallas_call | solution.py:199
  167.5 6.7 %all-to-all-start.3 = ((f32[16,2,8,128]{3,2,1,0:T(8,128)}), f32[16,2,8,128]{3,2,1,0:T(8,128)S(1)}, u32[]{:S(2)}, u32[]{:S(2)}) async-start(f32[16,2,8,128]{3,2,1,0:T(8,128)} %bitcast.48), calls=%async_computation.3 | async-start | bytes 262144 | tf_op jit(solution)/shard_map/all_to_all | solution.py:220
  174.2 9.2 %all-to-all-done.3 = f32[16,2,8,128]{3,2,1,0:T(8,128)S(1)} async-done(((f32[16,2,8,128]{3,2,1,0:T(8,128)}), f32[16,2,8,128]{3,2,1,0:T(8,128)S(1)}, u32[]{:S(2)}, u32[]{:S(2)}) %all-to-all-start.3) | async-done | bytes 131104 | tf_op jit(solution)/shard_map/all_to_all | solution.py:220
  (46 shorter events, 11.8 us)
Async XLA Ops:
  3.2 24.9 %all-to-all-start = ((f32[32,12,128]{2,1,0:T(8,128)}), f32[32,12,128]{2,1,0:T(8,128)S(1)}, u32[]{:S(2)}, u32[]{:S(2)}) async-start(f32[32,12,128]{2,1,0:T(8,128)} %pad_maximum_fusion), calls=%async_computation | async-start | bytes 524288 | tf_op jit(solution)/shard_map/all_to_all | solution.py:176
  18.0 35.8 %copy-start = (f32[4,128,8,128]{3,2,1,0:T(8,128)S(1)}, f32[4,128,8,128]{3,2,1,0:T(8,128)}, u32[]{:S(2)}) copy-start(f32[4,128,8,128]{3,2,1,0:T(8,128)} %param.2) | copy-start | bytes 6291460
  18.1 35.8 %collective-permute-start.6 = (f32[1024,128]{1,0:T(8,128)S(1)}, f32[1024,128]{1,0:T(8,128)}, u32[]{:S(2)}, u32[]{:S(2)}) collective-permute-start(f32[1024,128]{1,0:T(8,128)S(1)} %slice_bitcast_fusion), channel_id=1, source_target_pairs={{0,256},{16,272},{32,288},{48,304},{1,257},{17,273},{33,289},{49,3... | collective-permute-start | bytes 1572872 | tf_op jit(solution)/shard_map/ppermute | solution.py:167
  28.9 19.9 %all-to-all-start.1 = ((f32[16,17,128]{2,1,0:T(8,128)}), f32[16,17,128]{2,1,0:T(8,128)S(1)}, u32[]{:S(2)}, u32[]{:S(2)}) async-start(f32[16,17,128]{2,1,0:T(8,128)} %pad_maximum_fusion.1), calls=%async_computation.1 | async-start | bytes 393216 | tf_op jit(solution)/shard_map/all_to_all | solution.py:182
  49.9 81.4 %all-to-all-start.2 = ((f32[32,56,128]{2,1,0:T(8,128)}), f32[32,56,128]{2,1,0:T(8,128)S(1)}, u32[]{:S(2)}, u32[]{:S(2)}) async-start(f32[32,56,128]{2,1,0:T(8,128)} %broadcast_in_dim.38), calls=%async_computation.2 | async-start | bytes 1835008 | tf_op jit(solution)/shard_map/all_to_all | solution.py:185
  53.9 4.8 %copy-start.4 = (f32[1024,128]{1,0:T(8,128)}, f32[1024,128]{1,0:T(8,128)S(1)}, u32[]{:S(2)}) copy-start(f32[1024,128]{1,0:T(8,128)S(1)} %broadcast_select_fusion) | copy-start | bytes 1572868
  53.9 31.2 %collective-permute-start.7 = (f32[1024,128]{1,0:T(8,128)S(1)}, f32[1024,128]{1,0:T(8,128)}, u32[]{:S(2)}, u32[]{:S(2)}) collective-permute-start(f32[1024,128]{1,0:T(8,128)S(1)} %broadcast_select_fusion), channel_id=1, source_target_pairs={{0,128},{16,144},{32,160},{48,176},{256,384},{272,400},{288,416},{... | collective-permute-start | bytes 1572872 | tf_op jit(solution)/shard_map/ppermute | solution.py:167
  86.3 34.0 %copy-start.3 = (f32[1024,128]{1,0:T(8,128)}, f32[1024,128]{1,0:T(8,128)S(1)}, u32[]{:S(2)}) copy-start(f32[1024,128]{1,0:T(8,128)S(1)} %broadcast_select_fusion.1) | copy-start | bytes 1572868
  86.3 33.9 %collective-permute-start.8 = (f32[1024,128]{1,0:T(8,128)S(1)}, f32[1024,128]{1,0:T(8,128)}, u32[]{:S(2)}, u32[]{:S(2)}) collective-permute-start(f32[1024,128]{1,0:T(8,128)S(1)} %broadcast_select_fusion.1), channel_id=1, source_target_pairs={{0,64},{16,80},{32,96},{48,112},{256,320},{272,336},{288,352},{304... | collective-permute-start | bytes 1572872 | tf_op jit(solution)/shard_map/ppermute | solution.py:167
  89.2 18.8 %collective-permute-start.2 = (f32[512,128]{1,0:T(8,128)}, f32[512,128]{1,0:T(8,128)}, u32[]{:S(2)}, u32[]{:S(2)}) collective-permute-start(f32[512,128]{1,0:T(8,128)} %bitcast.22), channel_id=1, source_target_pairs={{0,12},{1,13},{2,14},{3,15},{16,28},{17,29},{18,30},{19,31},{32,44... | collective-permute-start | bytes 786440 | tf_op jit(solution)/shard_map/ppermute | solution.py:160
  91.7 16.3 %collective-permute-start.1 = (f32[512,128]{1,0:T(8,128)}, f32[512,128]{1,0:T(8,128)}, u32[]{:S(2)}, u32[]{:S(2)}) collective-permute-start(f32[512,128]{1,0:T(8,128)} %bitcast.22), channel_id=1, source_target_pairs={{0,8},{1,9},{2,10},{3,11},{16,24},{17,25},{18,26},{19,27},{32,40},... | collective-permute-start | bytes 786440 | tf_op jit(solution)/shard_map/ppermute | solution.py:160
  93.7 14.4 %collective-permute-start = (f32[512,128]{1,0:T(8,128)}, f32[512,128]{1,0:T(8,128)}, u32[]{:S(2)}, u32[]{:S(2)}) collective-permute-start(f32[512,128]{1,0:T(8,128)} %bitcast.22), channel_id=1, source_target_pairs={{0,4},{1,5},{2,6},{3,7},{16,20},{17,21},{18,22},{19,23},{32,36},{3... | collective-permute-start | bytes 786440 | tf_op jit(solution)/shard_map/ppermute | solution.py:160
  110.0 17.8 %collective-permute-start.5 = (f32[512,128]{1,0:T(8,128)}, f32[512,128]{1,0:T(8,128)S(1)}, u32[]{:S(2)}, u32[]{:S(2)}) collective-permute-start(f32[512,128]{1,0:T(8,128)} %add_select_fusion.p0), channel_id=1, source_target_pairs={{0,3},{1,2},{2,1},{3,0},{4,7},{5,6},{6,5},{7,4},{8,11},{9,10},{10,... | collective-permute-start | bytes 786440 | tf_op jit(solution)/shard_map/ppermute | solution.py:162
  116.0 37.0 %collective-permute-start.4 = (f32[512,128]{1,0:T(8,128)}, f32[512,128]{1,0:T(8,128)}, u32[]{:S(2)}, u32[]{:S(2)}) collective-permute-start(f32[512,128]{1,0:T(8,128)} %add_select_fusion.p0), channel_id=1, source_target_pairs={{0,2},{1,3},{2,0},{3,1},{4,6},{5,7},{6,4},{7,5},{8,10},{9,11},{10,... | collective-permute-start | bytes 786440 | tf_op jit(solution)/shard_map/ppermute | solution.py:162
  117.9 35.1 %collective-permute-start.3 = (f32[512,128]{1,0:T(8,128)}, f32[512,128]{1,0:T(8,128)}, u32[]{:S(2)}, u32[]{:S(2)}) collective-permute-start(f32[512,128]{1,0:T(8,128)} %add_select_fusion.p0), channel_id=1, source_target_pairs={{0,1},{1,0},{2,3},{3,2},{4,5},{5,4},{6,7},{7,6},{8,9},{9,8},{10,11... | collective-permute-start | bytes 786440 | tf_op jit(solution)/shard_map/ppermute | solution.py:162
  121.4 31.6 %collective-permute-start.11 = (f32[1024,128]{1,0:T(8,128)S(1)}, f32[1024,128]{1,0:T(8,128)}, u32[]{:S(2)}, u32[]{:S(2)}) collective-permute-start(f32[1024,128]{1,0:T(8,128)S(1)} %broadcast_select_fusion.2.v0), channel_id=1, source_target_pairs={{0,48},{16,32},{32,16},{48,0},{64,112},{80,96},{96,80},{112,64},{1... | collective-permute-start | bytes 1572872 | tf_op jit(solution)/shard_map/ppermute | solution.py:171
  125.3 27.7 %collective-permute-start.10 = (f32[1024,128]{1,0:T(8,128)S(1)}, f32[1024,128]{1,0:T(8,128)}, u32[]{:S(2)}, u32[]{:S(2)}) collective-permute-start(f32[1024,128]{1,0:T(8,128)S(1)} %broadcast_select_fusion.2.v0), channel_id=1, source_target_pairs={{0,32},{16,48},{32,0},{48,16},{64,96},{80,112},{96,64},{112,80},{1... | collective-permute-start | bytes 1572872 | tf_op jit(solution)/shard_map/ppermute | solution.py:171
  127.8 0.7 copy-start.1
  128.5 24.5 %collective-permute-start.9 = (f32[1024,128]{1,0:T(8,128)S(1)}, f32[1024,128]{1,0:T(8,128)}, u32[]{:S(2)}, u32[]{:S(2)}) collective-permute-start(f32[1024,128]{1,0:T(8,128)S(1)} %broadcast_select_fusion.2.v0), channel_id=1, source_target_pairs={{0,16},{16,0},{32,48},{48,32},{64,80},{80,64},{96,112},{112,96},{1... | collective-permute-start | bytes 1572872 | tf_op jit(solution)/shard_map/ppermute | solution.py:171
  131.3 21.8 %copy-start.2 = (f32[512,128]{1,0:T(8,128)S(1)}, f32[512,128]{1,0:T(8,128)}, u32[]{:S(2)}) copy-start(f32[512,128]{1,0:T(8,128)} %copy-done.1) | copy-start | bytes 786436
  167.5 15.9 %all-to-all-start.3 = ((f32[16,2,8,128]{3,2,1,0:T(8,128)}), f32[16,2,8,128]{3,2,1,0:T(8,128)S(1)}, u32[]{:S(2)}, u32[]{:S(2)}) async-start(f32[16,2,8,128]{3,2,1,0:T(8,128)} %bitcast.48), calls=%async_computation.3 | async-start | bytes 262144 | tf_op jit(solution)/shard_map/all_to_all | solution.py:220

commit v2 on v1

v2 whole, which is shorter than its diff:
```python
import functools

import jax
import jax.numpy as jnp
from jax import lax
from jax.experimental import pallas as pl
from jax.experimental.pallas import tpu as pltpu
from jax.sharding import PartitionSpec as P

highest = lax.Precision.HIGHEST
TB = 128
LEAD = 512
TILES = LEAD // TB
ORDER = (0, 1, 3, 2)
BIG = 56 << 20
VMEM = pl.BlockSpec(memory_space=pltpu.VMEM)
HBM = pl.BlockSpec(memory_space=pltpu.HBM)
SMEM = pl.BlockSpec(memory_space=pltpu.SMEM)


def dot(a, b):
    return jnp.dot(a, b, precision=highest, preferred_element_type=jnp.float32)


def dot_nt(a, b):
    return lax.dot_general(
        a, b, (((1,), (1,)), ((), ())), precision=highest, preferred_element_type=jnp.float32
    )


def recip(p):
    r = pltpu.reciprocal(p, approx=True)
    return r * (2.0 - p * r)


def factor_tile(m_ref):
    n, w = TB, 8
    for g in range(n // w):
        base = w * g
        rows = [jnp.broadcast_to(m_ref[base + k : base + k + 1, 0:n], (8, n)) for k in range(w)]
        erow = [jnp.broadcast_to(m_ref[base + k : base + k + 1, n:], (8, n)) for k in range(w)]
        a, l, r = {}, {}, {}
        for k in range(w):
            for i in range(k + 1):
                a[k, i] = jnp.broadcast_to(rows[k][:, base + i : base + i + 1], (8, n))
        for i in range(w):
            r[i] = recip(a[i, i])
            for k in range(i + 1, w):
                l[k, i] = a[k, i] * r[i]
            for k in range(i + 1, w):
                for j in range(i + 1, k + 1):
                    a[k, j] = a[k, j] - l[k, i] * a[j, i]
                rows[k] = rows[k] - l[k, i] * rows[i]
                erow[k] = erow[k] - l[k, i] * erow[i]
        for k in range(w):
            m_ref[base + k : base + k + 1, n:] = (erow[k] * lax.rsqrt(a[k, k]))[0:1]
        if g == n // w - 1:
            break
        q = [rows[k] * r[k] for k in range(w)]
        qe = [erow[k] * r[k] for k in range(w)]
        for k in range(w - 1, -1, -1):
            for m in range(k + 1, w):
                q[k] = q[k] - l[m, k] * q[m]
                qe[k] = qe[k] - l[m, k] * qe[m]
        for rb in range(g + 1, n // w):
            d = m_ref[8 * rb : 8 * rb + 8, 0:n]
            e = m_ref[8 * rb : 8 * rb + 8, n:]
            cols = [jnp.broadcast_to(d[:, base + k : base + k + 1], (8, n)) for k in range(w)]
            for k in range(w):
                d = d - cols[k] * q[k]
                e = e - cols[k] * qe[k]
            m_ref[8 * rb : 8 * rb + 8, 0:n] = d
            m_ref[8 * rb : 8 * rb + 8, n:] = e


def chol_kernel(ids_ref, t0, t1, t2, t3, x_hbm, x_ref, s_ref, m_ref, sem):
    n = TB
    x, group = lax.rem(ids_ref[0], 4), lax.rem(ids_ref[1], 4)
    for m, src in enumerate((t0, t1, t2, t3)):
        for at, k in enumerate(ORDER):
            rows = pl.ds(pl.multiple_of((x ^ k) * n, n), n)
            cols = pl.ds(pl.multiple_of((group ^ m) * n, n), n)
            s_ref[rows, cols] = src[n * at : n * at + n, :]
    eye = (
        lax.broadcasted_iota(jnp.int32, (n, n), 0) == lax.broadcasted_iota(jnp.int32, (n, n), 1)
    ).astype(jnp.float32)
    for k in range(TILES):
        sl = slice(n * k, n * k + n)
        m_ref[:, 0:n] = s_ref[sl, sl]
        m_ref[:, n:] = eye
        factor_tile(m_ref)
        inv = m_ref[:, n:]
        if k > 0:
            x_ref[sl, 0 : n * k] = -dot(inv, dot(s_ref[sl, 0 : n * k], x_ref[0 : n * k, 0 : n * k]))
        x_ref[sl, sl] = inv
        if k < TILES - 1:
            x_ref[sl, n * (k + 1) :] = jnp.zeros((n, LEAD - n * (k + 1)), jnp.float32)
            low = dot_nt(s_ref[n * (k + 1) :, sl], inv)
            s_ref[n * (k + 1) :, sl] = low
            for j in range(k + 1, TILES):
                o = n * (j - k - 1)
                s_ref[n * j :, n * j : n * j + n] = s_ref[n * j :, n * j : n * j + n] - dot_nt(
                    low[o:], low[o : o + n]
                )
    put_x = pltpu.make_async_copy(x_ref, x_hbm, sem.at[0])
    put_x.start()
    put_x.wait()


def panel_kernel(
    ids_ref, x_hbm, y_hbm, p0, p2, p13, factor_hbm, z_ref, x_ref, raw_ref, factor_ref, p_ref, y_ref, w_ref, sem
):
    n = TB
    my_row, core = ids_ref[0], lax.rem(ids_ref[1], 2)
    x, group = lax.rem(my_row, 4), lax.rem(ids_ref[1], 4)
    gets = [pltpu.make_async_copy(x_hbm, x_ref, sem.at[0]), pltpu.make_async_copy(y_hbm, raw_ref, sem.at[1])]
    for k, src in ((0, p0), (1, p13.at[0:LEAD]), (2, p2), (3, p13.at[LEAD:])):
        cols = pl.ds(pl.multiple_of((group ^ k) * n, n), n)
        gets.append(pltpu.make_async_copy(src, p_ref.at[:, cols], sem.at[2 + k]))
    for get in gets:
        get.start()
    for get in gets:
        get.wait()
    for at, k in enumerate(ORDER):
        for c in range(16):
            y_ref[pl.ds(pl.multiple_of((x ^ k) * n + 8 * c, 8), 8), :] = raw_ref[c, 8 * at : 8 * at + 8, :]
    row = lax.broadcasted_iota(jnp.int32, (LEAD, n), 0)
    col = lax.broadcasted_iota(jnp.int32, (LEAD, n), 1)
    whole_row = (row // n * 32 + my_row) * n + lax.rem(row, n)
    for i in range(TILES):
        upto = n * (i + 1)
        sl = slice(n * i, upto)
        inv = x_ref[sl, 0:upto]
        f = dot_nt(p_ref[:, 0:upto], inv)
        factor_ref[:, sl] = jnp.where(col + n * i <= whole_row, f, 0.0)
        w_ref[sl, :] = dot(inv, y_ref[0:upto, :])
    put = pltpu.make_async_copy(factor_ref, factor_hbm, sem.at[6])
    put.start()
    z = dot(factor_ref[pl.ds(pl.multiple_of(core * 256, 256), 256), :], w_ref[...])
    for a in range(2):
        for c in range(16):
            z_ref[16 * c + 8 * a : 16 * c + 8 * a + 8, :] = z[n * a + 8 * c : n * a + 8 * c + 8]

    @pl.when((my_row < TILES) & (core == 0))
    def _():
        for c in range(16):
            at = pl.multiple_of(my_row * n + 8 * c, 8)
            z_ref[16 * c : 16 * c + 8, :] = w_ref[pl.ds(at, 8), :]
    put.wait()


def trailing_kernel(
    ids_ref, x_hbm, factor_hbm, kernel_hbm, v0_hbm, v1_hbm, v2_hbm, v3_hbm, out_hbm,
    x_ref, factor_ref, kernel_ref, raw_ref, v_ref, f_ref, out_ref, sem,
):
    n = TB
    my_row, my_col = ids_ref[0], ids_ref[1]
    x = lax.rem(my_row, 4)
    gets = [
        pltpu.make_async_copy(src, raw_ref.at[k], sem.at[k])
        for k, src in enumerate((v0_hbm, v1_hbm, v2_hbm, v3_hbm))
    ]
    get_x = pltpu.make_async_copy(x_hbm, x_ref, sem.at[4])
    get_factor = pltpu.make_async_copy(factor_hbm, factor_ref, sem.at[5])
    tiles = [pl.ds(8 * n * a, 8 * n) for a in range(4)]
    get_tiles = [
        pltpu.make_async_copy(kernel_hbm.at[at], kernel_ref.at[at], sem.at[6 + a])
        for a, at in enumerate(tiles)
    ]
    puts = [
        pltpu.make_async_copy(out_ref.at[at], out_hbm.at[at], sem.at[10 + a])
        for a, at in enumerate(tiles)
    ]
    for copy in [*gets, get_x, get_factor, *get_tiles]:
        copy.start()
    for k in range(4):
        gets[k].wait()
        at = pl.ds(pl.multiple_of((x ^ k) * n, n), n)
        for b in range(8):
            v_ref[at, n * b : n * b + n] = raw_ref[k, pl.ds(b, n, stride=8), :]
    get_x.wait()
    for i in range(TILES):
        upto = n * (i + 1)
        f_ref[n * i : upto, :] = dot(x_ref[n * i : upto, 0:upto], v_ref[0:upto, :])
    get_factor.wait()
    for a in range(4):
        get_tiles[a].wait()
        for h in range(4):
            update = dot(factor_ref[n * a : n * a + n, :], f_ref[:, 256 * h : 256 * h + 256])
            for half in range(2):
                b = 2 * h + half
                at = pl.ds(8 * n * a + b, n, stride=8)
                left = kernel_ref[at, :] - update[:, n * half : n * half + n]
                if a == 0:
                    left = jnp.where(my_row < TILES, 0.0, left)
                if b == 0:
                    left = jnp.where(my_col < TILES, 0.0, left)
                out_ref[at, :] = left
        puts[a].start()
    for put in puts:
        put.wait()


def permute_z(block, hops):
    return lax.ppermute(block, "row", [(4 * a + x, 4 * b + x) for a, b in hops for x in range(4)])


def permute_xor(block, axis, k):
    return lax.ppermute(block, axis, [(i, i ^ k) for i in range(lax.axis_size(axis))])


def tree(block, depth, first):
    up, down = ([(0, 3)], [(0, 5)]) if first else ([(0, 1), (3, 4), (5, 6)], [(0, 7), (3, 2)])

    def pick(got):
        picked = block
        for hops, new in zip((up, down), got):
            hit = jnp.any(jnp.stack([depth == b for _, b in hops]))
            picked = jnp.where(hit, new, picked)
        return picked

    return [permute_z(block, up), permute_z(block, down)], pick


def per_device(kernel, targets):
    my_row = lax.axis_index("row")
    my_col = lax.axis_index("col")
    depth = my_row // 4
    f32 = jnp.float32
    ids = jnp.stack([my_row, my_col]).astype(jnp.int32)
    force = lax.optimization_barrier

    tile = kernel[0, :, 0, :]
    got = [lax.ppermute(tile, "col", [(c, c + d) for c in range(4)]) for d in (4, 8, 12)]
    tile = jnp.where(my_col < 4, tile, got[0] + got[1] + got[2])
    block = jnp.concatenate([tile, targets[0, 0].reshape(64, TB)], axis=0)
    got, pick = tree(block, depth, True)
    own = kernel[:, :, 0, :].reshape(LEAD, TB)
    block = pick(got)
    got, pick = tree(block, depth, False)
    own_got = lax.ppermute(own, "col", [(c, c + 8) for c in range(4)])
    got, own_got = force((got, own_got))
    block = pick(got)
    own = jnp.where((my_col >= 8) & (my_col < 12), own_got, own)

    block_1 = permute_xor(block, "row", 1)
    block_32 = permute_xor(jnp.concatenate([block, block_1], axis=0), "row", 3)
    lead = kernel[0].reshape(8 * TB, TB)
    got, pick = tree(lead, depth, True)
    own_got = lax.ppermute(own, "col", [(c, c + 4) for c in (0, 1, 2, 3, 8, 9, 10, 11)])
    block_32, got, own_got = force((block_32, got, own_got))
    lead = pick(got)
    own = jnp.where(my_col % 8 >= 4, own_got, own)
    blocks = [block, block_1, block_32[:192], block_32[192:]]

    t0 = jnp.concatenate([b[:TB] for b in blocks], axis=0)
    t2, t1 = permute_xor(t0, "col", 2), permute_xor(t0, "col", 1)
    got, pick = tree(lead, depth, False)
    own_2 = permute_xor(own, "col", 2)
    wide = jnp.stack([b[TB:].reshape(8, 8, TB) for b in blocks]).transpose(2, 0, 1, 3)
    wide = lax.all_to_all(jnp.repeat(wide.reshape(8, 32, TB), 2, axis=0), "col", 0, 0)
    t3 = permute_xor(t2, "col", 1)
    t1, t3, got, own_2, wide = force((t1, t3, got, own_2, wide))
    lead = pick(got)
    own_13 = permute_xor(jnp.concatenate([own, own_2], axis=0), "col", 1)
    leads = [lead] + [permute_xor(lead, "row", k) for k in (1, 2, 3)]

    inverse = pl.pallas_call(
        chol_kernel,
        out_shape=jax.ShapeDtypeStruct((LEAD, LEAD), f32),
        in_specs=[SMEM] + [VMEM] * 4,
        out_specs=HBM,
        scratch_shapes=[
            pltpu.VMEM((LEAD, LEAD), f32),
            pltpu.VMEM((LEAD, LEAD), f32),
            pltpu.VMEM((TB, 2 * TB), f32),
            pltpu.SemaphoreType.DMA((1,)),
        ],
        compiler_params=pltpu.CompilerParams(vmem_limit_bytes=BIG),
        cost_estimate=pl.CostEstimate(flops=2 * 10**10, bytes_accessed=3 << 20, transcendentals=0),
    )(ids, t0, t1, t2, t3)

    factor, z = pl.pallas_call(
        panel_kernel,
        out_shape=[
            jax.ShapeDtypeStruct((LEAD, LEAD), f32),
            jax.ShapeDtypeStruct((2 * TB, TB), f32),
        ],
        in_specs=[SMEM] + [HBM] * 5,
        out_specs=[HBM, VMEM],
        scratch_shapes=[
            pltpu.VMEM((LEAD, LEAD), f32),
            pltpu.VMEM((16, 32, TB), f32),
            pltpu.VMEM((LEAD, LEAD), f32),
            pltpu.VMEM((LEAD, LEAD), f32),
            pltpu.VMEM((LEAD, TB), f32),
            pltpu.VMEM((LEAD, TB), f32),
            pltpu.SemaphoreType.DMA((7,)),
        ],
        compiler_params=pltpu.CompilerParams(vmem_limit_bytes=BIG),
        cost_estimate=pl.CostEstimate(flops=2 * 10**9, bytes_accessed=4 << 20, transcendentals=0),
    )(ids, inverse, wide, own, own_2, own_13)

    trailing = pl.pallas_call(
        trailing_kernel,
        out_shape=jax.ShapeDtypeStruct((8 * LEAD, TB), f32),
        in_specs=[SMEM] + [HBM] * 7,
        out_specs=HBM,
        scratch_shapes=[
            pltpu.VMEM((LEAD, LEAD), f32),
            pltpu.VMEM((LEAD, LEAD), f32),
            pltpu.VMEM((8 * LEAD, TB), f32),
            pltpu.VMEM((4, 8 * TB, TB), f32),
            pltpu.VMEM((LEAD, 8 * TB), f32),
            pltpu.VMEM((LEAD, 8 * TB), f32),
            pltpu.VMEM((8 * LEAD, TB), f32),
            pltpu.SemaphoreType.DMA((14,)),
        ],
        compiler_params=pltpu.CompilerParams(vmem_limit_bytes=BIG),
        cost_estimate=pl.CostEstimate(flops=10**10, bytes_accessed=10 << 20, transcendentals=0),
    )(ids, inverse, factor, kernel.reshape(8 * LEAD, TB), *leads)

    got = lax.all_to_all(z.reshape(16, 2, 8, TB), "col", 0, 0).reshape(8, 2, 2, 8, TB)
    got = got.transpose(1, 2, 3, 0, 4).reshape(4, 8, 8 * TB)
    top = (jnp.arange(4, dtype=jnp.int32) == 0)[:, None, None] & (my_row < TILES)
    targets_out = jnp.where(top, got, targets[:, 0] - got)[:, None]
    return (
        factor.reshape(4, TB, LEAD),
        trailing.reshape(kernel.shape),
        targets_out,
    )


def solution(mesh):
    return jax.shard_map(
        per_device,
        mesh=mesh,
        in_specs=(P(None, "row", None, "col"), P(None, "row", "col", None)),
        out_specs=(P(None, "row", None), P(None, "row", None, "col"), P(None, "row", "col", None)),
        check_vma=False,
    )
```

time: 186 us -> 152 us (0.82)
  waiting for transfers between devices: 60.4 us -> 11.9 us
  starting transfers between devices: 74.6 us -> 85.1 us
  Pallas kernels: 35.5 us -> 42.1 us
  other arithmetic: 7.4 us -> 2.73 us
    ppermute x12 -> x23, starting transfers between devices: 40.7 us -> 75.1 us  [the longest x10 35.9 us: permute_xor(): lax.ppermute(block, axis, [(i, i ^ k) for i in range(lax.axis_size(axis))])]
    ppermute x12 -> x23, waiting for transfers between devices: 38.8 us -> 11.8 us  [the longest x10 10.9 us: permute_xor(): lax.ppermute(block, axis, [(i, i ^ k) for i in range(lax.axis_size(axis))])]
    all_to_all x4 -> x2, starting transfers between devices: 33.9 us -> 10 us  [the longest x1 5.89 us: per_device(): lax.all_to_all(z.reshape(16, 2, 8, TB), 'col', 0, 0).reshape(8, 2, 2, 8, TB)]
    all_to_all x4 -> x2, waiting for transfers between devices: 21.6 us -> 0.01 us  [the longest x1 0.01 us: per_device(): lax.all_to_all(jnp.repeat(wide.reshape(8, 32, TB), 2, axis=0), 'col', 0, 0)]
    pallas_call x1 -> x2, Pallas kernels: 13.8 us -> 18 us  [the longest x1 10.8 us: per_device(): pl.pallas_call(trailing_kernel, out_shape=jax.ShapeDtypeStruct((8 * LEAD,...]
    select_n x4 -> x7, other arithmetic: 4.24 us -> 1.3 us  [the longest x4 1.22 us: pick(): picked = jnp.where(hit, new, picked)]
    pallas_call x1, Pallas kernels: 21.7 us -> 24.1 us  [per_device(): pl.pallas_call(chol_kernel, out_shape=jax.ShapeDtypeStruct((LEAD, LEAD),...]
    unnamed x10 -> x26, local copies, waits for them, and re-layouts: 0.72 us -> 2.66 us
  transfers between devices with their start and end apart: 16 -> 25, of which waited for: 5 -> 3; matrix products, arithmetic and copies ran while one was open for 4% -> 4% of each run, Pallas kernels for 12% -> 28%
where the time goes in v2:
time: 152 us; the launch traced here: 151 us
  starting transfers between devices  85.1 us (56%)
  Pallas kernels  42.1 us (28%)
  waiting for transfers between devices  11.9 us (8%)
  local copies, waits for them, and re-layouts  8.12 us (5%)
  other arithmetic  2.73 us (2%)
    ppermute x10, starting transfers between devices, permute_xor(): lax.ppermute(block, axis, [(i, i ^ k) for i in range(lax.axis_size(axis))])  35.9 us
    pallas_call x1, Pallas kernels, per_device(): pl.pallas_call(chol_kernel, out_shape=jax.ShapeDtypeStruct((LEAD, LEAD),...  24.1 us
    ppermute x8, starting transfers between devices, permute_z(): lax.ppermute(block, 'row', [(4 * a + x, 4 * b + x) for a, b in hops for x...  19.7 us
    ppermute x10, waiting for transfers between devices, permute_xor(): lax.ppermute(block, axis, [(i, i ^ k) for i in range(lax.axis_size(axis))])  10.9 us
    pallas_call x1, Pallas kernels, per_device(): pl.pallas_call(trailing_kernel, out_shape=jax.ShapeDtypeStruct((8 * LEAD,...  10.8 us
    ppermute x3, starting transfers between devices, per_device(): lax.ppermute(tile, 'col', [(c, c + d) for c in range(4)])  10.2 us
    pallas_call x1, Pallas kernels, per_device(): pl.pallas_call(panel_kernel, out_shape=[jax.ShapeDtypeStruct((LEAD, LEAD)...  7.22 us
    ppermute x1, starting transfers between devices, per_device(): own_got = lax.ppermute(own, 'col', [(c, c + 8) for c in range(4)])  5.92 us
  transfers between devices with their start and end apart: 25, of which 3 were waited for; matrix products, arithmetic and copies ran while one was open for 4% of the time, Pallas kernels for 28%

profile of v2, /device:TPU:1, one launch (start us, length us, event | category | flops | bytes accessed | tf_op | source)
XLA Modules:
  0.0 151.2 jit_solution(8035926621803591384)
XLA Ops:
  1.7 6.7 %collective-permute-start.2 = (f32[128,128]{1,0:T(8,128)S(1)}, f32[128,128]{1,0:T(8,128)S(1)}, u32[]{:S(2)}, u32[]{:S(2)}) collective-permute-start(f32[128,128]{1,0:T(8,128)S(1)} %bitcast.38), channel_id=1, source_target_pairs={{0,12},{1,13},{2,14},{3,15},{16,28},{17,29},{18,30},{19,31},{32,44... | collective-permute-start | bytes 196616 | tf_op jit(solution)/shard_map/ppermute | solution.py:234
  8.4 2.2 %collective-permute-start.1 = (f32[128,128]{1,0:T(8,128)S(1)}, f32[128,128]{1,0:T(8,128)S(1)}, u32[]{:S(2)}, u32[]{:S(2)}) collective-permute-start(f32[128,128]{1,0:T(8,128)S(1)} %bitcast.39), channel_id=1, source_target_pairs={{0,8},{1,9},{2,10},{3,11},{16,24},{17,25},{18,26},{19,27},{32,40},... | collective-permute-start | bytes 196616 | tf_op jit(solution)/shard_map/ppermute | solution.py:234
  13.7 7.6 %collective-permute-start.4 = (f32[192,128]{1,0:T(8,128)S(1)}, f32[192,128]{1,0:T(8,128)S(1)}, u32[]{:S(2)}, u32[]{:S(2)}) collective-permute-start(f32[192,128]{1,0:T(8,128)S(1)} %pad_maximum_fusion.4), channel_id=1, source_target_pairs={{0,192},{16,208},{32,224},{48,240},{1,193},{17,209},{33,225},{49,2... | collective-permute-start | bytes 294920 | tf_op jit(solution)/shard_map/ppermute | solution.py:205
  21.4 3.7 %collective-permute-start.3 = (f32[192,128]{1,0:T(8,128)S(1)}, f32[192,128]{1,0:T(8,128)S(1)}, u32[]{:S(2)}, u32[]{:S(2)}) collective-permute-start(f32[192,128]{1,0:T(8,128)S(1)} %pad_maximum_fusion.4), channel_id=1, source_target_pairs={{0,320},{16,336},{32,352},{48,368},{1,321},{17,337},{33,353},{49,3... | collective-permute-start | bytes 294920 | tf_op jit(solution)/shard_map/ppermute | solution.py:205
  26.8 5.9 %collective-permute-start.7 = (f32[512,128]{1,0:T(8,128)S(1)}, f32[512,128]{1,0:T(8,128)S(1)}, u32[]{:S(2)}, u32[]{:S(2)}) collective-permute-start(f32[512,128]{1,0:T(8,128)S(1)} %bitcast.32), channel_id=1, source_target_pairs={{0,8},{1,9},{2,10},{3,11},{16,24},{17,25},{18,26},{19,27},{32,40},... | collective-permute-start | bytes 786440 | tf_op jit(solution)/shard_map/ppermute | solution.py:241
  36.5 1.9 %collective-permute-start.11 = (f32[1024,128]{1,0:T(8,128)S(1)}, f32[1024,128]{1,0:T(8,128)S(1)}, u32[]{:S(2)}, u32[]{:S(2)}) collective-permute-start(f32[1024,128]{1,0:T(8,128)S(1)} %slice_bitcast_fusion), channel_id=1, source_target_pairs={{0,320},{16,336},{32,352},{48,368},{1,321},{17,337},{33,353},{49,3... | collective-permute-start | bytes 1572872 | tf_op jit(solution)/shard_map/ppermute | solution.py:205
  39.8 3.1 %collective-permute-start.8 = (f32[192,128]{1,0:T(8,128)S(1)}, f32[192,128]{1,0:T(8,128)S(1)}, u32[]{:S(2)}, u32[]{:S(2)}) collective-permute-start(f32[192,128]{1,0:T(8,128)S(1)} %select_select_fusion.2), channel_id=1, source_target_pairs={{0,16},{16,0},{32,48},{48,32},{64,80},{80,64},{96,112},{112,96},{1... | collective-permute-start | bytes 294920 | tf_op jit(solution)/shard_map/ppermute | solution.py:209
  43.0 3.3 %collective-permute-start.12 = (f32[512,128]{1,0:T(8,128)S(1)}, f32[512,128]{1,0:T(8,128)S(1)}, u32[]{:S(2)}, u32[]{:S(2)}) collective-permute-start(f32[512,128]{1,0:T(8,128)S(1)} %broadcast_select_fusion.1), channel_id=1, source_target_pairs={{0,4},{1,5},{2,6},{3,7},{8,12},{9,13},{10,14},{11,15},{16,20},{17,... | collective-permute-start | bytes 786440 | tf_op jit(solution)/shard_map/ppermute | solution.py:250
  46.3 3.7 %collective-permute-start.9 = (f32[384,128]{1,0:T(8,128)S(1)}, f32[384,128]{1,0:T(8,128)S(1)}, u32[]{:S(2)}, u32[]{:S(2)}) collective-permute-start(f32[384,128]{1,0:T(8,128)S(1)} %pad_maximum_fusion.2), channel_id=1, source_target_pairs={{0,48},{16,32},{32,16},{48,0},{64,112},{80,96},{96,80},{112,64},{1... | collective-permute-start | bytes 589832 | tf_op jit(solution)/shard_map/ppermute | solution.py:209
  50.1 3.8 %collective-permute-done.9 = f32[384,128]{1,0:T(8,128)S(1)} collective-permute-done((f32[384,128]{1,0:T(8,128)S(1)}, f32[384,128]{1,0:T(8,128)S(1)}, u32[]{:S(2)}, u32[]{:S(2)}) %collective-permute-start.9) | collective-permute-done | bytes 196640 | tf_op jit(solution)/shard_map/ppermute | solution.py:209
  54.0 6.7 %collective-permute-start.14 = (f32[512,128]{1,0:T(8,128)S(1)}, f32[512,128]{1,0:T(8,128)S(1)}, u32[]{:S(2)}, u32[]{:S(2)}) collective-permute-start(f32[512,128]{1,0:T(8,128)S(1)} %pad_maximum_fusion.1.t0), channel_id=1, source_target_pairs={{0,2},{1,3},{2,0},{3,1},{4,6},{5,7},{6,4},{7,5},{8,10},{9,11},{10,... | collective-permute-start | bytes 786440 | tf_op jit(solution)/shard_map/ppermute | solution.py:209
  60.7 3.7 %collective-permute-start.13 = (f32[512,128]{1,0:T(8,128)S(1)}, f32[512,128]{1,0:T(8,128)S(1)}, u32[]{:S(2)}, u32[]{:S(2)}) collective-permute-start(f32[512,128]{1,0:T(8,128)S(1)} %pad_maximum_fusion.1.t0), channel_id=1, source_target_pairs={{0,1},{1,0},{2,3},{3,2},{4,5},{5,4},{6,7},{7,6},{8,9},{9,8},{10,11... | collective-permute-start | bytes 786440 | tf_op jit(solution)/shard_map/ppermute | solution.py:209
  69.0 4.1 %all-to-all-start = ((f32[16,32,128]{2,1,0:T(8,128)}), f32[16,32,128]{2,1,0:T(8,128)S(1)}, u32[]{:S(2)}, u32[]{:S(2)}) async-start(f32[16,32,128]{2,1,0:T(8,128)} %bitcast.11), calls=%async_computation | async-start | bytes 524288 | tf_op jit(solution)/shard_map/all_to_all | solution.py:261
  73.1 3.3 %collective-permute-start.18 = (f32[512,128]{1,0:T(8,128)S(1)}, f32[512,128]{1,0:T(8,128)S(1)}, u32[]{:S(2)}, u32[]{:S(2)}) collective-permute-start(f32[512,128]{1,0:T(8,128)S(1)} %broadcast_select_fusion.p0), channel_id=1, source_target_pairs={{0,2},{1,3},{2,0},{3,1},{4,6},{5,7},{6,4},{7,5},{8,10},{9,11},{10,... | collective-permute-start | bytes 786440 | tf_op jit(solution)/shard_map/ppermute | solution.py:209
  76.5 2.5 %collective-permute-start.15 = (f32[512,128]{1,0:T(8,128)S(1)}, f32[512,128]{1,0:T(8,128)S(1)}, u32[]{:S(2)}, u32[]{:S(2)}) collective-permute-start(f32[512,128]{1,0:T(8,128)S(1)} %collective-permute-done.14.t2), channel_id=1, source_target_pairs={{0,1},{1,0},{2,3},{3,2},{4,5},{5,4},{6,7},{7,6},{8,9},{9,8},{10,11... | collective-permute-start | bytes 786440 | tf_op jit(solution)/shard_map/ppermute | solution.py:209
  79.6 7.0 %collective-permute-done.18.p2 = f32[512,128]{1,0:T(8,128)S(1)} collective-permute-done((f32[512,128]{1,0:T(8,128)S(1)}, f32[512,128]{1,0:T(8,128)S(1)}, u32[]{:S(2)}, u32[]{:S(2)}) %collective-permute-start.18) | collective-permute-done | bytes 262176 | tf_op jit(solution)/shard_map/ppermute | solution.py:209
  87.5 3.7 %collective-permute-start.22 = (f32[1024,128]{1,0:T(8,128)S(1)}, f32[1024,128]{1,0:T(8,128)S(1)}, u32[]{:S(2)}, u32[]{:S(2)}) collective-permute-start(f32[1024,128]{1,0:T(8,128)S(1)} %select_select_fusion.v0_hbm), channel_id=1, source_target_pairs={{0,48},{16,32},{32,16},{48,0},{64,112},{80,96},{96,80},{112,64},{1... | collective-permute-start | bytes 1572872 | tf_op jit(solution)/shard_map/ppermute | solution.py:209
  91.3 2.6 %collective-permute-start.21 = (f32[1024,128]{1,0:T(8,128)S(1)}, f32[1024,128]{1,0:T(8,128)S(1)}, u32[]{:S(2)}, u32[]{:S(2)}) collective-permute-start(f32[1024,128]{1,0:T(8,128)S(1)} %select_select_fusion.v0_hbm), channel_id=1, source_target_pairs={{0,32},{16,48},{32,0},{48,16},{64,96},{80,112},{96,64},{112,80},{1... | collective-permute-start | bytes 1572872 | tf_op jit(solution)/shard_map/ppermute | solution.py:209
  93.8 2.7 %collective-permute-start.20 = (f32[1024,128]{1,0:T(8,128)S(1)}, f32[1024,128]{1,0:T(8,128)S(1)}, u32[]{:S(2)}, u32[]{:S(2)}) collective-permute-start(f32[1024,128]{1,0:T(8,128)S(1)} %select_select_fusion.v0_hbm), channel_id=1, source_target_pairs={{0,16},{16,0},{32,48},{48,32},{64,80},{80,64},{96,112},{112,96},{1... | collective-permute-start | bytes 1572872 | tf_op jit(solution)/shard_map/ppermute | solution.py:209
  96.6 3.8 %collective-permute-start.19 = (f32[1024,128]{1,0:T(8,128)S(1)}, f32[1024,128]{1,0:T(8,128)S(1)}, u32[]{:S(2)}, u32[]{:S(2)}) collective-permute-start(f32[1024,128]{1,0:T(8,128)S(1)} %pad_maximum_fusion), channel_id=1, source_target_pairs={{0,1},{1,0},{2,3},{3,2},{4,5},{5,4},{6,7},{7,6},{8,9},{9,8},{10,11... | collective-permute-start | bytes 1572872 | tf_op jit(solution)/shard_map/ppermute | solution.py:209
  100.4 24.1 %shard_map.49.x_hbm = f32[512,512]{1,0:T(8,128)} custom-call(s32[2]{0:T(128)} %pad_add_fusion.ids_ref, f32[512,128]{1,0:T(8,128)} %copy-done.2, f32[512,128]{1,0:T(8,128)} %copy-done.11, f32[512,128]{1,0:T(8,128)} %copy-done.10, f32[512,128]{1,0:T(8,128)} %copy-done.12), custom_call_target="tpu_custom_call" | custom-call | flops 20000000000 | bytes 3145728 | tf_op jit(solution)/shard_map/pallas_call | solution.py:268
  125.3 7.2 %shard_map.50 = (f32[512,512]{1,0:T(8,128)}, f32[256,128]{1,0:T(8,128)}) custom-call(s32[2]{0:T(128)} %pad_add_fusion.ids_ref, f32[512,512]{1,0:T(8,128)} %shard_map.49.x_hbm, f32[16,32,128]{2,1,0:T(8,128)} %copy-done.3, f32[512,128]{1,0:T(8,128)} %copy-done, f32[512,128]{1,0:T(8,128)} %copy-done.4, f32[1024,128]{1,0:T(8,128)} %copy-done.9), custom_call_target="tpu_custom_call" | custom-call | flops 2000000000 | bytes 4194304 | tf_op jit(solution)/shard_map/pallas_call | solution.py:283
  132.5 5.9 %all-to-all-start.1 = ((f32[16,2,8,128]{3,2,1,0:T(8,128)}), f32[16,2,8,128]{3,2,1,0:T(8,128)S(1)}, u32[]{:S(2)}, u32[]{:S(2)}) async-start(f32[16,2,8,128]{3,2,1,0:T(8,128)} %bitcast.42), calls=%async_computation.1 | async-start | bytes 262144 | tf_op jit(solution)/shard_map/all_to_all | solution.py:323
  139.6 10.8 %shard_map.51 = f32[4096,128]{1,0:T(8,128)} custom-call(s32[2]{0:T(128)} %pad_add_fusion.ids_ref, f32[512,512]{1,0:T(8,128)} %shard_map.49.x_hbm, f32[512,512]{1,0:T(8,128)} %get-tuple-element.29.factor_hbm, f32[4096,128]{1,0:T(8,128)} %bitcast.34, f32[1024,128]{1,0:T(8,128)} %copy-done.1, f32[1024,128]{1,0:T(8,128)} %copy-done.8, f32[1024,128]{1,0:T(8,128)} %copy-done.7, ...), custom_call_target="tpu_custom_call" | custom-call | flops 10000000000 | bytes 10485760 | tf_op jit(solution)/shard_map/pallas_call | solution.py:304
  (84 shorter events, 19.7 us)
Async XLA Ops:
  1.7 11.1 %collective-permute-start.2 = (f32[128,128]{1,0:T(8,128)S(1)}, f32[128,128]{1,0:T(8,128)S(1)}, u32[]{:S(2)}, u32[]{:S(2)}) collective-permute-start(f32[128,128]{1,0:T(8,128)S(1)} %bitcast.38), channel_id=1, source_target_pairs={{0,12},{1,13},{2,14},{3,15},{16,28},{17,29},{18,30},{19,31},{32,44... | collective-permute-start | bytes 196616 | tf_op jit(solution)/shard_map/ppermute | solution.py:234
  8.4 4.3 %collective-permute-start.1 = (f32[128,128]{1,0:T(8,128)S(1)}, f32[128,128]{1,0:T(8,128)S(1)}, u32[]{:S(2)}, u32[]{:S(2)}) collective-permute-start(f32[128,128]{1,0:T(8,128)S(1)} %bitcast.39), channel_id=1, source_target_pairs={{0,8},{1,9},{2,10},{3,11},{16,24},{17,25},{18,26},{19,27},{32,40},... | collective-permute-start | bytes 196616 | tf_op jit(solution)/shard_map/ppermute | solution.py:234
  13.7 19.0 %collective-permute-start.4 = (f32[192,128]{1,0:T(8,128)S(1)}, f32[192,128]{1,0:T(8,128)S(1)}, u32[]{:S(2)}, u32[]{:S(2)}) collective-permute-start(f32[192,128]{1,0:T(8,128)S(1)} %pad_maximum_fusion.4), channel_id=1, source_target_pairs={{0,192},{16,208},{32,224},{48,240},{1,193},{17,209},{33,225},{49,2... | collective-permute-start | bytes 294920 | tf_op jit(solution)/shard_map/ppermute | solution.py:205
  21.4 11.4 %collective-permute-start.3 = (f32[192,128]{1,0:T(8,128)S(1)}, f32[192,128]{1,0:T(8,128)S(1)}, u32[]{:S(2)}, u32[]{:S(2)}) collective-permute-start(f32[192,128]{1,0:T(8,128)S(1)} %pad_maximum_fusion.4), channel_id=1, source_target_pairs={{0,320},{16,336},{32,352},{48,368},{1,321},{17,337},{33,353},{49,3... | collective-permute-start | bytes 294920 | tf_op jit(solution)/shard_map/ppermute | solution.py:205
  26.8 12.9 %collective-permute-start.7 = (f32[512,128]{1,0:T(8,128)S(1)}, f32[512,128]{1,0:T(8,128)S(1)}, u32[]{:S(2)}, u32[]{:S(2)}) collective-permute-start(f32[512,128]{1,0:T(8,128)S(1)} %bitcast.32), channel_id=1, source_target_pairs={{0,8},{1,9},{2,10},{3,11},{16,24},{17,25},{18,26},{19,27},{32,40},... | collective-permute-start | bytes 786440 | tf_op jit(solution)/shard_map/ppermute | solution.py:241
  32.8 6.9 %collective-permute-start.6 = (f32[192,128]{1,0:T(8,128)S(1)}, f32[192,128]{1,0:T(8,128)S(1)}, u32[]{:S(2)}, u32[]{:S(2)}) collective-permute-start(f32[192,128]{1,0:T(8,128)S(1)} %select_select_fusion.3), channel_id=1, source_target_pairs={{0,448},{16,464},{32,480},{48,496},{192,128},{208,144},{224,160},{... | collective-permute-start | bytes 294920 | tf_op jit(solution)/shard_map/ppermute | solution.py:205
  34.1 5.6 %collective-permute-start.5 = (f32[192,128]{1,0:T(8,128)S(1)}, f32[192,128]{1,0:T(8,128)S(1)}, u32[]{:S(2)}, u32[]{:S(2)}) collective-permute-start(f32[192,128]{1,0:T(8,128)S(1)} %select_select_fusion.3), channel_id=1, source_target_pairs={{0,64},{16,80},{32,96},{48,112},{192,256},{208,272},{224,288},{240... | collective-permute-start | bytes 294920 | tf_op jit(solution)/shard_map/ppermute | solution.py:205
  36.5 13.6 %collective-permute-start.11 = (f32[1024,128]{1,0:T(8,128)S(1)}, f32[1024,128]{1,0:T(8,128)S(1)}, u32[]{:S(2)}, u32[]{:S(2)}) collective-permute-start(f32[1024,128]{1,0:T(8,128)S(1)} %slice_bitcast_fusion), channel_id=1, source_target_pairs={{0,320},{16,336},{32,352},{48,368},{1,321},{17,337},{33,353},{49,3... | collective-permute-start | bytes 1572872 | tf_op jit(solution)/shard_map/ppermute | solution.py:205
  38.4 11.7 %collective-permute-start.10 = (f32[1024,128]{1,0:T(8,128)S(1)}, f32[1024,128]{1,0:T(8,128)S(1)}, u32[]{:S(2)}, u32[]{:S(2)}) collective-permute-start(f32[1024,128]{1,0:T(8,128)S(1)} %slice_bitcast_fusion), channel_id=1, source_target_pairs={{0,192},{16,208},{32,224},{48,240},{1,193},{17,209},{33,225},{49,2... | collective-permute-start | bytes 1572872 | tf_op jit(solution)/shard_map/ppermute | solution.py:205
  39.8 6.5 %collective-permute-start.8 = (f32[192,128]{1,0:T(8,128)S(1)}, f32[192,128]{1,0:T(8,128)S(1)}, u32[]{:S(2)}, u32[]{:S(2)}) collective-permute-start(f32[192,128]{1,0:T(8,128)S(1)} %select_select_fusion.2), channel_id=1, source_target_pairs={{0,16},{16,0},{32,48},{48,32},{64,80},{80,64},{96,112},{112,96},{1... | collective-permute-start | bytes 294920 | tf_op jit(solution)/shard_map/ppermute | solution.py:209
  43.0 7.1 %collective-permute-start.12 = (f32[512,128]{1,0:T(8,128)S(1)}, f32[512,128]{1,0:T(8,128)S(1)}, u32[]{:S(2)}, u32[]{:S(2)}) collective-permute-start(f32[512,128]{1,0:T(8,128)S(1)} %broadcast_select_fusion.1), channel_id=1, source_target_pairs={{0,4},{1,5},{2,6},{3,7},{8,12},{9,13},{10,14},{11,15},{16,20},{17,... | collective-permute-start | bytes 786440 | tf_op jit(solution)/shard_map/ppermute | solution.py:250
  46.3 7.6 %collective-permute-start.9 = (f32[384,128]{1,0:T(8,128)S(1)}, f32[384,128]{1,0:T(8,128)S(1)}, u32[]{:S(2)}, u32[]{:S(2)}) collective-permute-start(f32[384,128]{1,0:T(8,128)S(1)} %pad_maximum_fusion.2), channel_id=1, source_target_pairs={{0,48},{16,32},{32,16},{48,0},{64,112},{80,96},{96,80},{112,64},{1... | collective-permute-start | bytes 589832 | tf_op jit(solution)/shard_map/ppermute | solution.py:209
  54.0 22.5 %collective-permute-start.14 = (f32[512,128]{1,0:T(8,128)S(1)}, f32[512,128]{1,0:T(8,128)S(1)}, u32[]{:S(2)}, u32[]{:S(2)}) collective-permute-start(f32[512,128]{1,0:T(8,128)S(1)} %pad_maximum_fusion.1.t0), channel_id=1, source_target_pairs={{0,2},{1,3},{2,0},{3,1},{4,6},{5,7},{6,4},{7,5},{8,10},{9,11},{10,... | collective-permute-start | bytes 786440 | tf_op jit(solution)/shard_map/ppermute | solution.py:209
  60.7 18.9 %collective-permute-start.13 = (f32[512,128]{1,0:T(8,128)S(1)}, f32[512,128]{1,0:T(8,128)S(1)}, u32[]{:S(2)}, u32[]{:S(2)}) collective-permute-start(f32[512,128]{1,0:T(8,128)S(1)} %pad_maximum_fusion.1.t0), channel_id=1, source_target_pairs={{0,1},{1,0},{2,3},{3,2},{4,5},{5,4},{6,7},{7,6},{8,9},{9,8},{10,11... | collective-permute-start | bytes 786440 | tf_op jit(solution)/shard_map/ppermute | solution.py:209
  65.5 21.2 %collective-permute-start.17 = (f32[1024,128]{1,0:T(8,128)S(1)}, f32[1024,128]{1,0:T(8,128)S(1)}, u32[]{:S(2)}, u32[]{:S(2)}) collective-permute-start(f32[1024,128]{1,0:T(8,128)S(1)} %select_select_fusion.1), channel_id=1, source_target_pairs={{0,448},{16,464},{32,480},{48,496},{192,128},{208,144},{224,160},{... | collective-permute-start | bytes 1572872 | tf_op jit(solution)/shard_map/ppermute | solution.py:205
  66.9 20.6 %collective-permute-start.16 = (f32[1024,128]{1,0:T(8,128)S(1)}, f32[1024,128]{1,0:T(8,128)S(1)}, u32[]{:S(2)}, u32[]{:S(2)}) collective-permute-start(f32[1024,128]{1,0:T(8,128)S(1)} %select_select_fusion.1), channel_id=1, source_target_pairs={{0,64},{16,80},{32,96},{48,112},{192,256},{208,272},{224,288},{240... | collective-permute-start | bytes 1572872 | tf_op jit(solution)/shard_map/ppermute | solution.py:205
  69.0 17.7 %all-to-all-start = ((f32[16,32,128]{2,1,0:T(8,128)}), f32[16,32,128]{2,1,0:T(8,128)S(1)}, u32[]{:S(2)}, u32[]{:S(2)}) async-start(f32[16,32,128]{2,1,0:T(8,128)} %bitcast.11), calls=%async_computation | async-start | bytes 524288 | tf_op jit(solution)/shard_map/all_to_all | solution.py:261
  73.1 13.5 %collective-permute-start.18 = (f32[512,128]{1,0:T(8,128)S(1)}, f32[512,128]{1,0:T(8,128)S(1)}, u32[]{:S(2)}, u32[]{:S(2)}) collective-permute-start(f32[512,128]{1,0:T(8,128)S(1)} %broadcast_select_fusion.p0), channel_id=1, source_target_pairs={{0,2},{1,3},{2,0},{3,1},{4,6},{5,7},{6,4},{7,5},{8,10},{9,11},{10,... | collective-permute-start | bytes 786440 | tf_op jit(solution)/shard_map/ppermute | solution.py:209
  76.5 10.2 %collective-permute-start.15 = (f32[512,128]{1,0:T(8,128)S(1)}, f32[512,128]{1,0:T(8,128)S(1)}, u32[]{:S(2)}, u32[]{:S(2)}) collective-permute-start(f32[512,128]{1,0:T(8,128)S(1)} %collective-permute-done.14.t2), channel_id=1, source_target_pairs={{0,1},{1,0},{2,3},{3,2},{4,5},{5,4},{6,7},{7,6},{8,9},{9,8},{10,11... | collective-permute-start | bytes 786440 | tf_op jit(solution)/shard_map/ppermute | solution.py:209
  87.5 50.9 %collective-permute-start.22 = (f32[1024,128]{1,0:T(8,128)S(1)}, f32[1024,128]{1,0:T(8,128)S(1)}, u32[]{:S(2)}, u32[]{:S(2)}) collective-permute-start(f32[1024,128]{1,0:T(8,128)S(1)} %select_select_fusion.v0_hbm), channel_id=1, source_target_pairs={{0,48},{16,32},{32,16},{48,0},{64,112},{80,96},{96,80},{112,64},{1... | collective-permute-start | bytes 1572872 | tf_op jit(solution)/shard_map/ppermute | solution.py:209
  91.3 47.2 %collective-permute-start.21 = (f32[1024,128]{1,0:T(8,128)S(1)}, f32[1024,128]{1,0:T(8,128)S(1)}, u32[]{:S(2)}, u32[]{:S(2)}) collective-permute-start(f32[1024,128]{1,0:T(8,128)S(1)} %select_select_fusion.v0_hbm), channel_id=1, source_target_pairs={{0,32},{16,48},{32,0},{48,16},{64,96},{80,112},{96,64},{112,80},{1... | collective-permute-start | bytes 1572872 | tf_op jit(solution)/shard_map/ppermute | solution.py:209
  93.8 44.6 %collective-permute-start.20 = (f32[1024,128]{1,0:T(8,128)S(1)}, f32[1024,128]{1,0:T(8,128)S(1)}, u32[]{:S(2)}, u32[]{:S(2)}) collective-permute-start(f32[1024,128]{1,0:T(8,128)S(1)} %select_select_fusion.v0_hbm), channel_id=1, source_target_pairs={{0,16},{16,0},{32,48},{48,32},{64,80},{80,64},{96,112},{112,96},{1... | collective-permute-start | bytes 1572872 | tf_op jit(solution)/shard_map/ppermute | solution.py:209
  96.6 27.9 %collective-permute-start.19 = (f32[1024,128]{1,0:T(8,128)S(1)}, f32[1024,128]{1,0:T(8,128)S(1)}, u32[]{:S(2)}, u32[]{:S(2)}) collective-permute-start(f32[1024,128]{1,0:T(8,128)S(1)} %pad_maximum_fusion), channel_id=1, source_target_pairs={{0,1},{1,0},{2,3},{3,2},{4,5},{5,4},{6,7},{7,6},{8,9},{9,8},{10,11... | collective-permute-start | bytes 1572872 | tf_op jit(solution)/shard_map/ppermute | solution.py:209
  132.5 17.9 %all-to-all-start.1 = ((f32[16,2,8,128]{3,2,1,0:T(8,128)}), f32[16,2,8,128]{3,2,1,0:T(8,128)S(1)}, u32[]{:S(2)}, u32[]{:S(2)}) async-start(f32[16,2,8,128]{3,2,1,0:T(8,128)} %bitcast.42), calls=%async_computation.1 | async-start | bytes 262144 | tf_op jit(solution)/shard_map/all_to_all | solution.py:323
  (14 other events, 227.8 us)

commit v3 on v2

--- a/solution.py
+++ b/solution.py
@@ -108,13 +108,13 @@
 
 
 def panel_kernel(
-    ids_ref, x_hbm, y_hbm, p0, p2, p13, factor_hbm, z_ref, x_ref, raw_ref, factor_ref, p_ref, y_ref, w_ref, sem
+    ids_ref, x_hbm, y_hbm, p0, p1, p2, p3, factor_hbm, z_ref, x_ref, raw_ref, factor_ref, p_ref, y_ref, w_ref, sem
 ):
     n = TB
     my_row, core = ids_ref[0], lax.rem(ids_ref[1], 2)
     x, group = lax.rem(my_row, 4), lax.rem(ids_ref[1], 4)
     gets = [pltpu.make_async_copy(x_hbm, x_ref, sem.at[0]), pltpu.make_async_copy(y_hbm, raw_ref, sem.at[1])]
-    for k, src in ((0, p0), (1, p13.at[0:LEAD]), (2, p2), (3, p13.at[LEAD:])):
+    for k, src in enumerate((p0, p1, p2, p3)):
         cols = pl.ds(pl.multiple_of((group ^ k) * n, n), n)
         gets.append(pltpu.make_async_copy(src, p_ref.at[:, cols], sem.at[2 + k]))
     for get in gets:
@@ -124,16 +124,18 @@
     for at, k in enumerate(ORDER):
         for c in range(16):
             y_ref[pl.ds(pl.multiple_of((x ^ k) * n + 8 * c, 8), 8), :] = raw_ref[c, 8 * at : 8 * at + 8, :]
-    row = lax.broadcasted_iota(jnp.int32, (LEAD, n), 0)
-    col = lax.broadcasted_iota(jnp.int32, (LEAD, n), 1)
-    whole_row = (row // n * 32 + my_row) * n + lax.rem(row, n)
-    for i in range(TILES):
-        upto = n * (i + 1)
-        sl = slice(n * i, upto)
+    for i in range(0, LEAD, 2 * n):
+        sl, upto = slice(i, i + 2 * n), i + 2 * n
         inv = x_ref[sl, 0:upto]
-        f = dot_nt(p_ref[:, 0:upto], inv)
-        factor_ref[:, sl] = jnp.where(col + n * i <= whole_row, f, 0.0)
         w_ref[sl, :] = dot(inv, y_ref[0:upto, :])
+        factor_ref[:, sl] = dot_nt(p_ref[:, 0:upto], inv)
+
+    @pl.when(my_row < TILES)
+    def _():
+        row = lax.broadcasted_iota(jnp.int32, (n, LEAD), 0) + my_row * n
+        lower = lax.broadcasted_iota(jnp.int32, (n, LEAD), 1) <= row
+        factor_ref[0:n, :] = jnp.where(lower, factor_ref[0:n, :], 0.0)
+
     put = pltpu.make_async_copy(factor_ref, factor_hbm, sem.at[6])
     put.start()
     z = dot(factor_ref[pl.ds(pl.multiple_of(core * 256, 256), 256), :], w_ref[...])
@@ -150,16 +152,12 @@
 
 
 def trailing_kernel(
-    ids_ref, x_hbm, factor_hbm, kernel_hbm, v0_hbm, v1_hbm, v2_hbm, v3_hbm, out_hbm,
+    ids_ref, x_hbm, factor_hbm, kernel_hbm, v_hbm, out_hbm,
     x_ref, factor_ref, kernel_ref, raw_ref, v_ref, f_ref, out_ref, sem,
 ):
     n = TB
     my_row, my_col = ids_ref[0], ids_ref[1]
-    x = lax.rem(my_row, 4)
-    gets = [
-        pltpu.make_async_copy(src, raw_ref.at[k], sem.at[k])
-        for k, src in enumerate((v0_hbm, v1_hbm, v2_hbm, v3_hbm))
-    ]
+    gets = [pltpu.make_async_copy(v_hbm.at[k], raw_ref.at[k], sem.at[k]) for k in range(4)]
     get_x = pltpu.make_async_copy(x_hbm, x_ref, sem.at[4])
     get_factor = pltpu.make_async_copy(factor_hbm, factor_ref, sem.at[5])
     tiles = [pl.ds(8 * n * a, 8 * n) for a in range(4)]
@@ -175,28 +173,31 @@
         copy.start()
     for k in range(4):
         gets[k].wait()
-        at = pl.ds(pl.multiple_of((x ^ k) * n, n), n)
         for b in range(8):
-            v_ref[at, n * b : n * b + n] = raw_ref[k, pl.ds(b, n, stride=8), :]
+            v_ref[n * k : n * k + n, n * b : n * b + n] = raw_ref[k, pl.ds(b, n, stride=8), :]
     get_x.wait()
-    for i in range(TILES):
-        upto = n * (i + 1)
-        f_ref[n * i : upto, :] = dot(x_ref[n * i : upto, 0:upto], v_ref[0:upto, :])
+    for i in range(0, LEAD, 2 * n):
+        upto = i + 2 * n
+        f_ref[i:upto, :] = dot(x_ref[i:upto, 0:upto], v_ref[0:upto, :])
     get_factor.wait()
-    for a in range(4):
-        get_tiles[a].wait()
+    for pair in range(2):
+        get_tiles[2 * pair].wait()
+        get_tiles[2 * pair + 1].wait()
         for h in range(4):
-            update = dot(factor_ref[n * a : n * a + n, :], f_ref[:, 256 * h : 256 * h + 256])
-            for half in range(2):
-                b = 2 * h + half
+            update = dot(
+                factor_ref[2 * n * pair : 2 * n * pair + 2 * n, :], f_ref[:, 256 * h : 256 * h + 256]
+            )
+            for up, half in ((0, 0), (0, 1), (1, 0), (1, 1)):
+                a, b = 2 * pair + up, 2 * h + half
                 at = pl.ds(8 * n * a + b, n, stride=8)
-                left = kernel_ref[at, :] - update[:, n * half : n * half + n]
+                left = kernel_ref[at, :] - update[n * up : n * up + n, n * half : n * half + n]
                 if a == 0:
                     left = jnp.where(my_row < TILES, 0.0, left)
                 if b == 0:
                     left = jnp.where(my_col < TILES, 0.0, left)
                 out_ref[at, :] = left
-        puts[a].start()
+        puts[2 * pair].start()
+        puts[2 * pair + 1].start()
     for put in puts:
         put.wait()
 
@@ -256,14 +257,14 @@
     t0 = jnp.concatenate([b[:TB] for b in blocks], axis=0)
     t2, t1 = permute_xor(t0, "col", 2), permute_xor(t0, "col", 1)
     got, pick = tree(lead, depth, False)
-    own_2 = permute_xor(own, "col", 2)
     wide = jnp.stack([b[TB:].reshape(8, 8, TB) for b in blocks]).transpose(2, 0, 1, 3)
     wide = lax.all_to_all(jnp.repeat(wide.reshape(8, 32, TB), 2, axis=0), "col", 0, 0)
     t3 = permute_xor(t2, "col", 1)
-    t1, t3, got, own_2, wide = force((t1, t3, got, own_2, wide))
-    lead = pick(got)
-    own_13 = permute_xor(jnp.concatenate([own, own_2], axis=0), "col", 1)
-    leads = [lead] + [permute_xor(lead, "row", k) for k in (1, 2, 3)]
+    t1, t3, got, wide = force((t1, t3, got, wide))
+    panel = [own] + [permute_xor(own, "col", k) for k in (1, 2, 3)]
+    leads = jnp.broadcast_to(pick(got)[None], (4, 8 * TB, TB))
+    groups = [[4 * z + x for x in range(4)] for z in range(lax.axis_size("row") // 4)]
+    leads = lax.all_to_all(leads, "row", 0, 0, axis_index_groups=groups)
 
     inverse = pl.pallas_call(
         chol_kernel,
@@ -279,6 +280,7 @@
         compiler_params=pltpu.CompilerParams(vmem_limit_bytes=BIG),
         cost_estimate=pl.CostEstimate(flops=2 * 10**10, bytes_accessed=3 << 20, transcendentals=0),
     )(ids, t0, t1, t2, t3)
+    inverse, leads = force((inverse, leads))
 
     factor, z = pl.pallas_call(
         panel_kernel,
@@ -286,7 +288,7 @@
             jax.ShapeDtypeStruct((LEAD, LEAD), f32),
             jax.ShapeDtypeStruct((2 * TB, TB), f32),
         ],
-        in_specs=[SMEM] + [HBM] * 5,
+        in_specs=[SMEM] + [HBM] * 6,
         out_specs=[HBM, VMEM],
         scratch_shapes=[
             pltpu.VMEM((LEAD, LEAD), f32),
@@ -299,12 +301,12 @@
         ],
         compiler_params=pltpu.CompilerParams(vmem_limit_bytes=BIG),
         cost_estimate=pl.CostEstimate(flops=2 * 10**9, bytes_accessed=4 << 20, transcendentals=0),
-    )(ids, inverse, wide, own, own_2, own_13)
+    )(ids, inverse, wide, *panel)
 
     trailing = pl.pallas_call(
         trailing_kernel,
         out_shape=jax.ShapeDtypeStruct((8 * LEAD, TB), f32),
-        in_specs=[SMEM] + [HBM] * 7,
+        in_specs=[SMEM] + [HBM] * 4,
         out_specs=HBM,
         scratch_shapes=[
             pltpu.VMEM((LEAD, LEAD), f32),
@@ -318,7 +320,7 @@
         ],
         compiler_params=pltpu.CompilerParams(vmem_limit_bytes=BIG),
         cost_estimate=pl.CostEstimate(flops=10**10, bytes_accessed=10 << 20, transcendentals=0),
-    )(ids, inverse, factor, kernel.reshape(8 * LEAD, TB), *leads)
+    )(ids, inverse, factor, kernel.reshape(8 * LEAD, TB), leads)
 
     got = lax.all_to_all(z.reshape(16, 2, 8, TB), "col", 0, 0).reshape(8, 2, 2, 8, TB)
     got = got.transpose(1, 2, 3, 0, 4).reshape(4, 8, 8 * TB)

time: 152 us -> 144 us (0.947)
  starting transfers between devices: 85.1 us -> 81.4 us
  waiting for transfers between devices: 11.9 us -> 8.99 us
    ppermute x10 -> x8, starting transfers between devices: 35.9 us -> 24 us  [permute_xor(): lax.ppermute(block, axis, [(i, i ^ k) for i in range(lax.axis_size(axis))])]
    ppermute x10 -> x8, waiting for transfers between devices: 10.9 us -> 4.04 us  [permute_xor(): lax.ppermute(block, axis, [(i, i ^ k) for i in range(lax.axis_size(axis))])]
    all_to_all x1, starting transfers between devices: 4.13 us -> 10 us  [per_device(): lax.all_to_all(jnp.repeat(wide.reshape(8, 32, TB), 2, axis=0), 'col', 0, 0)]
    all_to_all x0 -> x1, starting transfers between devices: none -> 3.8 us  [per_device(): leads = lax.all_to_all(leads, 'row', 0, 0, axis_index_groups=groups)]
    all_to_all x1, starting transfers between devices: 5.89 us -> 8.06 us  [per_device(): lax.all_to_all(z.reshape(16, 2, 8, TB), 'col', 0, 0).reshape(8, 2, 2, 8, TB)]
    all_to_all x0 -> x1, waiting for transfers between devices: none -> 2.02 us  [per_device(): leads = lax.all_to_all(leads, 'row', 0, 0, axis_index_groups=groups)]
    ppermute x1, starting transfers between devices: 5.92 us -> 3.92 us  [per_device(): own_got = lax.ppermute(own, 'col', [(c, c + 8) for c in range(4)])]
    ppermute x3, waiting for transfers between devices: 0.92 us -> 2.9 us  [per_device(): lax.ppermute(tile, 'col', [(c, c + d) for c in range(4)])]
  transfers between devices with their start and end apart: 25 -> 24, of which waited for: 3 -> 4; matrix products, arithmetic and copies ran while one was open for 4% -> 5% of each run, Pallas kernels for 28% -> 24%
where the time goes in v3:
time: 144 us; the launch traced here: 143 us
  starting transfers between devices  81.4 us (57%)
  Pallas kernels  41 us (28%)
  waiting for transfers between devices  8.99 us (6%)
  local copies, waits for them, and re-layouts  7.68 us (5%)
  other arithmetic  2.72 us (2%)
    pallas_call x1, Pallas kernels, per_device(): pl.pallas_call(chol_kernel, out_shape=jax.ShapeDtypeStruct((LEAD, LEAD),...  24.1 us
    ppermute x8, starting transfers between devices, permute_xor(): lax.ppermute(block, axis, [(i, i ^ k) for i in range(lax.axis_size(axis))])  24 us
    ppermute x8, starting transfers between devices, permute_z(): lax.ppermute(block, 'row', [(4 * a + x, 4 * b + x) for a, b in hops for x...  20 us
    pallas_call x1, Pallas kernels, per_device(): pl.pallas_call(trailing_kernel, out_shape=jax.ShapeDtypeStruct((8 * LEAD,...  10.5 us
    ppermute x3, starting transfers between devices, per_device(): lax.ppermute(tile, 'col', [(c, c + d) for c in range(4)])  10.2 us
    all_to_all x1, starting transfers between devices, per_device(): lax.all_to_all(jnp.repeat(wide.reshape(8, 32, TB), 2, axis=0), 'col', 0, 0)  10 us
    all_to_all x1, starting transfers between devices, per_device(): lax.all_to_all(z.reshape(16, 2, 8, TB), 'col', 0, 0).reshape(8, 2, 2, 8, TB)  8.06 us
    pallas_call x1, Pallas kernels, per_device(): pl.pallas_call(panel_kernel, out_shape=[jax.ShapeDtypeStruct((LEAD, LEAD)...  6.4 us
  transfers between devices with their start and end apart: 24, of which 4 were waited for; matrix products, arithmetic and copies ran while one was open for 5% of the time, Pallas kernels for 24%

profile of v3, /device:TPU:1, one launch (start us, length us, event | category | flops | bytes accessed | tf_op | source)
XLA Modules:
  0.0 143.0 jit_solution(9524223942009482555)
XLA Ops:
  1.7 5.0 %collective-permute-start = (f32[128,128]{1,0:T(8,128)S(1)}, f32[128,128]{1,0:T(8,128)S(1)}, u32[]{:S(2)}, u32[]{:S(2)}) collective-permute-start(f32[128,128]{1,0:T(8,128)S(1)} %bitcast.38), channel_id=1, source_target_pairs={{0,4},{1,5},{2,6},{3,7},{16,20},{17,21},{18,22},{19,23},{32,36},{3... | collective-permute-start | bytes 196616 | tf_op jit(solution)/shard_map/ppermute | solution.py:235
  6.8 3.9 %collective-permute-start.1 = (f32[128,128]{1,0:T(8,128)S(1)}, f32[128,128]{1,0:T(8,128)S(1)}, u32[]{:S(2)}, u32[]{:S(2)}) collective-permute-start(f32[128,128]{1,0:T(8,128)S(1)} %bitcast.39), channel_id=1, source_target_pairs={{0,8},{1,9},{2,10},{3,11},{16,24},{17,25},{18,26},{19,27},{32,40},... | collective-permute-start | bytes 196616 | tf_op jit(solution)/shard_map/ppermute | solution.py:235
  12.8 2.9 %collective-permute-done.2 = f32[128,128]{1,0:T(8,128)S(1)} collective-permute-done((f32[128,128]{1,0:T(8,128)S(1)}, f32[128,128]{1,0:T(8,128)S(1)}, u32[]{:S(2)}, u32[]{:S(2)}) %collective-permute-start.2) | collective-permute-done | bytes 65568 | tf_op jit(solution)/shard_map/ppermute | solution.py:235
  15.7 10.6 %collective-permute-start.3 = (f32[192,128]{1,0:T(8,128)S(1)}, f32[192,128]{1,0:T(8,128)S(1)}, u32[]{:S(2)}, u32[]{:S(2)}) collective-permute-start(f32[192,128]{1,0:T(8,128)S(1)} %pad_maximum_fusion.3), channel_id=1, source_target_pairs={{0,320},{16,336},{32,352},{48,368},{1,321},{17,337},{33,353},{49,3... | collective-permute-start | bytes 294920 | tf_op jit(solution)/shard_map/ppermute | solution.py:206
  27.7 1.7 %slice.44 = f32[4,128,1,128]{3,2,1,0:T(1,128)S(1)} slice(f32[4,128,8,128]{3,2,1,0:T(8,128)} %param.2), slice={[0:4], [0:128], [0:1], [0:128]} | slice | bytes 524288 | tf_op jit(solution)/shard_map/slice | solution.py:239
  29.4 3.9 %collective-permute-start.7 = (f32[512,128]{1,0:T(8,128)S(1)}, f32[512,128]{1,0:T(8,128)S(1)}, u32[]{:S(2)}, u32[]{:S(2)}) collective-permute-start(f32[512,128]{1,0:T(8,128)S(1)} %bitcast.32), channel_id=1, source_target_pairs={{0,8},{1,9},{2,10},{3,11},{16,24},{17,25},{18,26},{19,27},{32,40},... | collective-permute-start | bytes 786440 | tf_op jit(solution)/shard_map/ppermute | solution.py:242
  37.1 1.5 %collective-permute-start.10 = (f32[1024,128]{1,0:T(8,128)S(1)}, f32[1024,128]{1,0:T(8,128)S(1)}, u32[]{:S(2)}, u32[]{:S(2)}) collective-permute-start(f32[1024,128]{1,0:T(8,128)S(1)} %slice_bitcast_fusion), channel_id=1, source_target_pairs={{0,192},{16,208},{32,224},{48,240},{1,193},{17,209},{33,225},{49,2... | collective-permute-start | bytes 1572872 | tf_op jit(solution)/shard_map/ppermute | solution.py:206
  40.0 3.1 %collective-permute-start.8 = (f32[192,128]{1,0:T(8,128)S(1)}, f32[192,128]{1,0:T(8,128)S(1)}, u32[]{:S(2)}, u32[]{:S(2)}) collective-permute-start(f32[192,128]{1,0:T(8,128)S(1)} %select_select_fusion.2), channel_id=1, source_target_pairs={{0,16},{16,0},{32,48},{48,32},{64,80},{80,64},{96,112},{112,96},{1... | collective-permute-start | bytes 294920 | tf_op jit(solution)/shard_map/ppermute | solution.py:210
  45.4 4.4 %collective-permute-start.9 = (f32[384,128]{1,0:T(8,128)S(1)}, f32[384,128]{1,0:T(8,128)S(1)}, u32[]{:S(2)}, u32[]{:S(2)}) collective-permute-start(f32[384,128]{1,0:T(8,128)S(1)} %pad_maximum_fusion.1), channel_id=1, source_target_pairs={{0,48},{16,32},{32,16},{48,0},{64,112},{80,96},{96,80},{112,64},{1... | collective-permute-start | bytes 589832 | tf_op jit(solution)/shard_map/ppermute | solution.py:210
  49.8 3.2 %collective-permute-done.9 = f32[384,128]{1,0:T(8,128)S(1)} collective-permute-done((f32[384,128]{1,0:T(8,128)S(1)}, f32[384,128]{1,0:T(8,128)S(1)}, u32[]{:S(2)}, u32[]{:S(2)}) %collective-permute-start.9) | collective-permute-done | bytes 196640 | tf_op jit(solution)/shard_map/ppermute | solution.py:210
  53.0 4.3 %collective-permute-start.14 = (f32[512,128]{1,0:T(8,128)S(1)}, f32[512,128]{1,0:T(8,128)S(1)}, u32[]{:S(2)}, u32[]{:S(2)}) collective-permute-start(f32[512,128]{1,0:T(8,128)S(1)} %pad_maximum_fusion.t0), channel_id=1, source_target_pairs={{0,2},{1,3},{2,0},{3,1},{4,6},{5,7},{6,4},{7,5},{8,10},{9,11},{10,... | collective-permute-start | bytes 786440 | tf_op jit(solution)/shard_map/ppermute | solution.py:210
  62.0 10.0 %all-to-all-start = ((f32[16,32,128]{2,1,0:T(8,128)}), f32[16,32,128]{2,1,0:T(8,128)S(1)}, u32[]{:S(2)}, u32[]{:S(2)}) async-start(f32[16,32,128]{2,1,0:T(8,128)} %bitcast.11), calls=%async_computation | async-start | bytes 524288 | tf_op jit(solution)/shard_map/all_to_all | solution.py:261
  72.0 2.0 %collective-permute-start.13 = (f32[512,128]{1,0:T(8,128)S(1)}, f32[512,128]{1,0:T(8,128)S(1)}, u32[]{:S(2)}, u32[]{:S(2)}) collective-permute-start(f32[512,128]{1,0:T(8,128)S(1)} %pad_maximum_fusion.t0), channel_id=1, source_target_pairs={{0,1},{1,0},{2,3},{3,2},{4,5},{5,4},{6,7},{7,6},{8,9},{9,8},{10,11... | collective-permute-start | bytes 786440 | tf_op jit(solution)/shard_map/ppermute | solution.py:210
  74.1 2.3 %collective-permute-start.15 = (f32[512,128]{1,0:T(8,128)S(1)}, f32[512,128]{1,0:T(8,128)}, u32[]{:S(2)}, u32[]{:S(2)}) collective-permute-start(f32[512,128]{1,0:T(8,128)S(1)} %collective-permute-done.14.t2), channel_id=1, source_target_pairs={{0,1},{1,0},{2,3},{3,2},{4,5},{5,4},{6,7},{7,6},{8,9},{9,8},{10,11... | collective-permute-start | bytes 786440 | tf_op jit(solution)/shard_map/ppermute | solution.py:210
  77.0 2.0 %collective-permute-start.18 = (f32[512,128]{1,0:T(8,128)S(1)}, f32[512,128]{1,0:T(8,128)}, u32[]{:S(2)}, u32[]{:S(2)}) collective-permute-start(f32[512,128]{1,0:T(8,128)S(1)} %broadcast_select_fusion.p0), channel_id=1, source_target_pairs={{0,1},{1,0},{2,3},{3,2},{4,5},{5,4},{6,7},{7,6},{8,9},{9,8},{10,11... | collective-permute-start | bytes 786440 | tf_op jit(solution)/shard_map/ppermute | solution.py:210
  79.1 3.5 %collective-permute-start.19 = (f32[512,128]{1,0:T(8,128)S(1)}, f32[512,128]{1,0:T(8,128)S(1)}, u32[]{:S(2)}, u32[]{:S(2)}) collective-permute-start(f32[512,128]{1,0:T(8,128)S(1)} %broadcast_select_fusion.p0), channel_id=1, source_target_pairs={{0,2},{1,3},{2,0},{3,1},{4,6},{5,7},{6,4},{7,5},{8,10},{9,11},{10,... | collective-permute-start | bytes 786440 | tf_op jit(solution)/shard_map/ppermute | solution.py:210
  82.6 2.3 %collective-permute-start.20 = (f32[512,128]{1,0:T(8,128)S(1)}, f32[512,128]{1,0:T(8,128)}, u32[]{:S(2)}, u32[]{:S(2)}) collective-permute-start(f32[512,128]{1,0:T(8,128)S(1)} %broadcast_select_fusion.p0), channel_id=1, source_target_pairs={{0,3},{1,2},{2,1},{3,0},{4,7},{5,6},{6,5},{7,4},{8,11},{9,10},{10,... | collective-permute-start | bytes 786440 | tf_op jit(solution)/shard_map/ppermute | solution.py:210
  85.1 1.5 %broadcast_in_dim.20 = f32[4,1024,128]{2,1,0:T(8,128)} broadcast(f32[1024,128]{1,0:T(8,128)S(1)} %select_select_fusion), dimensions={1,2} | broadcast | bytes 2621440 | tf_op jit(solution)/shard_map/broadcast_in_dim | solution.py:265
  86.6 3.8 %all-to-all-start.1 = ((f32[4,1024,128]{2,1,0:T(8,128)}), f32[4,1024,128]{2,1,0:T(8,128)S(1)}, u32[]{:S(2)}, u32[]{:S(2)}) async-start(f32[4,1024,128]{2,1,0:T(8,128)} %broadcast_in_dim.20), calls=%async_computation.1 | async-start | bytes 4194304 | tf_op jit(solution)/shard_map/all_to_all | solution.py:267
  90.4 24.1 %shard_map.49.x_hbm = f32[512,512]{1,0:T(8,128)} custom-call(s32[2]{0:T(128)} %pad_add_fusion.ids_ref, f32[512,128]{1,0:T(8,128)} %copy-done.1, f32[512,128]{1,0:T(8,128)} %copy-done.6, f32[512,128]{1,0:T(8,128)} %copy-done.5, f32[512,128]{1,0:T(8,128)} %collective-permute-done.15.t3), custom_call_target="tpu_custom_call" | custom-call | flops 20000000000 | bytes 3145728 | tf_op jit(solution)/shard_map/pallas_call | solution.py:269
  114.4 2.0 %all-to-all-done.1.v_hbm = f32[4,1024,128]{2,1,0:T(8,128)S(1)} async-done(((f32[4,1024,128]{2,1,0:T(8,128)}), f32[4,1024,128]{2,1,0:T(8,128)S(1)}, u32[]{:S(2)}, u32[]{:S(2)}) %all-to-all-start.1) | async-done | bytes 2097184 | tf_op jit(solution)/shard_map/all_to_all | solution.py:267
  117.2 6.4 %shard_map.50 = (f32[512,512]{1,0:T(8,128)}, f32[256,128]{1,0:T(8,128)}) custom-call(s32[2]{0:T(128)} %pad_add_fusion.ids_ref, f32[512,512]{1,0:T(8,128)} %shard_map.49.x_hbm, f32[16,32,128]{2,1,0:T(8,128)} %copy-done.2, f32[512,128]{1,0:T(8,128)} %copy-done.3, f32[512,128]{1,0:T(8,128)} %collective-permute-done.18.p1, f32[512,128]{1,0:T(8,128)} %copy-done.7, ...), custom_call_target="tpu_custom_call" | custom-call | flops 2000000000 | bytes 4194304 | tf_op jit(solution)/shard_map/pallas_call | solution.py:285
  123.6 8.1 %all-to-all-start.2 = ((f32[16,2,8,128]{3,2,1,0:T(8,128)}), f32[16,2,8,128]{3,2,1,0:T(8,128)S(1)}, u32[]{:S(2)}, u32[]{:S(2)}) async-start(f32[16,2,8,128]{3,2,1,0:T(8,128)} %bitcast.42), calls=%async_computation.2 | async-start | bytes 262144 | tf_op jit(solution)/shard_map/all_to_all | solution.py:325
  131.7 10.5 %shard_map.51 = f32[4096,128]{1,0:T(8,128)} custom-call(s32[2]{0:T(128)} %pad_add_fusion.ids_ref, f32[512,512]{1,0:T(8,128)} %shard_map.49.x_hbm, f32[512,512]{1,0:T(8,128)} %get-tuple-element.32.factor_hbm, f32[4096,128]{1,0:T(8,128)} %bitcast.34, f32[4,1024,128]{2,1,0:T(8,128)} %copy-done), custom_call_target="tpu_custom_call" | custom-call | flops 10000000000 | bytes 10485760 | tf_op jit(solution)/shard_map/pallas_call | solution.py:306
  (72 shorter events, 18.6 us)
Async XLA Ops:
  1.7 11.1 %collective-permute-start = (f32[128,128]{1,0:T(8,128)S(1)}, f32[128,128]{1,0:T(8,128)S(1)}, u32[]{:S(2)}, u32[]{:S(2)}) collective-permute-start(f32[128,128]{1,0:T(8,128)S(1)} %bitcast.38), channel_id=1, source_target_pairs={{0,4},{1,5},{2,6},{3,7},{16,20},{17,21},{18,22},{19,23},{32,36},{3... | collective-permute-start | bytes 196616 | tf_op jit(solution)/shard_map/ppermute | solution.py:235
  6.8 6.0 %collective-permute-start.1 = (f32[128,128]{1,0:T(8,128)S(1)}, f32[128,128]{1,0:T(8,128)S(1)}, u32[]{:S(2)}, u32[]{:S(2)}) collective-permute-start(f32[128,128]{1,0:T(8,128)S(1)} %bitcast.39), channel_id=1, source_target_pairs={{0,8},{1,9},{2,10},{3,11},{16,24},{17,25},{18,26},{19,27},{32,40},... | collective-permute-start | bytes 196616 | tf_op jit(solution)/shard_map/ppermute | solution.py:235
  10.7 5.0 %collective-permute-start.2 = (f32[128,128]{1,0:T(8,128)S(1)}, f32[128,128]{1,0:T(8,128)S(1)}, u32[]{:S(2)}, u32[]{:S(2)}) collective-permute-start(f32[128,128]{1,0:T(8,128)S(1)} %bitcast.40), channel_id=1, source_target_pairs={{0,12},{1,13},{2,14},{3,15},{16,28},{17,29},{18,30},{19,31},{32,44... | collective-permute-start | bytes 196616 | tf_op jit(solution)/shard_map/ppermute | solution.py:235
  15.7 17.6 %collective-permute-start.3 = (f32[192,128]{1,0:T(8,128)S(1)}, f32[192,128]{1,0:T(8,128)S(1)}, u32[]{:S(2)}, u32[]{:S(2)}) collective-permute-start(f32[192,128]{1,0:T(8,128)S(1)} %pad_maximum_fusion.3), channel_id=1, source_target_pairs={{0,320},{16,336},{32,352},{48,368},{1,321},{17,337},{33,353},{49,3... | collective-permute-start | bytes 294920 | tf_op jit(solution)/shard_map/ppermute | solution.py:206
  26.4 7.0 %collective-permute-start.4 = (f32[192,128]{1,0:T(8,128)S(1)}, f32[192,128]{1,0:T(8,128)S(1)}, u32[]{:S(2)}, u32[]{:S(2)}) collective-permute-start(f32[192,128]{1,0:T(8,128)S(1)} %pad_maximum_fusion.3), channel_id=1, source_target_pairs={{0,192},{16,208},{32,224},{48,240},{1,193},{17,209},{33,225},{49,2... | collective-permute-start | bytes 294920 | tf_op jit(solution)/shard_map/ppermute | solution.py:206
  29.4 10.5 %collective-permute-start.7 = (f32[512,128]{1,0:T(8,128)S(1)}, f32[512,128]{1,0:T(8,128)S(1)}, u32[]{:S(2)}, u32[]{:S(2)}) collective-permute-start(f32[512,128]{1,0:T(8,128)S(1)} %bitcast.32), channel_id=1, source_target_pairs={{0,8},{1,9},{2,10},{3,11},{16,24},{17,25},{18,26},{19,27},{32,40},... | collective-permute-start | bytes 786440 | tf_op jit(solution)/shard_map/ppermute | solution.py:242
  33.4 6.5 %collective-permute-start.5 = (f32[192,128]{1,0:T(8,128)S(1)}, f32[192,128]{1,0:T(8,128)S(1)}, u32[]{:S(2)}, u32[]{:S(2)}) collective-permute-start(f32[192,128]{1,0:T(8,128)S(1)} %select_select_fusion.3), channel_id=1, source_target_pairs={{0,64},{16,80},{32,96},{48,112},{192,256},{208,272},{224,288},{240... | collective-permute-start | bytes 294920 | tf_op jit(solution)/shard_map/ppermute | solution.py:206
  34.7 5.2 %collective-permute-start.6 = (f32[192,128]{1,0:T(8,128)S(1)}, f32[192,128]{1,0:T(8,128)S(1)}, u32[]{:S(2)}, u32[]{:S(2)}) collective-permute-start(f32[192,128]{1,0:T(8,128)S(1)} %select_select_fusion.3), channel_id=1, source_target_pairs={{0,448},{16,464},{32,480},{48,496},{192,128},{208,144},{224,160},{... | collective-permute-start | bytes 294920 | tf_op jit(solution)/shard_map/ppermute | solution.py:206
  37.1 12.7 %collective-permute-start.10 = (f32[1024,128]{1,0:T(8,128)S(1)}, f32[1024,128]{1,0:T(8,128)S(1)}, u32[]{:S(2)}, u32[]{:S(2)}) collective-permute-start(f32[1024,128]{1,0:T(8,128)S(1)} %slice_bitcast_fusion), channel_id=1, source_target_pairs={{0,192},{16,208},{32,224},{48,240},{1,193},{17,209},{33,225},{49,2... | collective-permute-start | bytes 1572872 | tf_op jit(solution)/shard_map/ppermute | solution.py:206
  38.6 11.2 %collective-permute-start.11 = (f32[1024,128]{1,0:T(8,128)S(1)}, f32[1024,128]{1,0:T(8,128)S(1)}, u32[]{:S(2)}, u32[]{:S(2)}) collective-permute-start(f32[1024,128]{1,0:T(8,128)S(1)} %slice_bitcast_fusion), channel_id=1, source_target_pairs={{0,320},{16,336},{32,352},{48,368},{1,321},{17,337},{33,353},{49,3... | collective-permute-start | bytes 1572872 | tf_op jit(solution)/shard_map/ppermute | solution.py:206
  40.0 5.4 %collective-permute-start.8 = (f32[192,128]{1,0:T(8,128)S(1)}, f32[192,128]{1,0:T(8,128)S(1)}, u32[]{:S(2)}, u32[]{:S(2)}) collective-permute-start(f32[192,128]{1,0:T(8,128)S(1)} %select_select_fusion.2), channel_id=1, source_target_pairs={{0,16},{16,0},{32,48},{48,32},{64,80},{80,64},{96,112},{112,96},{1... | collective-permute-start | bytes 294920 | tf_op jit(solution)/shard_map/ppermute | solution.py:210
  43.2 6.6 %collective-permute-start.12 = (f32[512,128]{1,0:T(8,128)S(1)}, f32[512,128]{1,0:T(8,128)S(1)}, u32[]{:S(2)}, u32[]{:S(2)}) collective-permute-start(f32[512,128]{1,0:T(8,128)S(1)} %broadcast_select_fusion.1), channel_id=1, source_target_pairs={{0,4},{1,5},{2,6},{3,7},{8,12},{9,13},{10,14},{11,15},{16,20},{17,... | collective-permute-start | bytes 786440 | tf_op jit(solution)/shard_map/ppermute | solution.py:251
  45.4 7.6 %collective-permute-start.9 = (f32[384,128]{1,0:T(8,128)S(1)}, f32[384,128]{1,0:T(8,128)S(1)}, u32[]{:S(2)}, u32[]{:S(2)}) collective-permute-start(f32[384,128]{1,0:T(8,128)S(1)} %pad_maximum_fusion.1), channel_id=1, source_target_pairs={{0,48},{16,32},{32,16},{48,0},{64,112},{80,96},{96,80},{112,64},{1... | collective-permute-start | bytes 589832 | tf_op jit(solution)/shard_map/ppermute | solution.py:210
  53.0 21.0 %collective-permute-start.14 = (f32[512,128]{1,0:T(8,128)S(1)}, f32[512,128]{1,0:T(8,128)S(1)}, u32[]{:S(2)}, u32[]{:S(2)}) collective-permute-start(f32[512,128]{1,0:T(8,128)S(1)} %pad_maximum_fusion.t0), channel_id=1, source_target_pairs={{0,2},{1,3},{2,0},{3,1},{4,6},{5,7},{6,4},{7,5},{8,10},{9,11},{10,... | collective-permute-start | bytes 786440 | tf_op jit(solution)/shard_map/ppermute | solution.py:210
  58.5 24.2 %collective-permute-start.16 = (f32[1024,128]{1,0:T(8,128)S(1)}, f32[1024,128]{1,0:T(8,128)S(1)}, u32[]{:S(2)}, u32[]{:S(2)}) collective-permute-start(f32[1024,128]{1,0:T(8,128)S(1)} %select_select_fusion.1), channel_id=1, source_target_pairs={{0,64},{16,80},{32,96},{48,112},{192,256},{208,272},{224,288},{240... | collective-permute-start | bytes 1572872 | tf_op jit(solution)/shard_map/ppermute | solution.py:206
  59.8 25.2 %collective-permute-start.17 = (f32[1024,128]{1,0:T(8,128)S(1)}, f32[1024,128]{1,0:T(8,128)S(1)}, u32[]{:S(2)}, u32[]{:S(2)}) collective-permute-start(f32[1024,128]{1,0:T(8,128)S(1)} %select_select_fusion.1), channel_id=1, source_target_pairs={{0,448},{16,464},{32,480},{48,496},{192,128},{208,144},{224,160},{... | collective-permute-start | bytes 1572872 | tf_op jit(solution)/shard_map/ppermute | solution.py:206
  62.0 23.0 %all-to-all-start = ((f32[16,32,128]{2,1,0:T(8,128)}), f32[16,32,128]{2,1,0:T(8,128)S(1)}, u32[]{:S(2)}, u32[]{:S(2)}) async-start(f32[16,32,128]{2,1,0:T(8,128)} %bitcast.11), calls=%async_computation | async-start | bytes 524288 | tf_op jit(solution)/shard_map/all_to_all | solution.py:261
  72.0 7.1 %collective-permute-start.13 = (f32[512,128]{1,0:T(8,128)S(1)}, f32[512,128]{1,0:T(8,128)S(1)}, u32[]{:S(2)}, u32[]{:S(2)}) collective-permute-start(f32[512,128]{1,0:T(8,128)S(1)} %pad_maximum_fusion.t0), channel_id=1, source_target_pairs={{0,1},{1,0},{2,3},{3,2},{4,5},{5,4},{6,7},{7,6},{8,9},{9,8},{10,11... | collective-permute-start | bytes 786440 | tf_op jit(solution)/shard_map/ppermute | solution.py:210
  74.1 10.9 %collective-permute-start.15 = (f32[512,128]{1,0:T(8,128)S(1)}, f32[512,128]{1,0:T(8,128)}, u32[]{:S(2)}, u32[]{:S(2)}) collective-permute-start(f32[512,128]{1,0:T(8,128)S(1)} %collective-permute-done.14.t2), channel_id=1, source_target_pairs={{0,1},{1,0},{2,3},{3,2},{4,5},{5,4},{6,7},{7,6},{8,9},{9,8},{10,11... | collective-permute-start | bytes 786440 | tf_op jit(solution)/shard_map/ppermute | solution.py:210
  77.0 39.4 %collective-permute-start.18 = (f32[512,128]{1,0:T(8,128)S(1)}, f32[512,128]{1,0:T(8,128)}, u32[]{:S(2)}, u32[]{:S(2)}) collective-permute-start(f32[512,128]{1,0:T(8,128)S(1)} %broadcast_select_fusion.p0), channel_id=1, source_target_pairs={{0,1},{1,0},{2,3},{3,2},{4,5},{5,4},{6,7},{7,6},{8,9},{9,8},{10,11... | collective-permute-start | bytes 786440 | tf_op jit(solution)/shard_map/ppermute | solution.py:210
  79.1 37.4 %collective-permute-start.19 = (f32[512,128]{1,0:T(8,128)S(1)}, f32[512,128]{1,0:T(8,128)S(1)}, u32[]{:S(2)}, u32[]{:S(2)}) collective-permute-start(f32[512,128]{1,0:T(8,128)S(1)} %broadcast_select_fusion.p0), channel_id=1, source_target_pairs={{0,2},{1,3},{2,0},{3,1},{4,6},{5,7},{6,4},{7,5},{8,10},{9,11},{10,... | collective-permute-start | bytes 786440 | tf_op jit(solution)/shard_map/ppermute | solution.py:210
  82.6 33.8 %collective-permute-start.20 = (f32[512,128]{1,0:T(8,128)S(1)}, f32[512,128]{1,0:T(8,128)}, u32[]{:S(2)}, u32[]{:S(2)}) collective-permute-start(f32[512,128]{1,0:T(8,128)S(1)} %broadcast_select_fusion.p0), channel_id=1, source_target_pairs={{0,3},{1,2},{2,1},{3,0},{4,7},{5,6},{6,5},{7,4},{8,11},{9,10},{10,... | collective-permute-start | bytes 786440 | tf_op jit(solution)/shard_map/ppermute | solution.py:210
  86.6 29.9 %all-to-all-start.1 = ((f32[4,1024,128]{2,1,0:T(8,128)}), f32[4,1024,128]{2,1,0:T(8,128)S(1)}, u32[]{:S(2)}, u32[]{:S(2)}) async-start(f32[4,1024,128]{2,1,0:T(8,128)} %broadcast_in_dim.20), calls=%async_computation.1 | async-start | bytes 4194304 | tf_op jit(solution)/shard_map/all_to_all | solution.py:267
  123.6 18.6 %all-to-all-start.2 = ((f32[16,2,8,128]{3,2,1,0:T(8,128)}), f32[16,2,8,128]{3,2,1,0:T(8,128)S(1)}, u32[]{:S(2)}, u32[]{:S(2)}) async-start(f32[16,2,8,128]{3,2,1,0:T(8,128)} %bitcast.42), calls=%async_computation.2 | async-start | bytes 262144 | tf_op jit(solution)/shard_map/all_to_all | solution.py:325
  (8 other events, 73.5 us)

commit v4 on v3

--- a/solution.py
+++ b/solution.py
@@ -26,6 +26,15 @@
     return lax.dot_general(
         a, b, (((1,), (1,)), ((), ())), precision=highest, preferred_element_type=jnp.float32
     )
+
+
+def halves(a):
+    high = a.astype(jnp.bfloat16)
+    return high, (a - high.astype(jnp.float32)).astype(jnp.bfloat16)
+
+
+def dot_half(a, b):
+    return jnp.dot(a, b, preferred_element_type=jnp.float32)
 
 
 def recip(p):
@@ -119,15 +128,19 @@
         gets.append(pltpu.make_async_copy(src, p_ref.at[:, cols], sem.at[2 + k]))
     for get in gets:
         get.start()
-    for get in gets:
-        get.wait()
+    gets[1].wait()
     for at, k in enumerate(ORDER):
         for c in range(16):
             y_ref[pl.ds(pl.multiple_of((x ^ k) * n + 8 * c, 8), 8), :] = raw_ref[c, 8 * at : 8 * at + 8, :]
+    gets[0].wait()
+    for i in range(0, LEAD, 2 * n):
+        sl, upto = slice(i, i + 2 * n), i + 2 * n
+        w_ref[sl, :] = dot(x_ref[sl, 0:upto], y_ref[0:upto, :])
+    for get in gets[2:]:
+        get.wait()
     for i in range(0, LEAD, 2 * n):
         sl, upto = slice(i, i + 2 * n), i + 2 * n
         inv = x_ref[sl, 0:upto]
-        w_ref[sl, :] = dot(inv, y_ref[0:upto, :])
         factor_ref[:, sl] = dot_nt(p_ref[:, 0:upto], inv)
 
     @pl.when(my_row < TILES)
@@ -153,7 +166,7 @@
 
 def trailing_kernel(
     ids_ref, x_hbm, factor_hbm, kernel_hbm, v_hbm, out_hbm,
-    x_ref, factor_ref, kernel_ref, raw_ref, v_ref, f_ref, out_ref, sem,
+    x_ref, factor_ref, kernel_ref, raw_ref, v_ref, high_ref, low_ref, out_ref, sem,
 ):
     n = TB
     my_row, my_col = ids_ref[0], ids_ref[1]
@@ -178,15 +191,18 @@
     get_x.wait()
     for i in range(0, LEAD, 2 * n):
         upto = i + 2 * n
-        f_ref[i:upto, :] = dot(x_ref[i:upto, 0:upto], v_ref[0:upto, :])
+        high, low = halves(dot(x_ref[i:upto, 0:upto], v_ref[0:upto, :]))
+        high_ref[i:upto, :] = high
+        low_ref[i:upto, :] = low
     get_factor.wait()
     for pair in range(2):
         get_tiles[2 * pair].wait()
         get_tiles[2 * pair + 1].wait()
+        high, low = halves(factor_ref[2 * n * pair : 2 * n * pair + 2 * n, :])
         for h in range(4):
-            update = dot(
-                factor_ref[2 * n * pair : 2 * n * pair + 2 * n, :], f_ref[:, 256 * h : 256 * h + 256]
-            )
+            cols = slice(256 * h, 256 * h + 256)
+            update = dot_half(high, high_ref[:, cols]) + dot_half(high, low_ref[:, cols])
+            update = update + dot_half(low, high_ref[:, cols])
             for up, half in ((0, 0), (0, 1), (1, 0), (1, 1)):
                 a, b = 2 * pair + up, 2 * h + half
                 at = pl.ds(8 * n * a + b, n, stride=8)
@@ -314,7 +330,8 @@
             pltpu.VMEM((8 * LEAD, TB), f32),
             pltpu.VMEM((4, 8 * TB, TB), f32),
             pltpu.VMEM((LEAD, 8 * TB), f32),
-            pltpu.VMEM((LEAD, 8 * TB), f32),
+            pltpu.VMEM((LEAD, 8 * TB), jnp.bfloat16),
+            pltpu.VMEM((LEAD, 8 * TB), jnp.bfloat16),
             pltpu.VMEM((8 * LEAD, TB), f32),
             pltpu.SemaphoreType.DMA((14,)),
         ],

time: 144 us -> 143 us (level)
  Pallas kernels: 41 us -> 39.2 us
    pallas_call x1, Pallas kernels: 10.5 us -> 8.81 us  [per_device(): pl.pallas_call(trailing_kernel, out_shape=jax.ShapeDtypeStruct((8 * LEAD,...]
  transfers between devices with their start and end apart: 24 -> 24, of which waited for: 4 -> 5; matrix products, arithmetic and copies ran while one was open for 5% -> 5% of each run, Pallas kernels for 24% -> 23%
where the time goes in v4:
time: 143 us; the launch traced here: 142 us
  starting transfers between devices  81.4 us (57%)
  Pallas kernels  39.2 us (27%)
  waiting for transfers between devices  9.33 us (7%)
  local copies, waits for them, and re-layouts  7.68 us (5%)
  other arithmetic  2.72 us (2%)
    pallas_call x1, Pallas kernels, per_device(): pl.pallas_call(chol_kernel, out_shape=jax.ShapeDtypeStruct((LEAD, LEAD),...  24.1 us
    ppermute x8, starting transfers between devices, permute_xor(): lax.ppermute(block, axis, [(i, i ^ k) for i in range(lax.axis_size(axis))])  24 us
    ppermute x8, starting transfers between devices, permute_z(): lax.ppermute(block, 'row', [(4 * a + x, 4 * b + x) for a, b in hops for x...  20 us
    ppermute x3, starting transfers between devices, per_device(): lax.ppermute(tile, 'col', [(c, c + d) for c in range(4)])  10.2 us
    all_to_all x1, starting transfers between devices, per_device(): lax.all_to_all(jnp.repeat(wide.reshape(8, 32, TB), 2, axis=0), 'col', 0, 0)  10 us
    pallas_call x1, Pallas kernels, per_device(): pl.pallas_call(trailing_kernel, out_shape=jax.ShapeDtypeStruct((8 * LEAD,...  8.81 us
    all_to_all x1, starting transfers between devices, per_device(): lax.all_to_all(z.reshape(16, 2, 8, TB), 'col', 0, 0).reshape(8, 2, 2, 8, TB)  8.05 us
    pallas_call x1, Pallas kernels, per_device(): pl.pallas_call(panel_kernel, out_shape=[jax.ShapeDtypeStruct((LEAD, LEAD)...  6.29 us
  transfers between devices with their start and end apart: 24, of which 5 were waited for; matrix products, arithmetic and copies ran while one was open for 5% of the time, Pallas kernels for 23%

profile of v4, /device:TPU:1, one launch (start us, length us, event | category | flops | bytes accessed | tf_op | source)
XLA Modules:
  0.0 141.5 jit_solution(10792650022961664083)
XLA Ops:
  1.7 5.0 %collective-permute-start = (f32[128,128]{1,0:T(8,128)S(1)}, f32[128,128]{1,0:T(8,128)S(1)}, u32[]{:S(2)}, u32[]{:S(2)}) collective-permute-start(f32[128,128]{1,0:T(8,128)S(1)} %bitcast.38), channel_id=1, source_target_pairs={{0,4},{1,5},{2,6},{3,7},{16,20},{17,21},{18,22},{19,23},{32,36},{3... | collective-permute-start | bytes 196616 | tf_op jit(solution)/shard_map/ppermute | solution.py:251
  6.8 3.9 %collective-permute-start.1 = (f32[128,128]{1,0:T(8,128)S(1)}, f32[128,128]{1,0:T(8,128)S(1)}, u32[]{:S(2)}, u32[]{:S(2)}) collective-permute-start(f32[128,128]{1,0:T(8,128)S(1)} %bitcast.39), channel_id=1, source_target_pairs={{0,8},{1,9},{2,10},{3,11},{16,24},{17,25},{18,26},{19,27},{32,40},... | collective-permute-start | bytes 196616 | tf_op jit(solution)/shard_map/ppermute | solution.py:251
  12.8 2.9 %collective-permute-done.2 = f32[128,128]{1,0:T(8,128)S(1)} collective-permute-done((f32[128,128]{1,0:T(8,128)S(1)}, f32[128,128]{1,0:T(8,128)S(1)}, u32[]{:S(2)}, u32[]{:S(2)}) %collective-permute-start.2) | collective-permute-done | bytes 65568 | tf_op jit(solution)/shard_map/ppermute | solution.py:251
  15.7 10.6 %collective-permute-start.3 = (f32[192,128]{1,0:T(8,128)S(1)}, f32[192,128]{1,0:T(8,128)S(1)}, u32[]{:S(2)}, u32[]{:S(2)}) collective-permute-start(f32[192,128]{1,0:T(8,128)S(1)} %pad_maximum_fusion.3), channel_id=1, source_target_pairs={{0,320},{16,336},{32,352},{48,368},{1,321},{17,337},{33,353},{49,3... | collective-permute-start | bytes 294920 | tf_op jit(solution)/shard_map/ppermute | solution.py:222
  27.7 1.7 %slice.44 = f32[4,128,1,128]{3,2,1,0:T(1,128)S(1)} slice(f32[4,128,8,128]{3,2,1,0:T(8,128)} %param.2), slice={[0:4], [0:128], [0:1], [0:128]} | slice | bytes 524288 | tf_op jit(solution)/shard_map/slice | solution.py:255
  29.4 3.9 %collective-permute-start.7 = (f32[512,128]{1,0:T(8,128)S(1)}, f32[512,128]{1,0:T(8,128)S(1)}, u32[]{:S(2)}, u32[]{:S(2)}) collective-permute-start(f32[512,128]{1,0:T(8,128)S(1)} %bitcast.32), channel_id=1, source_target_pairs={{0,8},{1,9},{2,10},{3,11},{16,24},{17,25},{18,26},{19,27},{32,40},... | collective-permute-start | bytes 786440 | tf_op jit(solution)/shard_map/ppermute | solution.py:258
  37.1 1.5 %collective-permute-start.10 = (f32[1024,128]{1,0:T(8,128)S(1)}, f32[1024,128]{1,0:T(8,128)S(1)}, u32[]{:S(2)}, u32[]{:S(2)}) collective-permute-start(f32[1024,128]{1,0:T(8,128)S(1)} %slice_bitcast_fusion), channel_id=1, source_target_pairs={{0,192},{16,208},{32,224},{48,240},{1,193},{17,209},{33,225},{49,2... | collective-permute-start | bytes 1572872 | tf_op jit(solution)/shard_map/ppermute | solution.py:222
  40.0 3.1 %collective-permute-start.8 = (f32[192,128]{1,0:T(8,128)S(1)}, f32[192,128]{1,0:T(8,128)S(1)}, u32[]{:S(2)}, u32[]{:S(2)}) collective-permute-start(f32[192,128]{1,0:T(8,128)S(1)} %select_select_fusion.2), channel_id=1, source_target_pairs={{0,16},{16,0},{32,48},{48,32},{64,80},{80,64},{96,112},{112,96},{1... | collective-permute-start | bytes 294920 | tf_op jit(solution)/shard_map/ppermute | solution.py:226
  45.4 4.4 %collective-permute-start.9 = (f32[384,128]{1,0:T(8,128)S(1)}, f32[384,128]{1,0:T(8,128)S(1)}, u32[]{:S(2)}, u32[]{:S(2)}) collective-permute-start(f32[384,128]{1,0:T(8,128)S(1)} %pad_maximum_fusion.1), channel_id=1, source_target_pairs={{0,48},{16,32},{32,16},{48,0},{64,112},{80,96},{96,80},{112,64},{1... | collective-permute-start | bytes 589832 | tf_op jit(solution)/shard_map/ppermute | solution.py:226
  49.8 3.2 %collective-permute-done.9 = f32[384,128]{1,0:T(8,128)S(1)} collective-permute-done((f32[384,128]{1,0:T(8,128)S(1)}, f32[384,128]{1,0:T(8,128)S(1)}, u32[]{:S(2)}, u32[]{:S(2)}) %collective-permute-start.9) | collective-permute-done | bytes 196640 | tf_op jit(solution)/shard_map/ppermute | solution.py:226
  53.0 4.3 %collective-permute-start.14 = (f32[512,128]{1,0:T(8,128)S(1)}, f32[512,128]{1,0:T(8,128)S(1)}, u32[]{:S(2)}, u32[]{:S(2)}) collective-permute-start(f32[512,128]{1,0:T(8,128)S(1)} %pad_maximum_fusion.t0), channel_id=1, source_target_pairs={{0,2},{1,3},{2,0},{3,1},{4,6},{5,7},{6,4},{7,5},{8,10},{9,11},{10,... | collective-permute-start | bytes 786440 | tf_op jit(solution)/shard_map/ppermute | solution.py:226
  62.0 10.0 %all-to-all-start = ((f32[16,32,128]{2,1,0:T(8,128)}), f32[16,32,128]{2,1,0:T(8,128)S(1)}, u32[]{:S(2)}, u32[]{:S(2)}) async-start(f32[16,32,128]{2,1,0:T(8,128)} %bitcast.11), calls=%async_computation | async-start | bytes 524288 | tf_op jit(solution)/shard_map/all_to_all | solution.py:277
  72.0 2.0 %collective-permute-start.13 = (f32[512,128]{1,0:T(8,128)S(1)}, f32[512,128]{1,0:T(8,128)S(1)}, u32[]{:S(2)}, u32[]{:S(2)}) collective-permute-start(f32[512,128]{1,0:T(8,128)S(1)} %pad_maximum_fusion.t0), channel_id=1, source_target_pairs={{0,1},{1,0},{2,3},{3,2},{4,5},{5,4},{6,7},{7,6},{8,9},{9,8},{10,11... | collective-permute-start | bytes 786440 | tf_op jit(solution)/shard_map/ppermute | solution.py:226
  74.1 2.3 %collective-permute-start.15 = (f32[512,128]{1,0:T(8,128)S(1)}, f32[512,128]{1,0:T(8,128)}, u32[]{:S(2)}, u32[]{:S(2)}) collective-permute-start(f32[512,128]{1,0:T(8,128)S(1)} %collective-permute-done.14.t2), channel_id=1, source_target_pairs={{0,1},{1,0},{2,3},{3,2},{4,5},{5,4},{6,7},{7,6},{8,9},{9,8},{10,11... | collective-permute-start | bytes 786440 | tf_op jit(solution)/shard_map/ppermute | solution.py:226
  77.0 2.0 %collective-permute-start.18 = (f32[512,128]{1,0:T(8,128)S(1)}, f32[512,128]{1,0:T(8,128)}, u32[]{:S(2)}, u32[]{:S(2)}) collective-permute-start(f32[512,128]{1,0:T(8,128)S(1)} %broadcast_select_fusion.p0), channel_id=1, source_target_pairs={{0,1},{1,0},{2,3},{3,2},{4,5},{5,4},{6,7},{7,6},{8,9},{9,8},{10,11... | collective-permute-start | bytes 786440 | tf_op jit(solution)/shard_map/ppermute | solution.py:226
  79.1 3.5 %collective-permute-start.19 = (f32[512,128]{1,0:T(8,128)S(1)}, f32[512,128]{1,0:T(8,128)S(1)}, u32[]{:S(2)}, u32[]{:S(2)}) collective-permute-start(f32[512,128]{1,0:T(8,128)S(1)} %broadcast_select_fusion.p0), channel_id=1, source_target_pairs={{0,2},{1,3},{2,0},{3,1},{4,6},{5,7},{6,4},{7,5},{8,10},{9,11},{10,... | collective-permute-start | bytes 786440 | tf_op jit(solution)/shard_map/ppermute | solution.py:226
  82.6 2.3 %collective-permute-start.20 = (f32[512,128]{1,0:T(8,128)S(1)}, f32[512,128]{1,0:T(8,128)}, u32[]{:S(2)}, u32[]{:S(2)}) collective-permute-start(f32[512,128]{1,0:T(8,128)S(1)} %broadcast_select_fusion.p0), channel_id=1, source_target_pairs={{0,3},{1,2},{2,1},{3,0},{4,7},{5,6},{6,5},{7,4},{8,11},{9,10},{10,... | collective-permute-start | bytes 786440 | tf_op jit(solution)/shard_map/ppermute | solution.py:226
  85.1 1.5 %broadcast_in_dim.20 = f32[4,1024,128]{2,1,0:T(8,128)} broadcast(f32[1024,128]{1,0:T(8,128)S(1)} %select_select_fusion), dimensions={1,2} | broadcast | bytes 2621440 | tf_op jit(solution)/shard_map/broadcast_in_dim | solution.py:281
  86.6 3.8 %all-to-all-start.1 = ((f32[4,1024,128]{2,1,0:T(8,128)}), f32[4,1024,128]{2,1,0:T(8,128)S(1)}, u32[]{:S(2)}, u32[]{:S(2)}) async-start(f32[4,1024,128]{2,1,0:T(8,128)} %broadcast_in_dim.20), calls=%async_computation.1 | async-start | bytes 4194304 | tf_op jit(solution)/shard_map/all_to_all | solution.py:283
  90.4 24.1 %shard_map.49.x_hbm = f32[512,512]{1,0:T(8,128)} custom-call(s32[2]{0:T(128)} %pad_add_fusion.ids_ref, f32[512,128]{1,0:T(8,128)} %copy-done.1, f32[512,128]{1,0:T(8,128)} %copy-done.6, f32[512,128]{1,0:T(8,128)} %copy-done.5, f32[512,128]{1,0:T(8,128)} %collective-permute-done.15.t3), custom_call_target="tpu_custom_call" | custom-call | flops 20000000000 | bytes 3145728 | tf_op jit(solution)/shard_map/pallas_call | solution.py:285
  114.4 2.0 %all-to-all-done.1.v_hbm = f32[4,1024,128]{2,1,0:T(8,128)S(1)} async-done(((f32[4,1024,128]{2,1,0:T(8,128)}), f32[4,1024,128]{2,1,0:T(8,128)S(1)}, u32[]{:S(2)}, u32[]{:S(2)}) %all-to-all-start.1) | async-done | bytes 2097184 | tf_op jit(solution)/shard_map/all_to_all | solution.py:283
  117.2 6.3 %shard_map.50 = (f32[512,512]{1,0:T(8,128)}, f32[256,128]{1,0:T(8,128)}) custom-call(s32[2]{0:T(128)} %pad_add_fusion.ids_ref, f32[512,512]{1,0:T(8,128)} %shard_map.49.x_hbm, f32[16,32,128]{2,1,0:T(8,128)} %copy-done.2, f32[512,128]{1,0:T(8,128)} %copy-done.3, f32[512,128]{1,0:T(8,128)} %collective-permute-done.18.p1, f32[512,128]{1,0:T(8,128)} %copy-done.7, ...), custom_call_target="tpu_custom_call" | custom-call | flops 2000000000 | bytes 4194304 | tf_op jit(solution)/shard_map/pallas_call | solution.py:301
  123.5 8.1 %all-to-all-start.2 = ((f32[16,2,8,128]{3,2,1,0:T(8,128)}), f32[16,2,8,128]{3,2,1,0:T(8,128)S(1)}, u32[]{:S(2)}, u32[]{:S(2)}) async-start(f32[16,2,8,128]{3,2,1,0:T(8,128)} %bitcast.42), calls=%async_computation.2 | async-start | bytes 262144 | tf_op jit(solution)/shard_map/all_to_all | solution.py:342
  131.6 8.8 %shard_map.51 = f32[4096,128]{1,0:T(8,128)} custom-call(s32[2]{0:T(128)} %pad_add_fusion.ids_ref, f32[512,512]{1,0:T(8,128)} %shard_map.49.x_hbm, f32[512,512]{1,0:T(8,128)} %get-tuple-element.32.factor_hbm, f32[4096,128]{1,0:T(8,128)} %bitcast.34, f32[4,1024,128]{2,1,0:T(8,128)} %copy-done), custom_call_target="tpu_custom_call" | custom-call | flops 10000000000 | bytes 10485760 | tf_op jit(solution)/shard_map/pallas_call | solution.py:322
  (72 shorter events, 19.0 us)
Async XLA Ops:
  1.7 11.1 %collective-permute-start = (f32[128,128]{1,0:T(8,128)S(1)}, f32[128,128]{1,0:T(8,128)S(1)}, u32[]{:S(2)}, u32[]{:S(2)}) collective-permute-start(f32[128,128]{1,0:T(8,128)S(1)} %bitcast.38), channel_id=1, source_target_pairs={{0,4},{1,5},{2,6},{3,7},{16,20},{17,21},{18,22},{19,23},{32,36},{3... | collective-permute-start | bytes 196616 | tf_op jit(solution)/shard_map/ppermute | solution.py:251
  6.8 6.0 %collective-permute-start.1 = (f32[128,128]{1,0:T(8,128)S(1)}, f32[128,128]{1,0:T(8,128)S(1)}, u32[]{:S(2)}, u32[]{:S(2)}) collective-permute-start(f32[128,128]{1,0:T(8,128)S(1)} %bitcast.39), channel_id=1, source_target_pairs={{0,8},{1,9},{2,10},{3,11},{16,24},{17,25},{18,26},{19,27},{32,40},... | collective-permute-start | bytes 196616 | tf_op jit(solution)/shard_map/ppermute | solution.py:251
  10.7 5.0 %collective-permute-start.2 = (f32[128,128]{1,0:T(8,128)S(1)}, f32[128,128]{1,0:T(8,128)S(1)}, u32[]{:S(2)}, u32[]{:S(2)}) collective-permute-start(f32[128,128]{1,0:T(8,128)S(1)} %bitcast.40), channel_id=1, source_target_pairs={{0,12},{1,13},{2,14},{3,15},{16,28},{17,29},{18,30},{19,31},{32,44... | collective-permute-start | bytes 196616 | tf_op jit(solution)/shard_map/ppermute | solution.py:251
  15.7 17.6 %collective-permute-start.3 = (f32[192,128]{1,0:T(8,128)S(1)}, f32[192,128]{1,0:T(8,128)S(1)}, u32[]{:S(2)}, u32[]{:S(2)}) collective-permute-start(f32[192,128]{1,0:T(8,128)S(1)} %pad_maximum_fusion.3), channel_id=1, source_target_pairs={{0,320},{16,336},{32,352},{48,368},{1,321},{17,337},{33,353},{49,3... | collective-permute-start | bytes 294920 | tf_op jit(solution)/shard_map/ppermute | solution.py:222
  26.4 7.0 %collective-permute-start.4 = (f32[192,128]{1,0:T(8,128)S(1)}, f32[192,128]{1,0:T(8,128)S(1)}, u32[]{:S(2)}, u32[]{:S(2)}) collective-permute-start(f32[192,128]{1,0:T(8,128)S(1)} %pad_maximum_fusion.3), channel_id=1, source_target_pairs={{0,192},{16,208},{32,224},{48,240},{1,193},{17,209},{33,225},{49,2... | collective-permute-start | bytes 294920 | tf_op jit(solution)/shard_map/ppermute | solution.py:222
  29.4 10.5 %collective-permute-start.7 = (f32[512,128]{1,0:T(8,128)S(1)}, f32[512,128]{1,0:T(8,128)S(1)}, u32[]{:S(2)}, u32[]{:S(2)}) collective-permute-start(f32[512,128]{1,0:T(8,128)S(1)} %bitcast.32), channel_id=1, source_target_pairs={{0,8},{1,9},{2,10},{3,11},{16,24},{17,25},{18,26},{19,27},{32,40},... | collective-permute-start | bytes 786440 | tf_op jit(solution)/shard_map/ppermute | solution.py:258
  33.4 6.5 %collective-permute-start.5 = (f32[192,128]{1,0:T(8,128)S(1)}, f32[192,128]{1,0:T(8,128)S(1)}, u32[]{:S(2)}, u32[]{:S(2)}) collective-permute-start(f32[192,128]{1,0:T(8,128)S(1)} %select_select_fusion.3), channel_id=1, source_target_pairs={{0,64},{16,80},{32,96},{48,112},{192,256},{208,272},{224,288},{240... | collective-permute-start | bytes 294920 | tf_op jit(solution)/shard_map/ppermute | solution.py:222
  34.7 5.2 %collective-permute-start.6 = (f32[192,128]{1,0:T(8,128)S(1)}, f32[192,128]{1,0:T(8,128)S(1)}, u32[]{:S(2)}, u32[]{:S(2)}) collective-permute-start(f32[192,128]{1,0:T(8,128)S(1)} %select_select_fusion.3), channel_id=1, source_target_pairs={{0,448},{16,464},{32,480},{48,496},{192,128},{208,144},{224,160},{... | collective-permute-start | bytes 294920 | tf_op jit(solution)/shard_map/ppermute | solution.py:222
  37.1 12.7 %collective-permute-start.10 = (f32[1024,128]{1,0:T(8,128)S(1)}, f32[1024,128]{1,0:T(8,128)S(1)}, u32[]{:S(2)}, u32[]{:S(2)}) collective-permute-start(f32[1024,128]{1,0:T(8,128)S(1)} %slice_bitcast_fusion), channel_id=1, source_target_pairs={{0,192},{16,208},{32,224},{48,240},{1,193},{17,209},{33,225},{49,2... | collective-permute-start | bytes 1572872 | tf_op jit(solution)/shard_map/ppermute | solution.py:222
  38.6 11.2 %collective-permute-start.11 = (f32[1024,128]{1,0:T(8,128)S(1)}, f32[1024,128]{1,0:T(8,128)S(1)}, u32[]{:S(2)}, u32[]{:S(2)}) collective-permute-start(f32[1024,128]{1,0:T(8,128)S(1)} %slice_bitcast_fusion), channel_id=1, source_target_pairs={{0,320},{16,336},{32,352},{48,368},{1,321},{17,337},{33,353},{49,3... | collective-permute-start | bytes 1572872 | tf_op jit(solution)/shard_map/ppermute | solution.py:222
  40.0 5.4 %collective-permute-start.8 = (f32[192,128]{1,0:T(8,128)S(1)}, f32[192,128]{1,0:T(8,128)S(1)}, u32[]{:S(2)}, u32[]{:S(2)}) collective-permute-start(f32[192,128]{1,0:T(8,128)S(1)} %select_select_fusion.2), channel_id=1, source_target_pairs={{0,16},{16,0},{32,48},{48,32},{64,80},{80,64},{96,112},{112,96},{1... | collective-permute-start | bytes 294920 | tf_op jit(solution)/shard_map/ppermute | solution.py:226
  43.2 6.6 %collective-permute-start.12 = (f32[512,128]{1,0:T(8,128)S(1)}, f32[512,128]{1,0:T(8,128)S(1)}, u32[]{:S(2)}, u32[]{:S(2)}) collective-permute-start(f32[512,128]{1,0:T(8,128)S(1)} %broadcast_select_fusion.1), channel_id=1, source_target_pairs={{0,4},{1,5},{2,6},{3,7},{8,12},{9,13},{10,14},{11,15},{16,20},{17,... | collective-permute-start | bytes 786440 | tf_op jit(solution)/shard_map/ppermute | solution.py:267
  45.4 7.6 %collective-permute-start.9 = (f32[384,128]{1,0:T(8,128)S(1)}, f32[384,128]{1,0:T(8,128)S(1)}, u32[]{:S(2)}, u32[]{:S(2)}) collective-permute-start(f32[384,128]{1,0:T(8,128)S(1)} %pad_maximum_fusion.1), channel_id=1, source_target_pairs={{0,48},{16,32},{32,16},{48,0},{64,112},{80,96},{96,80},{112,64},{1... | collective-permute-start | bytes 589832 | tf_op jit(solution)/shard_map/ppermute | solution.py:226
  53.0 21.0 %collective-permute-start.14 = (f32[512,128]{1,0:T(8,128)S(1)}, f32[512,128]{1,0:T(8,128)S(1)}, u32[]{:S(2)}, u32[]{:S(2)}) collective-permute-start(f32[512,128]{1,0:T(8,128)S(1)} %pad_maximum_fusion.t0), channel_id=1, source_target_pairs={{0,2},{1,3},{2,0},{3,1},{4,6},{5,7},{6,4},{7,5},{8,10},{9,11},{10,... | collective-permute-start | bytes 786440 | tf_op jit(solution)/shard_map/ppermute | solution.py:226
  58.5 24.2 %collective-permute-start.16 = (f32[1024,128]{1,0:T(8,128)S(1)}, f32[1024,128]{1,0:T(8,128)S(1)}, u32[]{:S(2)}, u32[]{:S(2)}) collective-permute-start(f32[1024,128]{1,0:T(8,128)S(1)} %select_select_fusion.1), channel_id=1, source_target_pairs={{0,64},{16,80},{32,96},{48,112},{192,256},{208,272},{224,288},{240... | collective-permute-start | bytes 1572872 | tf_op jit(solution)/shard_map/ppermute | solution.py:222
  59.8 25.2 %collective-permute-start.17 = (f32[1024,128]{1,0:T(8,128)S(1)}, f32[1024,128]{1,0:T(8,128)S(1)}, u32[]{:S(2)}, u32[]{:S(2)}) collective-permute-start(f32[1024,128]{1,0:T(8,128)S(1)} %select_select_fusion.1), channel_id=1, source_target_pairs={{0,448},{16,464},{32,480},{48,496},{192,128},{208,144},{224,160},{... | collective-permute-start | bytes 1572872 | tf_op jit(solution)/shard_map/ppermute | solution.py:222
  62.0 23.0 %all-to-all-start = ((f32[16,32,128]{2,1,0:T(8,128)}), f32[16,32,128]{2,1,0:T(8,128)S(1)}, u32[]{:S(2)}, u32[]{:S(2)}) async-start(f32[16,32,128]{2,1,0:T(8,128)} %bitcast.11), calls=%async_computation | async-start | bytes 524288 | tf_op jit(solution)/shard_map/all_to_all | solution.py:277
  72.0 7.1 %collective-permute-start.13 = (f32[512,128]{1,0:T(8,128)S(1)}, f32[512,128]{1,0:T(8,128)S(1)}, u32[]{:S(2)}, u32[]{:S(2)}) collective-permute-start(f32[512,128]{1,0:T(8,128)S(1)} %pad_maximum_fusion.t0), channel_id=1, source_target_pairs={{0,1},{1,0},{2,3},{3,2},{4,5},{5,4},{6,7},{7,6},{8,9},{9,8},{10,11... | collective-permute-start | bytes 786440 | tf_op jit(solution)/shard_map/ppermute | solution.py:226
  74.1 10.9 %collective-permute-start.15 = (f32[512,128]{1,0:T(8,128)S(1)}, f32[512,128]{1,0:T(8,128)}, u32[]{:S(2)}, u32[]{:S(2)}) collective-permute-start(f32[512,128]{1,0:T(8,128)S(1)} %collective-permute-done.14.t2), channel_id=1, source_target_pairs={{0,1},{1,0},{2,3},{3,2},{4,5},{5,4},{6,7},{7,6},{8,9},{9,8},{10,11... | collective-permute-start | bytes 786440 | tf_op jit(solution)/shard_map/ppermute | solution.py:226
  77.0 39.4 %collective-permute-start.18 = (f32[512,128]{1,0:T(8,128)S(1)}, f32[512,128]{1,0:T(8,128)}, u32[]{:S(2)}, u32[]{:S(2)}) collective-permute-start(f32[512,128]{1,0:T(8,128)S(1)} %broadcast_select_fusion.p0), channel_id=1, source_target_pairs={{0,1},{1,0},{2,3},{3,2},{4,5},{5,4},{6,7},{7,6},{8,9},{9,8},{10,11... | collective-permute-start | bytes 786440 | tf_op jit(solution)/shard_map/ppermute | solution.py:226
  79.1 37.4 %collective-permute-start.19 = (f32[512,128]{1,0:T(8,128)S(1)}, f32[512,128]{1,0:T(8,128)S(1)}, u32[]{:S(2)}, u32[]{:S(2)}) collective-permute-start(f32[512,128]{1,0:T(8,128)S(1)} %broadcast_select_fusion.p0), channel_id=1, source_target_pairs={{0,2},{1,3},{2,0},{3,1},{4,6},{5,7},{6,4},{7,5},{8,10},{9,11},{10,... | collective-permute-start | bytes 786440 | tf_op jit(solution)/shard_map/ppermute | solution.py:226
  82.6 33.8 %collective-permute-start.20 = (f32[512,128]{1,0:T(8,128)S(1)}, f32[512,128]{1,0:T(8,128)}, u32[]{:S(2)}, u32[]{:S(2)}) collective-permute-start(f32[512,128]{1,0:T(8,128)S(1)} %broadcast_select_fusion.p0), channel_id=1, source_target_pairs={{0,3},{1,2},{2,1},{3,0},{4,7},{5,6},{6,5},{7,4},{8,11},{9,10},{10,... | collective-permute-start | bytes 786440 | tf_op jit(solution)/shard_map/ppermute | solution.py:226
  86.6 29.9 %all-to-all-start.1 = ((f32[4,1024,128]{2,1,0:T(8,128)}), f32[4,1024,128]{2,1,0:T(8,128)S(1)}, u32[]{:S(2)}, u32[]{:S(2)}) async-start(f32[4,1024,128]{2,1,0:T(8,128)} %broadcast_in_dim.20), calls=%async_computation.1 | async-start | bytes 4194304 | tf_op jit(solution)/shard_map/all_to_all | solution.py:283
  123.5 17.2 %all-to-all-start.2 = ((f32[16,2,8,128]{3,2,1,0:T(8,128)}), f32[16,2,8,128]{3,2,1,0:T(8,128)S(1)}, u32[]{:S(2)}, u32[]{:S(2)}) async-start(f32[16,2,8,128]{3,2,1,0:T(8,128)} %bitcast.42), calls=%async_computation.2 | async-start | bytes 262144 | tf_op jit(solution)/shard_map/all_to_all | solution.py:342
  (8 other events, 72.0 us)

commit v5 on v4

--- a/solution.py
+++ b/solution.py
@@ -123,7 +123,7 @@
     my_row, core = ids_ref[0], lax.rem(ids_ref[1], 2)
     x, group = lax.rem(my_row, 4), lax.rem(ids_ref[1], 4)
     gets = [pltpu.make_async_copy(x_hbm, x_ref, sem.at[0]), pltpu.make_async_copy(y_hbm, raw_ref, sem.at[1])]
-    for k, src in enumerate((p0, p1, p2, p3)):
+    for k, src in enumerate((p0, p1.at[LEAD:], p2, p3)):
         cols = pl.ds(pl.multiple_of((group ^ k) * n, n), n)
         gets.append(pltpu.make_async_copy(src, p_ref.at[:, cols], sem.at[2 + k]))
     for get in gets:
@@ -271,13 +271,14 @@
     blocks = [block, block_1, block_32[:192], block_32[192:]]
 
     t0 = jnp.concatenate([b[:TB] for b in blocks], axis=0)
-    t2, t1 = permute_xor(t0, "col", 2), permute_xor(t0, "col", 1)
+    t2 = permute_xor(t0, "col", 2)
+    t1 = permute_xor(jnp.concatenate([t0, own], axis=0), "col", 1)
     got, pick = tree(lead, depth, False)
     wide = jnp.stack([b[TB:].reshape(8, 8, TB) for b in blocks]).transpose(2, 0, 1, 3)
     wide = lax.all_to_all(jnp.repeat(wide.reshape(8, 32, TB), 2, axis=0), "col", 0, 0)
     t3 = permute_xor(t2, "col", 1)
     t1, t3, got, wide = force((t1, t3, got, wide))
-    panel = [own] + [permute_xor(own, "col", k) for k in (1, 2, 3)]
+    panel = [own, t1, permute_xor(own, "col", 2), permute_xor(own, "col", 3)]
     leads = jnp.broadcast_to(pick(got)[None], (4, 8 * TB, TB))
     groups = [[4 * z + x for x in range(4)] for z in range(lax.axis_size("row") // 4)]
     leads = lax.all_to_all(leads, "row", 0, 0, axis_index_groups=groups)

time: 143 us -> 139 us (0.972)
  starting transfers between devices: 81.4 us -> 75.5 us
  waiting for transfers between devices: 9.33 us -> 12.6 us
    all_to_all x1, starting transfers between devices: 10 us -> 4.29 us  [per_device(): lax.all_to_all(jnp.repeat(wide.reshape(8, 32, TB), 2, axis=0), 'col', 0, 0)]
    all_to_all x1, starting transfers between devices: 8.05 us -> 4.42 us  [per_device(): lax.all_to_all(z.reshape(16, 2, 8, TB), 'col', 0, 0).reshape(8, 2, 2, 8, TB)]
    ppermute x8 -> x7, starting transfers between devices: 24 us -> 26.9 us  [permute_xor(): lax.ppermute(block, axis, [(i, i ^ k) for i in range(lax.axis_size(axis))])]
    ppermute x8 -> x7, waiting for transfers between devices: 4.04 us -> 5.61 us  [permute_xor(): lax.ppermute(block, axis, [(i, i ^ k) for i in range(lax.axis_size(axis))])]
  transfers between devices with their start and end apart: 24 -> 23, of which waited for: 5 -> 7; matrix products, arithmetic and copies ran while one was open for 5% -> 5% of each run, Pallas kernels for 23% -> 24%
where the time goes in v5:
time: 139 us; the launch traced here: 138 us
  starting transfers between devices  75.5 us (54%)
  Pallas kernels  39.3 us (28%)
  waiting for transfers between devices  12.6 us (9%)
  local copies, waits for them, and re-layouts  6.98 us (5%)
  other arithmetic  2.71 us (2%)
    ppermute x7, starting transfers between devices, permute_xor(): lax.ppermute(block, axis, [(i, i ^ k) for i in range(lax.axis_size(axis))])  26.9 us
    pallas_call x1, Pallas kernels, per_device(): pl.pallas_call(chol_kernel, out_shape=jax.ShapeDtypeStruct((LEAD, LEAD),...  24.1 us
    ppermute x8, starting transfers between devices, permute_z(): lax.ppermute(block, 'row', [(4 * a + x, 4 * b + x) for a, b in hops for x...  20.7 us
    ppermute x3, starting transfers between devices, per_device(): lax.ppermute(tile, 'col', [(c, c + d) for c in range(4)])  10.2 us
    pallas_call x1, Pallas kernels, per_device(): pl.pallas_call(trailing_kernel, out_shape=jax.ShapeDtypeStruct((8 * LEAD,...  8.8 us
    pallas_call x1, Pallas kernels, per_device(): pl.pallas_call(panel_kernel, out_shape=[jax.ShapeDtypeStruct((LEAD, LEAD)...  6.33 us
    ppermute x7, waiting for transfers between devices, permute_xor(): lax.ppermute(block, axis, [(i, i ^ k) for i in range(lax.axis_size(axis))])  5.61 us
    all_to_all x1, starting transfers between devices, per_device(): lax.all_to_all(z.reshape(16, 2, 8, TB), 'col', 0, 0).reshape(8, 2, 2, 8, TB)  4.42 us
  transfers between devices with their start and end apart: 23, of which 7 were waited for; matrix products, arithmetic and copies ran while one was open for 5% of the time, Pallas kernels for 24%

profile of v5, /device:TPU:1, one launch (start us, length us, event | category | flops | bytes accessed | tf_op | source)
XLA Modules:
  0.0 138.3 jit_solution(4110764264614089300)
XLA Ops:
  1.7 5.0 %collective-permute-start = (f32[128,128]{1,0:T(8,128)S(1)}, f32[128,128]{1,0:T(8,128)S(1)}, u32[]{:S(2)}, u32[]{:S(2)}) collective-permute-start(f32[128,128]{1,0:T(8,128)S(1)} %bitcast.38), channel_id=1, source_target_pairs={{0,4},{1,5},{2,6},{3,7},{16,20},{17,21},{18,22},{19,23},{32,36},{3... | collective-permute-start | bytes 196616 | tf_op jit(solution)/shard_map/ppermute | solution.py:251
  6.8 3.9 %collective-permute-start.1 = (f32[128,128]{1,0:T(8,128)S(1)}, f32[128,128]{1,0:T(8,128)S(1)}, u32[]{:S(2)}, u32[]{:S(2)}) collective-permute-start(f32[128,128]{1,0:T(8,128)S(1)} %bitcast.39), channel_id=1, source_target_pairs={{0,8},{1,9},{2,10},{3,11},{16,24},{17,25},{18,26},{19,27},{32,40},... | collective-permute-start | bytes 196616 | tf_op jit(solution)/shard_map/ppermute | solution.py:251
  12.8 2.9 %collective-permute-done.2 = f32[128,128]{1,0:T(8,128)S(1)} collective-permute-done((f32[128,128]{1,0:T(8,128)S(1)}, f32[128,128]{1,0:T(8,128)S(1)}, u32[]{:S(2)}, u32[]{:S(2)}) %collective-permute-start.2) | collective-permute-done | bytes 65568 | tf_op jit(solution)/shard_map/ppermute | solution.py:251
  15.7 10.6 %collective-permute-start.3 = (f32[192,128]{1,0:T(8,128)S(1)}, f32[192,128]{1,0:T(8,128)S(1)}, u32[]{:S(2)}, u32[]{:S(2)}) collective-permute-start(f32[192,128]{1,0:T(8,128)S(1)} %pad_maximum_fusion.3), channel_id=1, source_target_pairs={{0,320},{16,336},{32,352},{48,368},{1,321},{17,337},{33,353},{49,3... | collective-permute-start | bytes 294920 | tf_op jit(solution)/shard_map/ppermute | solution.py:222
  27.7 1.7 %slice.44 = f32[4,128,1,128]{3,2,1,0:T(1,128)S(1)} slice(f32[4,128,8,128]{3,2,1,0:T(8,128)} %param.2), slice={[0:4], [0:128], [0:1], [0:128]} | slice | bytes 524288 | tf_op jit(solution)/shard_map/slice | solution.py:255
  29.4 3.9 %collective-permute-start.7 = (f32[512,128]{1,0:T(8,128)S(1)}, f32[512,128]{1,0:T(8,128)S(1)}, u32[]{:S(2)}, u32[]{:S(2)}) collective-permute-start(f32[512,128]{1,0:T(8,128)S(1)} %bitcast.32), channel_id=1, source_target_pairs={{0,8},{1,9},{2,10},{3,11},{16,24},{17,25},{18,26},{19,27},{32,40},... | collective-permute-start | bytes 786440 | tf_op jit(solution)/shard_map/ppermute | solution.py:258
  37.1 1.5 %collective-permute-start.10 = (f32[1024,128]{1,0:T(8,128)S(1)}, f32[1024,128]{1,0:T(8,128)S(1)}, u32[]{:S(2)}, u32[]{:S(2)}) collective-permute-start(f32[1024,128]{1,0:T(8,128)S(1)} %slice_bitcast_fusion), channel_id=1, source_target_pairs={{0,192},{16,208},{32,224},{48,240},{1,193},{17,209},{33,225},{49,2... | collective-permute-start | bytes 1572872 | tf_op jit(solution)/shard_map/ppermute | solution.py:222
  40.0 3.1 %collective-permute-start.8 = (f32[192,128]{1,0:T(8,128)S(1)}, f32[192,128]{1,0:T(8,128)S(1)}, u32[]{:S(2)}, u32[]{:S(2)}) collective-permute-start(f32[192,128]{1,0:T(8,128)S(1)} %select_select_fusion.2), channel_id=1, source_target_pairs={{0,16},{16,0},{32,48},{48,32},{64,80},{80,64},{96,112},{112,96},{1... | collective-permute-start | bytes 294920 | tf_op jit(solution)/shard_map/ppermute | solution.py:226
  45.4 4.4 %collective-permute-start.9 = (f32[384,128]{1,0:T(8,128)S(1)}, f32[384,128]{1,0:T(8,128)S(1)}, u32[]{:S(2)}, u32[]{:S(2)}) collective-permute-start(f32[384,128]{1,0:T(8,128)S(1)} %pad_maximum_fusion.1), channel_id=1, source_target_pairs={{0,48},{16,32},{32,16},{48,0},{64,112},{80,96},{96,80},{112,64},{1... | collective-permute-start | bytes 589832 | tf_op jit(solution)/shard_map/ppermute | solution.py:226
  49.8 3.2 %collective-permute-done.9 = f32[384,128]{1,0:T(8,128)S(1)} collective-permute-done((f32[384,128]{1,0:T(8,128)S(1)}, f32[384,128]{1,0:T(8,128)S(1)}, u32[]{:S(2)}, u32[]{:S(2)}) %collective-permute-start.9) | collective-permute-done | bytes 196640 | tf_op jit(solution)/shard_map/ppermute | solution.py:226
  55.4 2.0 %collective-permute-start.17 = (f32[1024,128]{1,0:T(8,128)S(1)}, f32[1024,128]{1,0:T(8,128)S(1)}, u32[]{:S(2)}, u32[]{:S(2)}) collective-permute-start(f32[1024,128]{1,0:T(8,128)S(1)} %select_select_fusion.1), channel_id=1, source_target_pairs={{0,448},{16,464},{32,480},{48,496},{192,128},{208,144},{224,160},{... | collective-permute-start | bytes 1572872 | tf_op jit(solution)/shard_map/ppermute | solution.py:222
  57.6 7.7 %collective-permute-start.13 = (f32[1024,128]{1,0:T(8,128)S(1)}, f32[1024,128]{1,0:T(8,128)S(1)}, u32[]{:S(2)}, u32[]{:S(2)}) collective-permute-start(f32[1024,128]{1,0:T(8,128)S(1)} %get-tuple-element.35), channel_id=1, source_target_pairs={{0,1},{1,0},{2,3},{3,2},{4,5},{5,4},{6,7},{7,6},{8,9},{9,8},{10,11... | collective-permute-start | bytes 1572872 | tf_op jit(solution)/shard_map/ppermute | solution.py:226
  65.4 3.5 %collective-permute-start.14 = (f32[512,128]{1,0:T(8,128)S(1)}, f32[512,128]{1,0:T(8,128)}, u32[]{:S(2)}, u32[]{:S(2)}) collective-permute-start(f32[512,128]{1,0:T(8,128)S(1)} %pad_maximum_fusion.t0), channel_id=1, source_target_pairs={{0,2},{1,3},{2,0},{3,1},{4,6},{5,7},{6,4},{7,5},{8,10},{9,11},{10,... | collective-permute-start | bytes 786440 | tf_op jit(solution)/shard_map/ppermute | solution.py:226
  69.7 4.3 %all-to-all-start = ((f32[16,32,128]{2,1,0:T(8,128)}), f32[16,32,128]{2,1,0:T(8,128)S(1)}, u32[]{:S(2)}, u32[]{:S(2)}) async-start(f32[16,32,128]{2,1,0:T(8,128)} %bitcast.11), calls=%async_computation | async-start | bytes 524288 | tf_op jit(solution)/shard_map/all_to_all | solution.py:278
  74.0 1.6 %collective-permute-done.14.t2 = f32[512,128]{1,0:T(8,128)} collective-permute-done((f32[512,128]{1,0:T(8,128)S(1)}, f32[512,128]{1,0:T(8,128)}, u32[]{:S(2)}, u32[]{:S(2)}) %collective-permute-start.14) | collective-permute-done | bytes 262176 | tf_op jit(solution)/shard_map/ppermute | solution.py:226
  75.6 2.6 %collective-permute-start.15 = (f32[512,128]{1,0:T(8,128)}, f32[512,128]{1,0:T(8,128)}, u32[]{:S(2)}, u32[]{:S(2)}) collective-permute-start(f32[512,128]{1,0:T(8,128)} %collective-permute-done.14.t2), channel_id=1, source_target_pairs={{0,1},{1,0},{2,3},{3,2},{4,5},{5,4},{6,7},{7,6},{8,9},{9,8},{10,11... | collective-permute-start | bytes 786440 | tf_op jit(solution)/shard_map/ppermute | solution.py:226
  78.8 3.6 %collective-permute-start.18 = (f32[512,128]{1,0:T(8,128)S(1)}, f32[512,128]{1,0:T(8,128)}, u32[]{:S(2)}, u32[]{:S(2)}) collective-permute-start(f32[512,128]{1,0:T(8,128)S(1)} %get-tuple-element.36.p0), channel_id=1, source_target_pairs={{0,2},{1,3},{2,0},{3,1},{4,6},{5,7},{6,4},{7,5},{8,10},{9,11},{10,... | collective-permute-start | bytes 786440 | tf_op jit(solution)/shard_map/ppermute | solution.py:226
  82.4 1.9 %collective-permute-start.19 = (f32[512,128]{1,0:T(8,128)S(1)}, f32[512,128]{1,0:T(8,128)}, u32[]{:S(2)}, u32[]{:S(2)}) collective-permute-start(f32[512,128]{1,0:T(8,128)S(1)} %get-tuple-element.36.p0), channel_id=1, source_target_pairs={{0,3},{1,2},{2,1},{3,0},{4,7},{5,6},{6,5},{7,4},{8,11},{9,10},{10,... | collective-permute-start | bytes 786440 | tf_op jit(solution)/shard_map/ppermute | solution.py:226
  87.3 3.8 %all-to-all-start.1 = ((f32[4,1024,128]{2,1,0:T(8,128)}), f32[4,1024,128]{2,1,0:T(8,128)S(1)}, u32[]{:S(2)}, u32[]{:S(2)}) async-start(f32[4,1024,128]{2,1,0:T(8,128)} %broadcast_in_dim.20), calls=%async_computation.1 | async-start | bytes 4194304 | tf_op jit(solution)/shard_map/all_to_all | solution.py:284
  91.1 24.1 %shard_map.49.x_hbm = f32[512,512]{1,0:T(8,128)} custom-call(s32[2]{0:T(128)} %pad_add_fusion.ids_ref, f32[512,128]{1,0:T(8,128)} %copy-done.1, f32[1024,128]{1,0:T(8,128)} %copy-done.5, f32[512,128]{1,0:T(8,128)} %collective-permute-done.14.t2, f32[512,128]{1,0:T(8,128)} %collective-permute-done.15.t3), custom_call_target="tpu_custom_call" | custom-call | flops 20000000000 | bytes 3145728 | tf_op jit(solution)/shard_map/pallas_call | solution.py:286
  115.2 2.4 %all-to-all-done.1.v_hbm = f32[4,1024,128]{2,1,0:T(8,128)S(1)} async-done(((f32[4,1024,128]{2,1,0:T(8,128)}), f32[4,1024,128]{2,1,0:T(8,128)S(1)}, u32[]{:S(2)}, u32[]{:S(2)}) %all-to-all-start.1) | async-done | bytes 2097184 | tf_op jit(solution)/shard_map/all_to_all | solution.py:284
  117.6 6.3 %shard_map.50 = (f32[512,512]{1,0:T(8,128)}, f32[256,128]{1,0:T(8,128)}) custom-call(s32[2]{0:T(128)} %pad_add_fusion.ids_ref, f32[512,512]{1,0:T(8,128)} %shard_map.49.x_hbm, f32[16,32,128]{2,1,0:T(8,128)} %copy-done.2, f32[512,128]{1,0:T(8,128)} %copy-done.3, f32[1024,128]{1,0:T(8,128)} %copy-done.5, f32[512,128]{1,0:T(8,128)} %collective-permute-done.18.p2, ...), custom_call_target="tpu_custom_call" | custom-call | flops 2000000000 | bytes 4194304 | tf_op jit(solution)/shard_map/pallas_call | solution.py:302
  123.9 4.4 %all-to-all-start.2 = ((f32[16,2,8,128]{3,2,1,0:T(8,128)}), f32[16,2,8,128]{3,2,1,0:T(8,128)S(1)}, u32[]{:S(2)}, u32[]{:S(2)}) async-start(f32[16,2,8,128]{3,2,1,0:T(8,128)} %bitcast.42), calls=%async_computation.2 | async-start | bytes 262144 | tf_op jit(solution)/shard_map/all_to_all | solution.py:343
  128.4 8.8 %shard_map.51 = f32[4096,128]{1,0:T(8,128)} custom-call(s32[2]{0:T(128)} %pad_add_fusion.ids_ref, f32[512,512]{1,0:T(8,128)} %shard_map.49.x_hbm, f32[512,512]{1,0:T(8,128)} %get-tuple-element.32.factor_hbm, f32[4096,128]{1,0:T(8,128)} %bitcast.34, f32[4,1024,128]{2,1,0:T(8,128)} %copy-done), custom_call_target="tpu_custom_call" | custom-call | flops 10000000000 | bytes 10485760 | tf_op jit(solution)/shard_map/pallas_call | solution.py:323
  (67 shorter events, 19.7 us)
Async XLA Ops:
  1.7 11.1 %collective-permute-start = (f32[128,128]{1,0:T(8,128)S(1)}, f32[128,128]{1,0:T(8,128)S(1)}, u32[]{:S(2)}, u32[]{:S(2)}) collective-permute-start(f32[128,128]{1,0:T(8,128)S(1)} %bitcast.38), channel_id=1, source_target_pairs={{0,4},{1,5},{2,6},{3,7},{16,20},{17,21},{18,22},{19,23},{32,36},{3... | collective-permute-start | bytes 196616 | tf_op jit(solution)/shard_map/ppermute | solution.py:251
  6.8 6.0 %collective-permute-start.1 = (f32[128,128]{1,0:T(8,128)S(1)}, f32[128,128]{1,0:T(8,128)S(1)}, u32[]{:S(2)}, u32[]{:S(2)}) collective-permute-start(f32[128,128]{1,0:T(8,128)S(1)} %bitcast.39), channel_id=1, source_target_pairs={{0,8},{1,9},{2,10},{3,11},{16,24},{17,25},{18,26},{19,27},{32,40},... | collective-permute-start | bytes 196616 | tf_op jit(solution)/shard_map/ppermute | solution.py:251
  10.7 5.0 %collective-permute-start.2 = (f32[128,128]{1,0:T(8,128)S(1)}, f32[128,128]{1,0:T(8,128)S(1)}, u32[]{:S(2)}, u32[]{:S(2)}) collective-permute-start(f32[128,128]{1,0:T(8,128)S(1)} %bitcast.40), channel_id=1, source_target_pairs={{0,12},{1,13},{2,14},{3,15},{16,28},{17,29},{18,30},{19,31},{32,44... | collective-permute-start | bytes 196616 | tf_op jit(solution)/shard_map/ppermute | solution.py:251
  15.7 17.6 %collective-permute-start.3 = (f32[192,128]{1,0:T(8,128)S(1)}, f32[192,128]{1,0:T(8,128)S(1)}, u32[]{:S(2)}, u32[]{:S(2)}) collective-permute-start(f32[192,128]{1,0:T(8,128)S(1)} %pad_maximum_fusion.3), channel_id=1, source_target_pairs={{0,320},{16,336},{32,352},{48,368},{1,321},{17,337},{33,353},{49,3... | collective-permute-start | bytes 294920 | tf_op jit(solution)/shard_map/ppermute | solution.py:222
  26.4 7.0 %collective-permute-start.4 = (f32[192,128]{1,0:T(8,128)S(1)}, f32[192,128]{1,0:T(8,128)S(1)}, u32[]{:S(2)}, u32[]{:S(2)}) collective-permute-start(f32[192,128]{1,0:T(8,128)S(1)} %pad_maximum_fusion.3), channel_id=1, source_target_pairs={{0,192},{16,208},{32,224},{48,240},{1,193},{17,209},{33,225},{49,2... | collective-permute-start | bytes 294920 | tf_op jit(solution)/shard_map/ppermute | solution.py:222
  29.4 10.5 %collective-permute-start.7 = (f32[512,128]{1,0:T(8,128)S(1)}, f32[512,128]{1,0:T(8,128)S(1)}, u32[]{:S(2)}, u32[]{:S(2)}) collective-permute-start(f32[512,128]{1,0:T(8,128)S(1)} %bitcast.32), channel_id=1, source_target_pairs={{0,8},{1,9},{2,10},{3,11},{16,24},{17,25},{18,26},{19,27},{32,40},... | collective-permute-start | bytes 786440 | tf_op jit(solution)/shard_map/ppermute | solution.py:258
  33.4 6.5 %collective-permute-start.5 = (f32[192,128]{1,0:T(8,128)S(1)}, f32[192,128]{1,0:T(8,128)S(1)}, u32[]{:S(2)}, u32[]{:S(2)}) collective-permute-start(f32[192,128]{1,0:T(8,128)S(1)} %select_select_fusion.3), channel_id=1, source_target_pairs={{0,64},{16,80},{32,96},{48,112},{192,256},{208,272},{224,288},{240... | collective-permute-start | bytes 294920 | tf_op jit(solution)/shard_map/ppermute | solution.py:222
  34.7 5.2 %collective-permute-start.6 = (f32[192,128]{1,0:T(8,128)S(1)}, f32[192,128]{1,0:T(8,128)S(1)}, u32[]{:S(2)}, u32[]{:S(2)}) collective-permute-start(f32[192,128]{1,0:T(8,128)S(1)} %select_select_fusion.3), channel_id=1, source_target_pairs={{0,448},{16,464},{32,480},{48,496},{192,128},{208,144},{224,160},{... | collective-permute-start | bytes 294920 | tf_op jit(solution)/shard_map/ppermute | solution.py:222
  37.1 12.7 %collective-permute-start.10 = (f32[1024,128]{1,0:T(8,128)S(1)}, f32[1024,128]{1,0:T(8,128)S(1)}, u32[]{:S(2)}, u32[]{:S(2)}) collective-permute-start(f32[1024,128]{1,0:T(8,128)S(1)} %slice_bitcast_fusion), channel_id=1, source_target_pairs={{0,192},{16,208},{32,224},{48,240},{1,193},{17,209},{33,225},{49,2... | collective-permute-start | bytes 1572872 | tf_op jit(solution)/shard_map/ppermute | solution.py:222
  38.6 11.2 %collective-permute-start.11 = (f32[1024,128]{1,0:T(8,128)S(1)}, f32[1024,128]{1,0:T(8,128)S(1)}, u32[]{:S(2)}, u32[]{:S(2)}) collective-permute-start(f32[1024,128]{1,0:T(8,128)S(1)} %slice_bitcast_fusion), channel_id=1, source_target_pairs={{0,320},{16,336},{32,352},{48,368},{1,321},{17,337},{33,353},{49,3... | collective-permute-start | bytes 1572872 | tf_op jit(solution)/shard_map/ppermute | solution.py:222
  40.0 5.4 %collective-permute-start.8 = (f32[192,128]{1,0:T(8,128)S(1)}, f32[192,128]{1,0:T(8,128)S(1)}, u32[]{:S(2)}, u32[]{:S(2)}) collective-permute-start(f32[192,128]{1,0:T(8,128)S(1)} %select_select_fusion.2), channel_id=1, source_target_pairs={{0,16},{16,0},{32,48},{48,32},{64,80},{80,64},{96,112},{112,96},{1... | collective-permute-start | bytes 294920 | tf_op jit(solution)/shard_map/ppermute | solution.py:226
  43.2 6.6 %collective-permute-start.12 = (f32[512,128]{1,0:T(8,128)S(1)}, f32[512,128]{1,0:T(8,128)S(1)}, u32[]{:S(2)}, u32[]{:S(2)}) collective-permute-start(f32[512,128]{1,0:T(8,128)S(1)} %broadcast_select_fusion.1), channel_id=1, source_target_pairs={{0,4},{1,5},{2,6},{3,7},{8,12},{9,13},{10,14},{11,15},{16,20},{17,... | collective-permute-start | bytes 786440 | tf_op jit(solution)/shard_map/ppermute | solution.py:267
  45.4 7.6 %collective-permute-start.9 = (f32[384,128]{1,0:T(8,128)S(1)}, f32[384,128]{1,0:T(8,128)S(1)}, u32[]{:S(2)}, u32[]{:S(2)}) collective-permute-start(f32[384,128]{1,0:T(8,128)S(1)} %pad_maximum_fusion.1), channel_id=1, source_target_pairs={{0,48},{16,32},{32,16},{48,0},{64,112},{80,96},{96,80},{112,64},{1... | collective-permute-start | bytes 589832 | tf_op jit(solution)/shard_map/ppermute | solution.py:226
  54.1 28.3 %collective-permute-start.16 = (f32[1024,128]{1,0:T(8,128)S(1)}, f32[1024,128]{1,0:T(8,128)S(1)}, u32[]{:S(2)}, u32[]{:S(2)}) collective-permute-start(f32[1024,128]{1,0:T(8,128)S(1)} %select_select_fusion.1), channel_id=1, source_target_pairs={{0,64},{16,80},{32,96},{48,112},{192,256},{208,272},{224,288},{240... | collective-permute-start | bytes 1572872 | tf_op jit(solution)/shard_map/ppermute | solution.py:222
  55.4 30.2 %collective-permute-start.17 = (f32[1024,128]{1,0:T(8,128)S(1)}, f32[1024,128]{1,0:T(8,128)S(1)}, u32[]{:S(2)}, u32[]{:S(2)}) collective-permute-start(f32[1024,128]{1,0:T(8,128)S(1)} %select_select_fusion.1), channel_id=1, source_target_pairs={{0,448},{16,464},{32,480},{48,496},{192,128},{208,144},{224,160},{... | collective-permute-start | bytes 1572872 | tf_op jit(solution)/shard_map/ppermute | solution.py:222
  57.6 29.7 %copy-start.3 = (f32[512,128]{1,0:T(8,128)}, f32[512,128]{1,0:T(8,128)S(1)}, u32[]{:S(2)}) copy-start(f32[512,128]{1,0:T(8,128)S(1)} %get-tuple-element.36.p0) | copy-start | bytes 786436
  57.6 28.1 %collective-permute-start.13 = (f32[1024,128]{1,0:T(8,128)S(1)}, f32[1024,128]{1,0:T(8,128)S(1)}, u32[]{:S(2)}, u32[]{:S(2)}) collective-permute-start(f32[1024,128]{1,0:T(8,128)S(1)} %get-tuple-element.35), channel_id=1, source_target_pairs={{0,1},{1,0},{2,3},{3,2},{4,5},{5,4},{6,7},{7,6},{8,9},{9,8},{10,11... | collective-permute-start | bytes 1572872 | tf_op jit(solution)/shard_map/ppermute | solution.py:226
  65.4 10.2 %collective-permute-start.14 = (f32[512,128]{1,0:T(8,128)S(1)}, f32[512,128]{1,0:T(8,128)}, u32[]{:S(2)}, u32[]{:S(2)}) collective-permute-start(f32[512,128]{1,0:T(8,128)S(1)} %pad_maximum_fusion.t0), channel_id=1, source_target_pairs={{0,2},{1,3},{2,0},{3,1},{4,6},{5,7},{6,4},{7,5},{8,10},{9,11},{10,... | collective-permute-start | bytes 786440 | tf_op jit(solution)/shard_map/ppermute | solution.py:226
  69.7 16.0 %all-to-all-start = ((f32[16,32,128]{2,1,0:T(8,128)}), f32[16,32,128]{2,1,0:T(8,128)S(1)}, u32[]{:S(2)}, u32[]{:S(2)}) async-start(f32[16,32,128]{2,1,0:T(8,128)} %bitcast.11), calls=%async_computation | async-start | bytes 524288 | tf_op jit(solution)/shard_map/all_to_all | solution.py:278
  75.6 10.1 %collective-permute-start.15 = (f32[512,128]{1,0:T(8,128)}, f32[512,128]{1,0:T(8,128)}, u32[]{:S(2)}, u32[]{:S(2)}) collective-permute-start(f32[512,128]{1,0:T(8,128)} %collective-permute-done.14.t2), channel_id=1, source_target_pairs={{0,1},{1,0},{2,3},{3,2},{4,5},{5,4},{6,7},{7,6},{8,9},{9,8},{10,11... | collective-permute-start | bytes 786440 | tf_op jit(solution)/shard_map/ppermute | solution.py:226
  78.8 38.8 %collective-permute-start.18 = (f32[512,128]{1,0:T(8,128)S(1)}, f32[512,128]{1,0:T(8,128)}, u32[]{:S(2)}, u32[]{:S(2)}) collective-permute-start(f32[512,128]{1,0:T(8,128)S(1)} %get-tuple-element.36.p0), channel_id=1, source_target_pairs={{0,2},{1,3},{2,0},{3,1},{4,6},{5,7},{6,4},{7,5},{8,10},{9,11},{10,... | collective-permute-start | bytes 786440 | tf_op jit(solution)/shard_map/ppermute | solution.py:226
  82.4 35.2 %collective-permute-start.19 = (f32[512,128]{1,0:T(8,128)S(1)}, f32[512,128]{1,0:T(8,128)}, u32[]{:S(2)}, u32[]{:S(2)}) collective-permute-start(f32[512,128]{1,0:T(8,128)S(1)} %get-tuple-element.36.p0), channel_id=1, source_target_pairs={{0,3},{1,2},{2,1},{3,0},{4,7},{5,6},{6,5},{7,4},{8,11},{9,10},{10,... | collective-permute-start | bytes 786440 | tf_op jit(solution)/shard_map/ppermute | solution.py:226
  87.3 30.3 %all-to-all-start.1 = ((f32[4,1024,128]{2,1,0:T(8,128)}), f32[4,1024,128]{2,1,0:T(8,128)S(1)}, u32[]{:S(2)}, u32[]{:S(2)}) async-start(f32[4,1024,128]{2,1,0:T(8,128)} %broadcast_in_dim.20), calls=%async_computation.1 | async-start | bytes 4194304 | tf_op jit(solution)/shard_map/all_to_all | solution.py:284
  123.9 13.6 %all-to-all-start.2 = ((f32[16,2,8,128]{3,2,1,0:T(8,128)}), f32[16,2,8,128]{3,2,1,0:T(8,128)S(1)}, u32[]{:S(2)}, u32[]{:S(2)}) async-start(f32[16,2,8,128]{3,2,1,0:T(8,128)} %bitcast.42), calls=%async_computation.2 | async-start | bytes 262144 | tf_op jit(solution)/shard_map/all_to_all | solution.py:343
  (5 other events, 40.6 us)
